TPU v7x, 32 devices: a whole 2x2x4 slice. The times are simulated.
32 devices in a mesh: dp: 8 (over y, x, core), mp: 4 (over z).
Axes of the slice: x: 2, y: 2, z: 4, core: 2. Of those that a mesh axis runs over, the one named last changes fastest.
Arguments:
- hidden: bfloat16 [8192, 2048], P('dp', 'mp'), may hold values from -6 to 6
- teacher: bfloat16 [8192, 2048], P('dp', 'mp'), may hold values from -6 to 6
- lengths: int32 [8], replicated, may hold values from 256 to 1024, as said below
- feature_params: bfloat16 [2048, 18], P(('dp', 'mp')), may hold values from -10 to 3, as said below
- decay_down: bfloat16 [2048, 96], P(('dp', 'mp')), may hold values from -0.125 to 0.125
- rate_down: bfloat16 [2048, 96], P(('dp', 'mp')), may hold values from -0.125 to 0.125
- gate_down: bfloat16 [2048, 256], P(('dp', 'mp')), may hold values from -0.125 to 0.125
- decay_up: bfloat16 [96, 2048], P('dp', 'mp'), may hold values from -0.625 to 0.625
- rate_up: bfloat16 [96, 2048], P('dp', 'mp'), may hold values from -0.625 to 0.625
- gate_up: bfloat16 [256, 2048], P('dp', 'mp'), may hold values from -0.375 to 0.375
- receptance: bfloat16 [2048, 2048], P('dp', 'mp'), may hold values from -0.125 to 0.125
- key_proj: bfloat16 [2048, 2048], P('dp', 'mp'), may hold values from -0.125 to 0.125
- value_proj: bfloat16 [2048, 2048], P('dp', 'mp'), may hold values from -0.125 to 0.125
- output_proj: bfloat16 [2048, 2048], P('mp', 'dp'), may hold values from -0.1875 to 0.1875
- ffn_key: bfloat16 [2048, 8192], P('dp', 'mp'), may hold values from -0.125 to 0.125
- ffn_value: bfloat16 [8192, 2048], P('mp', 'dp'), may hold values from -0.0625 to 0.0625
Outputs:
- out_state: bfloat16 [8192, 2048], P('dp', 'mp')
- grad_hidden: float32 [8192, 2048], P('dp', 'mp')
- grad_params: float32 [2048, 18], P(('dp', 'mp'))
- grad_decay_down: float32 [2048, 96], P(('dp', 'mp'))
- grad_rate_down: float32 [2048, 96], P(('dp', 'mp'))
- grad_gate_down: float32 [2048, 256], P(('dp', 'mp'))
- grad_decay_up: float32 [96, 2048], P('dp', 'mp')
- grad_rate_up: float32 [96, 2048], P('dp', 'mp')
- grad_gate_up: float32 [256, 2048], P('dp', 'mp')
- grad_receptance: float32 [2048, 2048], P('dp', 'mp')
- grad_key_proj: float32 [2048, 2048], P('dp', 'mp')
- grad_value_proj: float32 [2048, 2048], P('dp', 'mp')
- grad_output_proj: float32 [2048, 2048], P('mp', 'dp')
- grad_ffn_key: float32 [2048, 8192], P('dp', 'mp')
- grad_ffn_value: float32 [8192, 2048], P('mp', 'dp')
Inputs may be any that keep to these rules, and one draw needn't show every extreme that they name: `lengths`: each sequence's valid tokens fill its first slots; one sequence holds 1024 valid tokens and one holds 256. `feature_params`: the columns are in the order that the steps list.
All inputs are finite; a program needn't handle non-finite values.
Results may differ from a plain program's by a relative error of at most 0.015.
Values may be sent and summed in bfloat16 or wider, within the bound.
A program may use at most 576 MiB of HBM per device.

v0:
```python
from functools import partial
import math

import jax
import jax.numpy as jnp
from jax import lax
from jax.sharding import PartitionSpec as P

SUBSPACE_SIZE = 64
SEQ_LEN = 1024


hi_prec = lax.Precision.HIGHEST
norm_eps = 1e-05
group_eps = 0.00064


def matmul(left_op, right_op):
    return jnp.dot(left_op, right_op, preferred_element_type=jnp.float32)


def contract_rows(left_op, right_op):
    return jnp.einsum("tk,tn->kn", left_op, right_op, preferred_element_type=jnp.float32)


def against(grad_op, weight_op):
    return jnp.einsum("tn,kn->tk", grad_op, weight_op, preferred_element_type=jnp.float32)


def layer_norm(values, scale_in, offset):
    centre = jnp.mean(values, axis=-1, keepdims=True)
    centred = values - centre
    spread = jnp.mean(centred * centred, axis=-1, keepdims=True)
    return centred * lax.rsqrt(spread + norm_eps) * scale_in + offset


def shifted(values):
    grid_view = values.reshape(values.shape[0] // SEQ_LEN, SEQ_LEN, values.shape[1])
    earlier = jnp.concatenate([jnp.zeros_like(grid_view[:, :1]), grid_view[:, :-1]], axis=1)
    return earlier.reshape(values.shape)


def section_in(hidden, scale_in, offset, mix_rates):
    standardized_source = layer_norm(hidden, scale_in, offset)
    shift_diff = shifted(standardized_source) - standardized_source
    return tuple((standardized_source + shift_diff * mix_rates[:, column] for column in range(6)))


def section_out(residual, scale_in, offset, mix_rate):
    standardized_source = layer_norm(residual, scale_in, offset)
    return standardized_source + (shifted(standardized_source) - standardized_source) * mix_rate


def to_heads(values, seq_dev, block_len):
    seq_slots = values.shape[0] // seq_dev
    subspaces_each_shard = values.shape[1] // SUBSPACE_SIZE
    shaped = values.reshape(
        seq_dev, seq_slots // block_len, block_len, subspaces_each_shard, SUBSPACE_SIZE
    )
    shaped = shaped.transpose(1, 0, 3, 2, 4)
    return shaped.reshape(
        seq_slots // block_len, seq_dev * subspaces_each_shard, block_len, SUBSPACE_SIZE
    )


def from_heads(values, seq_dev, subspaces_each_shard):
    block_count = values.shape[0]
    block_len = values.shape[2]
    shaped = values.reshape(block_count, seq_dev, subspaces_each_shard, block_len, SUBSPACE_SIZE)
    shaped = shaped.transpose(1, 0, 3, 2, 4)
    return shaped.reshape(seq_dev * block_count * block_len, subspaces_each_shard * SUBSPACE_SIZE)


def unit_lower_inverse(lower_part):
    product = partial(jnp.einsum, precision=hi_prec)
    block_len = lower_part.shape[-1]
    identity = jnp.eye(block_len, dtype=jnp.float32)
    accum = identity + lower_part
    power = lower_part
    for level in range(max(block_len.bit_length() - 2, 0)):
        power = product("bts,bsu->btu", power, power)
        accum = accum + product("bts,bsu->btu", accum, power)
    return accum


def block_step(state, members):
    acceptance_matrix, log_decay, remove_dir, write_dir, value_rows, key_rows = members
    product = partial(jnp.einsum, precision=hi_prec)
    running = jnp.cumsum(log_decay, axis=1)
    grown = jnp.exp(running)
    shrunk = jnp.exp(-running)
    before = jnp.exp(running - log_decay)
    recept_hat = acceptance_matrix * grown
    remove_hat = remove_dir * before
    write_til = write_dir * shrunk
    key_til = key_rows * shrunk
    block_len = acceptance_matrix.shape[1]
    places = jnp.arange(block_len)
    strict = places[:, None] > places[None, :]
    within = places[:, None] >= places[None, :]
    lower_write = jnp.where(strict, product("btn,bsn->bts", remove_hat, write_til), 0.0)
    lower_key = jnp.where(strict, product("btn,bsn->bts", remove_hat, key_til), 0.0)
    read_write = jnp.where(within, product("btn,bsn->bts", recept_hat, write_til), 0.0)
    read_key = jnp.where(within, product("btn,bsn->bts", recept_hat, key_til), 0.0)
    right_side = product("btj,bij->bti", remove_hat, state) + product(
        "bts,bsi->bti", lower_key, value_rows
    )
    removed = product("bts,bsi->bti", unit_lower_inverse(lower_write), right_side)
    outputs = product("btj,bij->bti", recept_hat, state) + product(
        "bts,bsi->bti", read_write, removed
    )
    outputs = outputs + product("bts,bsi->bti", read_key, value_rows)
    final_decay = grown[:, -1:, :]
    state = state * final_decay + product("bti,btj->bij", removed, write_til * final_decay)
    state = state + product("bti,btj->bij", value_rows, key_til * final_decay)
    return (state, outputs)


def time_mixer(
    acceptance_matrix,
    keys_in,
    payload_source,
    decay_in,
    rate_in,
    sigmoid_source,
    columns,
    valid,
    seq_dev,
):
    position_count, part_width = acceptance_matrix.shape
    subspaces_each_shard = part_width // SUBSPACE_SIZE
    log_decay = -jnp.exp(-jax.nn.softplus(-(decay_in + columns[:, 0])) - 0.5)
    learn_rate = jax.nn.sigmoid(rate_in + columns[:, 1])
    scaled_keys = (keys_in * columns[:, 2]).reshape(
        position_count, subspaces_each_shard, SUBSPACE_SIZE
    )
    unit_keys = scaled_keys * lax.rsqrt(
        jnp.sum(scaled_keys * scaled_keys, axis=-1, keepdims=True) + 1e-06
    )
    unit_keys = unit_keys.reshape(position_count, part_width)
    lagged_lookups = keys_in * (1.0 + (learn_rate - 1.0) * columns[:, 3])
    live = valid[:, None] > 0.5
    log_decay = jnp.where(live, log_decay, 0.0)
    unit_keys = jnp.where(live, unit_keys, 0.0)
    lagged_lookups = jnp.where(live, lagged_lookups, 0.0)
    block_len = math.gcd(position_count // seq_dev, 64)
    arranged = tuple(
        (
            to_heads(member, seq_dev, block_len)
            for member in (
                acceptance_matrix,
                log_decay,
                -unit_keys,
                unit_keys * learn_rate,
                payload_source,
                lagged_lookups,
            )
        )
    )
    start_state = jnp.zeros((arranged[0].shape[1], SUBSPACE_SIZE, SUBSPACE_SIZE), jnp.float32)
    final_state, outputs = lax.scan(block_step, start_state, arranged)
    grouped = from_heads(outputs, seq_dev, subspaces_each_shard).reshape(
        position_count, subspaces_each_shard, SUBSPACE_SIZE
    )
    centre = jnp.mean(grouped, axis=-1, keepdims=True)
    centred = grouped - centre
    spread = jnp.mean(centred * centred, axis=-1, keepdims=True)
    standardized_source = (centred * lax.rsqrt(spread + group_eps)).reshape(
        position_count, part_width
    ) * columns[:, 5] + columns[:, 6]
    current_reward = jnp.sum(
        (acceptance_matrix * lagged_lookups * columns[:, 4]).reshape(
            position_count, subspaces_each_shard, SUBSPACE_SIZE
        ),
        axis=-1,
        keepdims=True,
    )
    current_reward = (
        current_reward * payload_source.reshape(position_count, subspaces_each_shard, SUBSPACE_SIZE)
    ).reshape(position_count, part_width)
    return (standardized_source + current_reward) * sigmoid_source


def body(
    hidden,
    teacher,
    lengths,
    feature_params,
    decay_down,
    rate_down,
    gate_down,
    decay_up,
    rate_up,
    gate_up,
    receptance,
    key_proj,
    value_proj,
    output_proj,
    ffn_key,
    ffn_value,
):
    position_count, part_width = hidden.shape
    seq_dev = position_count // SEQ_LEN
    mp_index = lax.axis_index("mp")
    col_start = mp_index * part_width
    quarter = position_count // lax.axis_size("mp")
    row_start = mp_index * quarter
    own_lengths = lax.dynamic_slice_in_dim(lengths, lax.axis_index("dp") * seq_dev, seq_dev)
    places = jnp.arange(SEQ_LEN, dtype=jnp.int32)
    valid = (places[None, :] < own_lengths[:, None]).astype(jnp.float32).reshape(position_count)
    loss_scale = position_count * lax.axis_size("dp") / jnp.sum(lengths).astype(jnp.float32)
    whole = lax.all_gather(hidden, "mp", axis=1, tiled=True).astype(jnp.float32)
    fwd_big = (
        lax.all_gather(receptance, "dp", axis=0, tiled=True),
        lax.all_gather(key_proj, "dp", axis=0, tiled=True),
        lax.all_gather(value_proj, "dp", axis=0, tiled=True),
        lax.all_gather(decay_up, "dp", axis=0, tiled=True),
        lax.all_gather(rate_up, "dp", axis=0, tiled=True),
        lax.all_gather(gate_up, "dp", axis=0, tiled=True),
        lax.all_gather(ffn_key, "dp", axis=0, tiled=True),
        lax.all_gather(output_proj, "dp", axis=1, tiled=True),
        lax.all_gather(ffn_value, "dp", axis=1, tiled=True),
    )
    fwd_small = (
        lax.all_gather(decay_down, ("dp", "mp"), axis=0, tiled=True),
        lax.all_gather(rate_down, ("dp", "mp"), axis=0, tiled=True),
        lax.all_gather(gate_down, ("dp", "mp"), axis=0, tiled=True),
        lax.all_gather(feature_params, ("dp", "mp"), axis=0, tiled=True),
    )
    recept_w, key_w, value_w, decay_up_w, rate_up_w, gate_up_w, ffn_key_w, output_w, ffn_value_w = (
        fwd_big
    )
    decay_down_w, rate_down_w, gate_down_w, params_low = fwd_small
    params = params_low.astype(jnp.float32)
    model_width = whole.shape[1]
    mixed, back_in = jax.vjp(section_in, whole, params[:, 0], params[:, 1], params[:, 2:8])
    mix_r, mix_w, mix_k, mix_v, mix_a, mix_g = tuple(
        (member.astype(jnp.bfloat16) for member in mixed)
    )
    acceptance_matrix = matmul(mix_r, recept_w)
    keys_in = matmul(mix_k, key_w)
    payload_source = matmul(mix_v, value_w)
    decay_hid = jnp.tanh(matmul(mix_w, decay_down_w))
    decay_low = decay_hid.astype(jnp.bfloat16)
    rate_low = matmul(mix_a, rate_down_w).astype(jnp.bfloat16)
    gate_hid = jax.nn.sigmoid(matmul(mix_g, gate_down_w))
    gate_low = gate_hid.astype(jnp.bfloat16)
    decay_in = matmul(decay_low, decay_up_w)
    rate_in = matmul(rate_low, rate_up_w)
    sigmoid_source = matmul(gate_low, gate_up_w)
    columns = lax.dynamic_slice_in_dim(params, col_start, part_width, 0)[:, 8:15]
    mixer = partial(time_mixer, valid=valid, seq_dev=seq_dev)
    masked_result, back_core = jax.vjp(
        mixer,
        acceptance_matrix,
        keys_in,
        payload_source,
        decay_in,
        rate_in,
        sigmoid_source,
        columns,
    )
    gated_low = masked_result.astype(jnp.bfloat16)
    residual = whole + lax.psum(matmul(gated_low, output_w).astype(jnp.bfloat16), "mp").astype(
        jnp.float32
    )
    ffn_in, back_out = jax.vjp(section_out, residual, params[:, 15], params[:, 16], params[:, 17])
    ffn_low = ffn_in.astype(jnp.bfloat16)
    pre_act = matmul(ffn_low, ffn_key_w)
    active = jnp.maximum(pre_act, 0.0)
    squared = (active * active).astype(jnp.bfloat16)
    ffn_part = lax.psum_scatter(
        matmul(squared, ffn_value_w).astype(jnp.bfloat16), "mp", scatter_dimension=1, tiled=True
    ).astype(jnp.float32)
    result = lax.dynamic_slice_in_dim(residual, col_start, part_width, 1) + ffn_part
    grad_result = loss_scale * valid[:, None] * (result - teacher.astype(jnp.float32))
    grad_full = lax.all_gather(grad_result.astype(jnp.bfloat16), "mp", axis=1, tiled=True).astype(
        grad_result.dtype
    )
    grad_low = grad_full.astype(jnp.bfloat16)
    grad_ffn_value = contract_rows(squared, grad_low)
    grad_squared = against(grad_low, ffn_value_w)
    grad_pre = (grad_squared * 2.0 * active).astype(jnp.bfloat16)
    d_resid_part, d_scale_two, d_offset_two, d_mix_two = back_out(against(grad_pre, ffn_key_w))
    d_residual = grad_full + lax.psum(d_resid_part.astype(jnp.bfloat16), "mp").astype(jnp.float32)
    d_low = d_residual.astype(jnp.bfloat16)
    grad_output_proj = contract_rows(gated_low, d_low)
    grads_core = back_core(against(d_low, output_w))
    d_recept, d_keys, d_values, d_decay, d_rate, d_gate = tuple(
        (member.astype(jnp.bfloat16) for member in grads_core[:6])
    )
    d_columns = grads_core[6]
    grad_decay_up = contract_rows(decay_low, d_decay)
    grad_rate_up = contract_rows(rate_low, d_rate)
    grad_gate_up = contract_rows(gate_low, d_gate)
    d_decay_hid, d_rate_hid, d_gate_hid = (
        lax.psum(against(d_decay, decay_up_w).astype(jnp.bfloat16), "mp").astype(jnp.float32),
        lax.psum(against(d_rate, rate_up_w).astype(jnp.bfloat16), "mp").astype(jnp.float32),
        lax.psum(against(d_gate, gate_up_w).astype(jnp.bfloat16), "mp").astype(jnp.float32),
    )
    d_decay_pre = (d_decay_hid * (1.0 - decay_hid * decay_hid)).astype(jnp.bfloat16)
    d_rate_pre = d_rate_hid.astype(jnp.bfloat16)
    d_gate_pre = (d_gate_hid * gate_hid * (1.0 - gate_hid)).astype(jnp.bfloat16)

    def own_rows(values):
        return lax.dynamic_slice_in_dim(values, row_start, quarter, 0)

    def place_rows(values):
        return lax.dynamic_update_slice_in_dim(
            jnp.zeros((position_count, values.shape[1]), jnp.float32), values, row_start, 0
        )

    grad_decay_down = contract_rows(own_rows(mix_w), own_rows(d_decay_pre))
    grad_rate_down = contract_rows(own_rows(mix_a), own_rows(d_rate_pre))
    grad_gate_down = contract_rows(own_rows(mix_g), own_rows(d_gate_pre))
    cotangents = (
        against(d_recept, recept_w),
        place_rows(against(own_rows(d_decay_pre), decay_down_w)),
        against(d_keys, key_w),
        against(d_values, value_w),
        place_rows(against(own_rows(d_rate_pre), rate_down_w)),
        place_rows(against(own_rows(d_gate_pre), gate_down_w)),
    )
    d_in_part, d_scale_one, d_offset_one, d_mix_one = back_in(cotangents)
    grad_hidden = lax.dynamic_slice_in_dim(d_residual, col_start, part_width, 1) + lax.psum_scatter(
        d_in_part.astype(jnp.bfloat16), "mp", scatter_dimension=1, tiled=True
    ).astype(jnp.float32)
    core_grads = lax.dynamic_update_slice_in_dim(
        jnp.zeros((model_width, 7), jnp.float32), d_columns, col_start, 0
    )
    grad_params = jnp.concatenate(
        [
            d_scale_one[:, None],
            d_offset_one[:, None],
            d_mix_one,
            core_grads,
            d_scale_two[:, None],
            d_offset_two[:, None],
            d_mix_two[:, None],
        ],
        axis=1,
    )
    small_grads = (
        lax.psum_scatter(grad_decay_down, ("dp", "mp"), scatter_dimension=0, tiled=True),
        lax.psum_scatter(grad_rate_down, ("dp", "mp"), scatter_dimension=0, tiled=True),
        lax.psum_scatter(grad_gate_down, ("dp", "mp"), scatter_dimension=0, tiled=True),
        lax.psum_scatter(grad_params, ("dp", "mp"), scatter_dimension=0, tiled=True),
    )
    grad_receptance = contract_rows(mix_r, d_recept)
    grad_key_proj = contract_rows(mix_k, d_keys)
    grad_value_proj = contract_rows(mix_v, d_values)
    grad_ffn_key = contract_rows(ffn_low, grad_pre)
    big_grads = (
        lax.psum_scatter(
            grad_receptance.astype(jnp.bfloat16), "dp", scatter_dimension=0, tiled=True
        ).astype(jnp.float32),
        lax.psum_scatter(
            grad_key_proj.astype(jnp.bfloat16), "dp", scatter_dimension=0, tiled=True
        ).astype(jnp.float32),
        lax.psum_scatter(
            grad_value_proj.astype(jnp.bfloat16), "dp", scatter_dimension=0, tiled=True
        ).astype(jnp.float32),
        lax.psum_scatter(
            grad_decay_up.astype(jnp.bfloat16), "dp", scatter_dimension=0, tiled=True
        ).astype(jnp.float32),
        lax.psum_scatter(
            grad_rate_up.astype(jnp.bfloat16), "dp", scatter_dimension=0, tiled=True
        ).astype(jnp.float32),
        lax.psum_scatter(
            grad_gate_up.astype(jnp.bfloat16), "dp", scatter_dimension=0, tiled=True
        ).astype(jnp.float32),
        lax.psum_scatter(
            grad_ffn_key.astype(jnp.bfloat16), "dp", scatter_dimension=0, tiled=True
        ).astype(jnp.float32),
        lax.psum_scatter(
            grad_output_proj.astype(jnp.bfloat16), "dp", scatter_dimension=1, tiled=True
        ).astype(jnp.float32),
        lax.psum_scatter(
            grad_ffn_value.astype(jnp.bfloat16), "dp", scatter_dimension=1, tiled=True
        ).astype(jnp.float32),
    )
    return (
        result.astype(jnp.bfloat16),
        grad_hidden,
        small_grads[3],
        small_grads[0],
        small_grads[1],
        small_grads[2],
        big_grads[3],
        big_grads[4],
        big_grads[5],
        big_grads[0],
        big_grads[1],
        big_grads[2],
        big_grads[7],
        big_grads[6],
        big_grads[8],
    )


def solution(mesh):
    in_specs = (
        P("dp", "mp"),
        P("dp", "mp"),
        P(),
        P(("dp", "mp"), None),
        P(("dp", "mp"), None),
        P(("dp", "mp"), None),
        P(("dp", "mp"), None),
        P("dp", "mp"),
        P("dp", "mp"),
        P("dp", "mp"),
        P("dp", "mp"),
        P("dp", "mp"),
        P("dp", "mp"),
        P("mp", "dp"),
        P("dp", "mp"),
        P("mp", "dp"),
    )
    out_specs = (
        P("dp", "mp"),
        P("dp", "mp"),
        P(("dp", "mp"), None),
        P(("dp", "mp"), None),
        P(("dp", "mp"), None),
        P(("dp", "mp"), None),
        P("dp", "mp"),
        P("dp", "mp"),
        P("dp", "mp"),
        P("dp", "mp"),
        P("dp", "mp"),
        P("dp", "mp"),
        P("mp", "dp"),
        P("dp", "mp"),
        P("mp", "dp"),
    )
    return jax.shard_map(body, mesh=mesh, in_specs=in_specs, out_specs=out_specs, check_vma=False)
```

profile of v0, /device:TPU:0, one launch (start us, length us, event | category | flops | bytes accessed | tf_op | source)
XLA Modules:
  0.0 3967.3 jit_solution(17272178907327520022)
XLA Ops:
  11.4 74.5 %all-gather = bf16[32,64,18]{1,2,0:T(8,128)(2,1)S(1)} all-gather(bf16[1,64,18]{1,2,0:T(8,128)(2,1)} %bitcast.1073), channel_id=1, replica_groups=mesh['dp'=8,'mp'=4] {'dp','mp'}, dimensions={0}, use_global_device_ids=true | all-gather | bytes 76032 | tf_op jit(solution)/shard_map/all_gather | solution.py:228
  86.7 70.0 %all_gather.47 = bf16[2048,96]{1,0:T(8,128)(2,1)S(1)} all-gather(bf16[64,96]{1,0:T(8,128)(2,1)} %param.24), channel_id=1, replica_groups=mesh['dp'=8,'mp'=4] {'dp','mp'}, dimensions={0}, use_global_device_ids=true | all-gather | bytes 405504 | tf_op jit(solution)/shard_map/all_gather | solution.py:225
  156.8 8.4 all-gather.1
  165.2 70.0 %all_gather.50 = bf16[2048,96]{1,0:T(8,128)(2,1)S(1)} all-gather(bf16[64,96]{1,0:T(8,128)(2,1)S(1)} %copy-done.101), channel_id=1, replica_groups=mesh['dp'=8,'mp'=4] {'dp','mp'}, dimensions={0}, use_global_device_ids=true | all-gather | bytes 405504 | tf_op jit(solution)/shard_map/all_gather | solution.py:226
  236.6 9.0 all-gather.2
  246.2 9.5 all_gather.55
  272.5 10.5 fusion.233
  394.0 525.1 %while.101 = (s32[]{:T(128)}, f32[8,64,64]{2,1,0:T(8,128)S(1)}, f32[16,8,64,64]{2,3,1,0:T(8,128)}, f32[16,8,64,64]{3,1,2,0:T(8,128)}, f32[16,8,64,64]{3,1,2,0:T(...) while((s32[]{:T(128)}, f32[8,64,64]{2,1,0:T(8,128)S(1)}, ...), condition=%wide.region_5.6_spmd.clone.clone, body=%wide.region_3.0_spmd.clone.clone.sunk | while | flops 557228032 | bytes 25391976 | solution.py:161
  955.2 151.4 %all-reduce.28.cloned.1.call-done = bf16[1024,2048]{1,0:T(8,128)(2,1)} async-done(((bf16[1024,2048]{1,0:T(8,128)(2,1)}), bf16[1024,2048]{1,0:T(8,128)(2,1)}) %all-reduce.28.cloned.1.call-update) | async-done | bytes 4194320 | tf_op jit(solution)/shard_map/psum | solution.py:264
  1106.6 8.2 convert_add_fusion
  1129.9 32.2 all-gather.25.cloned.1.call-done
  1162.1 14.4 fusion.311
  1176.5 43.6 %all-gather.27.cloned.1.call-done = bf16[2048,2048]{1,0:T(8,128)(2,1)} async-done(((bf16[2048,256]{1,0:T(8,128)(2,1)}), bf16[2048,2048]{1,0:T(8,128)(2,1)}) %all-gather.27.cloned.1.call-update) | async-done | bytes 8388624 | tf_op jit(solution)/shard_map/all_gather | solution.py:222
  1220.1 15.0 convolution_convert_fusion.2
  1237.7 74.3 %reduce-scatter.20.cloned.1.call-done = bf16[1024,512]{1,0:T(8,128)(2,1)} async-done(((bf16[1024,2048]{1,0:T(8,128)(2,1)}), bf16[1024,512]{1,0:T(8,128)(2,1)}) %reduce-scatter.20.cloned.1.call-update) | async-done | bytes 1048592 | tf_op jit(solution)/shard_map/reduce_scatter | solution.py:272
  1315.7 81.4 %all-gather.29.cloned.1.call-done = bf16[1024,2048]{1,0:T(8,128)(2,1)} async-done(((bf16[1024,512]{1,0:T(8,128)(2,1)}), bf16[1024,2048]{1,0:T(8,128)(2,1)}) %all-gather.29.cloned.1.call-update) | async-done | bytes 4194320 | tf_op jit(solution)/shard_map/all_gather | solution.py:277
  1397.1 14.1 multiply_convert_fusion
  1411.2 12.8 fusion.312
  1431.6 8.6 split.8
  1440.2 14.2 multiply_reduce_fusion.3
  1477.8 8.4 copy_bitcast_fusion.21
  1486.2 130.6 %all-reduce.30.cloned.1.call-done = bf16[1024,2048]{1,0:T(8,128)(2,1)} async-done(((bf16[1024,2048]{1,0:T(8,128)(2,1)}), bf16[1024,2048]{1,0:T(8,128)(2,1)}) %all-reduce.30.cloned.1.call-update) | async-done | bytes 4194320 | tf_op jit(solution)/shard_map/psum | solution.py:285
  1616.7 8.7 fusion.297
  1641.0 7.9 fusion.244
  1664.1 1111.1 %while.102 = (s32[]{:T(128)}, f32[8,64,64]{2,1,0:T(8,128)S(1)}, f32[16,8,64,64]{3,2,1,0:T(8,128)}, f32[16,8,64,64]{3,2,1,0:T(8,128)}, f32[16,8,64,64]{3,2,1,0:T(...) while((s32[]{:T(128)}, f32[8,64,64]{2,1,0:T(8,128)S(1)}, ...), condition=%wide.region_25.26_spmd.clone.clone, body=%wide.region_20.25_spmd.clone.clone.sunk | while | flops 1111555584 | bytes 34787900 | solution.py:161
  2806.8 7.5 copy.393
  2853.6 7.4 copy.404
  2866.1 11.5 multiply_reduce_fusion.14
  2886.5 7.7 fusion.314
  2899.8 32.4 all-reduce.32.cloned.1.call-done
  2949.9 28.6 multiply_reduce_fusion.9
  2978.5 8.6 split.9
  2990.5 16.9 fusion.239
  3034.7 14.7 convolution_convert_fusion
  3049.7 14.0 convolution_convert_fusion.1
  3084.9 16.4 fusion.298
  3111.6 8.8 convert_add_fusion.1
  3123.6 20.5 reduce-scatter.44.cloned.1.call-done
  3145.5 39.8 %reduce-scatter.38.cloned.1.call-done = bf16[512,256]{1,0:T(8,128)(2,1)} async-done(((bf16[512,2048]{1,0:T(8,128)(2,1)}), bf16[512,256]{1,0:T(8,128)(2,1)}) %reduce-scatter.38.cloned.1.call-update) | async-done | bytes 262160 | tf_op jit(solution)/shard_map/reduce_scatter | solution.py:375
  3187.1 43.2 %reduce-scatter.34.cloned.1.call-done = bf16[256,512]{1,0:T(8,128)(2,1)} async-done(((bf16[2048,512]{1,0:T(8,128)(2,1)}), bf16[256,512]{1,0:T(8,128)(2,1)}) %reduce-scatter.34.cloned.1.call-update) | async-done | bytes 262160 | tf_op jit(solution)/shard_map/reduce_scatter | solution.py:357
  3232.1 43.5 %reduce-scatter.32.cloned.1.call-done = bf16[256,512]{1,0:T(8,128)(2,1)} async-done(((bf16[2048,512]{1,0:T(8,128)(2,1)}), bf16[256,512]{1,0:T(8,128)(2,1)}) %reduce-scatter.32.cloned.1.call-update) | async-done | bytes 262160 | tf_op jit(solution)/shard_map/reduce_scatter | solution.py:354
  3277.5 42.7 %reduce-scatter.36.cloned.1.call-done = bf16[256,512]{1,0:T(8,128)(2,1)} async-done(((bf16[2048,512]{1,0:T(8,128)(2,1)}), bf16[256,512]{1,0:T(8,128)(2,1)}) %reduce-scatter.36.cloned.1.call-update) | async-done | bytes 262160 | tf_op jit(solution)/shard_map/reduce_scatter | solution.py:360
  3322.0 73.2 %reduce-scatter.42.cloned.1.call-done = bf16[2048,256]{1,0:T(8,128)(2,1)} async-done(((bf16[2048,2048]{1,0:T(8,128)(2,1)}), bf16[2048,256]{1,0:T(8,128)(2,1)}) %reduce-scatter.42.cloned.1.call-update) | async-done | bytes 1048592 | tf_op jit(solution)/shard_map/reduce_scatter | solution.py:378
  3397.9 72.1 %reduce-scatter.40.cloned.1.call-done = bf16[256,2048]{1,0:T(8,128)(2,1)} async-done(((bf16[2048,2048]{1,0:T(8,128)(2,1)}), bf16[256,2048]{1,0:T(8,128)(2,1)}) %reduce-scatter.40.cloned.1.call-update) | async-done | bytes 1048592 | tf_op jit(solution)/shard_map/reduce_scatter | solution.py:372
  3472.8 76.4 %reduce-scatter.22.cloned.1.call-done = bf16[1024,512]{1,0:T(8,128)(2,1)} async-done(((bf16[1024,2048]{1,0:T(8,128)(2,1)}), bf16[1024,512]{1,0:T(8,128)(2,1)}) %reduce-scatter.22.cloned.1.call-update) | async-done | bytes 1048592 | tf_op jit(solution)/shard_map/reduce_scatter | solution.py:325
  3552.7 135.1 %reduce-scatter.24.cloned.1.call-done = f32[64,96]{1,0:T(8,128)} async-done(((f32[2048,96]{1,0:T(8,128)}), f32[64,96]{1,0:T(8,128)}) %reduce-scatter.24.cloned.1.call-update) | async-done | bytes 24592 | tf_op jit(solution)/shard_map/reduce_scatter | solution.py:344
  3687.9 134.7 %reduce-scatter.26.cloned.1.call-done = f32[64,96]{1,0:T(8,128)} async-done(((f32[2048,96]{1,0:T(8,128)}), f32[64,96]{1,0:T(8,128)}) %reduce-scatter.26.cloned.1.call-update) | async-done | bytes 24592 | tf_op jit(solution)/shard_map/reduce_scatter | solution.py:345
  3822.6 137.7 %reduce-scatter.28.cloned.1.call-done = f32[64,256]{1,0:T(8,128)} async-done(((f32[2048,256]{1,0:T(8,128)}), f32[64,256]{1,0:T(8,128)}) %reduce-scatter.28.cloned.1.call-update) | async-done | bytes 65552 | tf_op jit(solution)/shard_map/reduce_scatter | solution.py:346
  (1876 shorter events, 2070.5 us)
Async XLA Ops:
  7.2 158.0 %copy-start.101 = (bf16[64,96]{1,0:T(8,128)(2,1)S(1)}, bf16[64,96]{1,0:T(8,128)(2,1)}, u32[]{:S(2)}) copy-start(bf16[64,96]{1,0:T(8,128)(2,1)} %param.25) | copy-start | bytes 36868
  7.2 228.0 %copy-start.113 = (s32[8]{0:T(128)S(1)}, s32[8]{0:T(128)}, u32[]{:S(2)}) copy-start(s32[8]{0:T(128)} %param.22) | copy-start | bytes 100
  7.2 229.4 %copy-start.102 = (bf16[12,512]{1,0:T(8,128)(2,1)S(1)}, bf16[12,512]{1,0:T(8,128)(2,1)}, u32[]{:S(2)}) copy-start(bf16[12,512]{1,0:T(8,128)(2,1)} %param.28) | copy-start | bytes 36868
  7.2 239.0 %copy-start.98 = (bf16[32,512]{1,0:T(8,128)(2,1)S(1)}, bf16[32,512]{1,0:T(8,128)(2,1)}, u32[]{:S(2)}) copy-start(bf16[32,512]{1,0:T(8,128)(2,1)} %param.29) | copy-start | bytes 98308
  7.2 248.7 %all-gather.13.cloned.1.call-start = ((), (), s32[]{:S(2)}) async-start(), calls=%async_computation.13 | async-start | bytes 5242880 | tf_op jit(solution)/shard_map/all_gather | solution.py:212
  8.0 275.0 %all-gather.19.cloned.1.call-start = ((), (), s32[]{:S(2)}) async-start(), calls=%async_computation.16 | async-start | bytes 2359296 | tf_op jit(solution)/shard_map/all_gather | solution.py:214
  8.7 283.9 %all-gather.15.cloned.1.call-start = ((), (), s32[]{:S(2)}) async-start(), calls=%async_computation.14 | async-start | bytes 2359296 | tf_op jit(solution)/shard_map/all_gather | solution.py:215
  9.4 325.0 %all-gather.17.cloned.1.call-start = ((), (), s32[]{:S(2)}) async-start(), calls=%async_computation.15 | async-start | bytes 2359296 | tf_op jit(solution)/shard_map/all_gather | solution.py:216
  10.0 928.9 %all-gather.21.cloned.1.call-start = ((), (), s32[]{:S(2)}) async-start(), calls=%async_computation.17 | async-start | bytes 1081344 | tf_op jit(solution)/shard_map/all_gather | solution.py:227
  10.6 936.7 %all-gather.23.cloned.1.call-start = ((), (), s32[]{:S(2)}) async-start(), calls=%async_computation.18 | async-start | bytes 2359296 | tf_op jit(solution)/shard_map/all_gather | solution.py:221
  11.2 1095.4 %all-reduce.28.cloned.1.call-start = ((), (), s32[]{:S(2)}) async-start(), calls=%async_computation.19 | async-start | bytes 8388608 | tf_op jit(solution)/shard_map/psum | solution.py:264
  86.7 175.9 %copy-start.80 = (f32[2048,1]{0,1:T(1,128)}, f32[2048,1]{0,1:T(1,128)S(1)}, u32[]{:S(2)}) copy-start(f32[2048,1]{0,1:T(1,128)S(1)} %get-tuple-element.2564) | copy-start | bytes 24580
  86.7 182.5 %copy-start.71 = (f32[2048,1]{0,1:T(1,128)}, f32[2048,1]{0,1:T(1,128)S(1)}, u32[]{:S(2)}) copy-start(f32[2048,1]{0,1:T(1,128)S(1)} %get-tuple-element.2571) | copy-start | bytes 24580
  86.7 182.5 %copy-start.82 = (f32[2048,1]{0,1:T(1,128)}, f32[2048,1]{0,1:T(1,128)S(1)}, u32[]{:S(2)}) copy-start(f32[2048,1]{0,1:T(1,128)S(1)} %get-tuple-element.2565) | copy-start | bytes 24580
  86.7 182.5 %copy-start.84 = (f32[2048,1]{0,1:T(1,128)}, f32[2048,1]{0,1:T(1,128)S(1)}, u32[]{:S(2)}) copy-start(f32[2048,1]{0,1:T(1,128)S(1)} %get-tuple-element.2566) | copy-start | bytes 24580
  86.7 182.5 %copy-start.86 = (f32[2048,1]{0,1:T(1,128)}, f32[2048,1]{0,1:T(1,128)S(1)}, u32[]{:S(2)}) copy-start(f32[2048,1]{0,1:T(1,128)S(1)} %get-tuple-element.2567) | copy-start | bytes 24580
  86.7 182.5 %copy-start.88 = (f32[2048,1]{0,1:T(1,128)}, f32[2048,1]{0,1:T(1,128)S(1)}, u32[]{:S(2)}) copy-start(f32[2048,1]{0,1:T(1,128)S(1)} %get-tuple-element.2568) | copy-start | bytes 24580
  86.7 182.5 %copy-start.90 = (f32[2048,1]{0,1:T(1,128)}, f32[2048,1]{0,1:T(1,128)S(1)}, u32[]{:S(2)}) copy-start(f32[2048,1]{0,1:T(1,128)S(1)} %get-tuple-element.2569) | copy-start | bytes 24580
  156.8 149.2 %copy-start.40 = (bf16[2048,96]{1,0:T(8,128)(2,1)}, bf16[2048,96]{1,0:T(8,128)(2,1)S(1)}, u32[]{:S(2)}) copy-start(bf16[2048,96]{1,0:T(8,128)(2,1)S(1)} %all_gather.47) | copy-start | bytes 1179652
  165.2 145.2 %copy-start.60 = (bf16[96,512]{1,0:T(8,128)(2,1)}, bf16[96,512]{1,0:T(8,128)(2,1)S(1)}, u32[]{:S(2)}) copy-start(bf16[96,512]{1,0:T(8,128)(2,1)S(1)} %reshape.556) | copy-start | bytes 294916
  235.2 75.7 %copy-start.38 = (bf16[2048,96]{1,0:T(8,128)(2,1)}, bf16[2048,96]{1,0:T(8,128)(2,1)S(1)}, u32[]{:S(2)}) copy-start(bf16[2048,96]{1,0:T(8,128)(2,1)S(1)} %all_gather.50) | copy-start | bytes 1179652
  236.6 75.8 %copy-start.103 = (pred[1024]{0:T(1024)(128)(4,1)}, pred[1024]{0:T(1024)(128)(4,1)S(1)}, u32[]{:S(2)}) copy-start(pred[1024]{0:T(1024)(128)(4,1)S(1)} %convert_compare_fusion) | copy-start | bytes 3076
  255.8 56.6 %copy-start.99 = (f32[512,1]{0,1:T(1,128)}, f32[512,1]{0,1:T(1,128)S(1)}, u32[]{:S(2)}) copy-start(f32[512,1]{0,1:T(1,128)S(1)} %get-tuple-element.2572) | copy-start | bytes 6148
  255.9 56.6 %copy-start.105 = (f32[512,1]{0,1:T(1,128)}, f32[512,1]{0,1:T(1,128)S(1)}, u32[]{:S(2)}) copy-start(f32[512,1]{0,1:T(1,128)S(1)} %get-tuple-element.2575) | copy-start | bytes 6148
  255.9 56.6 %copy-start.107 = (f32[512,1]{0,1:T(1,128)}, f32[512,1]{0,1:T(1,128)S(1)}, u32[]{:S(2)}) copy-start(f32[512,1]{0,1:T(1,128)S(1)} %get-tuple-element.2577) | copy-start | bytes 6148
  953.7 208.4 %all-gather.25.cloned.1.call-start = ((), (), s32[]{:S(2)}) async-start(), calls=%async_computation.20 | async-start | bytes 9437184 | tf_op jit(solution)/shard_map/all_gather | solution.py:220
  954.4 265.7 %all-gather.27.cloned.1.call-start = ((), (), s32[]{:S(2)}) async-start(), calls=%async_computation.21 | async-start | bytes 9437184 | tf_op jit(solution)/shard_map/all_gather | solution.py:222
  955.2 356.9 %reduce-scatter.20.cloned.1.call-start = ((), (), s32[]{:S(2)}) async-start(), calls=%async_computation.22 | async-start | bytes 5242880 | tf_op jit(solution)/shard_map/reduce_scatter | solution.py:272
  1235.1 76.9 %copy-start.56 = (bf16[1024,512]{1,0:T(8,128)(2,1)S(1)}, bf16[1024,512]{1,0:T(8,128)(2,1)}, u32[]{:S(2)}) copy-start(bf16[1024,512]{1,0:T(8,128)(2,1)} %param.21) | copy-start | bytes 3145732
  1235.1 162.0 %all-gather.29.cloned.1.call-start = ((), (), s32[]{:S(2)}) async-start(), calls=%async_computation.23 | async-start | bytes 5242880 | tf_op jit(solution)/shard_map/all_gather | solution.py:277
  1315.7 301.0 %all-reduce.30.cloned.1.call-start = ((), (), s32[]{:S(2)}) async-start(), calls=%async_computation.24 | async-start | bytes 8388608 | tf_op jit(solution)/shard_map/psum | solution.py:285
  1463.1 1469.2 %all-reduce.32.cloned.1.call-start = ((), (), s32[]{:S(2)}) async-start(), calls=%async_computation.37 | async-start | bytes 1835008 | tf_op jit(solution)/shard_map/psum | solution.py:297
  2884.6 237.6 %reduce-scatter.30.cloned.1.call-start = ((), (), s32[]{:S(2)}) async-start(), calls=%async_computation.29 | async-start | bytes 294912 | tf_op jit(solution)/shard_map/reduce_scatter | solution.py:369
  2885.9 258.1 %reduce-scatter.44.cloned.1.call-start = ((), (), s32[]{:S(2)}) async-start(), calls=%async_computation.36 | async-start | bytes 1081344
  3009.1 176.3 %reduce-scatter.38.cloned.1.call-start = ((), (), s32[]{:S(2)}) async-start(), calls=%async_computation.33 | async-start | bytes 2359296 | tf_op jit(solution)/shard_map/reduce_scatter | solution.py:375
  3016.4 214.0 %reduce-scatter.34.cloned.1.call-start = ((), (), s32[]{:S(2)}) async-start(), calls=%async_computation.31 | async-start | bytes 2359296 | tf_op jit(solution)/shard_map/reduce_scatter | solution.py:357
  3022.4 253.3 %reduce-scatter.32.cloned.1.call-start = ((), (), s32[]{:S(2)}) async-start(), calls=%async_computation.30 | async-start | bytes 2359296 | tf_op jit(solution)/shard_map/reduce_scatter | solution.py:354
  3028.6 291.6 %reduce-scatter.36.cloned.1.call-start = ((), (), s32[]{:S(2)}) async-start(), calls=%async_computation.32 | async-start | bytes 2359296 | tf_op jit(solution)/shard_map/reduce_scatter | solution.py:360
  3034.7 360.6 %reduce-scatter.42.cloned.1.call-start = ((), (), s32[]{:S(2)}) async-start(), calls=%async_computation.35 | async-start | bytes 9437184 | tf_op jit(solution)/shard_map/reduce_scatter | solution.py:378
  3049.4 420.6 %reduce-scatter.40.cloned.1.call-start = ((), (), s32[]{:S(2)}) async-start(), calls=%async_computation.34 | async-start | bytes 9437184 | tf_op jit(solution)/shard_map/reduce_scatter | solution.py:372
  3063.8 485.4 %reduce-scatter.22.cloned.1.call-start = ((), (), s32[]{:S(2)}) async-start(), calls=%async_computation.25 | async-start | bytes 5242880 | tf_op jit(solution)/shard_map/reduce_scatter | solution.py:325
  3073.0 614.9 %reduce-scatter.24.cloned.1.call-start = ((), (), s32[]{:S(2)}) async-start(), calls=%async_computation.26 | async-start | bytes 1081344 | tf_op jit(solution)/shard_map/reduce_scatter | solution.py:344
  3075.8 746.8 %reduce-scatter.26.cloned.1.call-start = ((), (), s32[]{:S(2)}) async-start(), calls=%async_computation.27 | async-start | bytes 1081344 | tf_op jit(solution)/shard_map/reduce_scatter | solution.py:345
  3078.7 881.6 %reduce-scatter.28.cloned.1.call-start = ((), (), s32[]{:S(2)}) async-start(), calls=%async_computation.28 | async-start | bytes 2162688 | tf_op jit(solution)/shard_map/reduce_scatter | solution.py:346
  3101.3 19.0 collective-permute-start.2
  3102.6 18.0 collective-permute-start
  3103.9 16.4 collective-permute-start.3
  3109.3 11.3 collective-permute-start.1
  (99 other events, 683.9 us)
Sparse Core Ops, SparseCore 0:
  9.6 88.8 all-gather.12
  100.4 26.5 all-gather.18
  128.9 28.6 all-gather.14
  159.3 28.2 all-gather.16
  190.4 53.9 all-gather.20
  246.1 27.0 all-gather.22
  953.8 152.7 all-reduce.27
  1108.6 53.3 all-gather.24
  1164.1 55.9 all-gather.26
  1235.2 76.7 reduce-scatter.19
  1315.8 81.2 all-gather.28
  1463.2 153.4 all-reduce.29
  2884.8 47.4 all-reduce.31
  2935.4 32.8 reduce-scatter.29
  3009.2 134.8 reduce-scatter.43
  3147.5 37.7 reduce-scatter.37
  3189.0 41.2 reduce-scatter.33
  3234.4 41.2 reduce-scatter.31
  3278.9 41.2 reduce-scatter.35
  3323.9 71.2 reduce-scatter.41
  3398.7 71.2 reduce-scatter.39
  3472.4 76.7 reduce-scatter.21
  3552.0 135.8 reduce-scatter.23
  3690.6 131.9 reduce-scatter.25
  3825.5 134.7 reduce-scatter.27
where the time goes:
time: 4000 us; the launch traced here: 3970 us
  matrix products  1550 us (39%)
  waiting for transfers between devices  1370 us (34%)
  local copies, waits for them, and re-layouts  413 us (10%)
  other arithmetic  335 us (8%)
  blocking collectives  258 us (6%)
    dot_general x240, matrix products, unit_lower_inverse(): accum = accum + product('bts,bsu->btu', accum, power)  333 us
    dot_general x240, matrix products, unit_lower_inverse(): power = product('bts,bsu->btu', power, power)  333 us
    psum x1, waiting for transfers between devices, body(): lax.psum(matmul(gated_low, output_w).astype(jnp.bfloat16), 'mp')  151 us
    reduce_scatter x1, waiting for transfers between devices, body(): lax.psum_scatter(grad_gate_down, ('dp', 'mp'), scatter_dimension=0, tiled...  138 us
    reduce_scatter x1, waiting for transfers between devices, body(): lax.psum_scatter(grad_decay_down, ('dp', 'mp'), scatter_dimension=0, tile...  135 us
    reduce_scatter x1, waiting for transfers between devices, body(): lax.psum_scatter(grad_rate_down, ('dp', 'mp'), scatter_dimension=0, tiled...  135 us
    psum x1, waiting for transfers between devices, body(): lax.psum(d_resid_part.astype(jnp.bfloat16), 'mp').astype(jnp.float32)  131 us
    dynamic_slice x112, local copies, waits for them, and re-layouts, time_mixer(): final_state, outputs = lax.scan(block_step, start_state, arranged)  115 us
  transfers between devices with their start and end apart: 29, of which 18 were waited for; matrix products, arithmetic and copies ran while one was open for 24% of the time, Pallas kernels for 0%

commit v1 on v0

v1 whole, which is shorter than its diff:
```python
from functools import partial
import math

import jax
import jax.numpy as jnp
from jax import lax
from jax.experimental import pallas as pl
from jax.experimental.pallas import tpu as pltpu
from jax.sharding import PartitionSpec as P

norm_eps = 1e-05
SUBSPACE_SIZE = 64
SEQ_LEN = 1024
group_eps = 0.00064
CHUNK = 64
PAIR = 2 * SUBSPACE_SIZE
CHUNKS_FWD = 2
CHUNKS_BWD = 2
DECAY_SCALE = math.exp(-0.5)


def dot_nn(left_op, right_op):
    return lax.dot_general(left_op, right_op, (((1,), (0,)), ((), ())), preferred_element_type=jnp.float32)


def dot_nt(left_op, right_op):
    return lax.dot_general(left_op, right_op, (((1,), (1,)), ((), ())), preferred_element_type=jnp.float32)


def dot_tn(left_op, right_op):
    return lax.dot_general(left_op, right_op, (((0,), (0,)), ((), ())), preferred_element_type=jnp.float32)


def low(values):
    return values.astype(jnp.bfloat16)


def split_dot(ones_op, values):
    top = low(values)
    rest = values - top.astype(jnp.float32)
    mid = low(rest)
    tail = low(rest - mid.astype(jnp.float32))
    return dot_nn(ones_op, top) + dot_nn(ones_op, mid) + dot_nn(ones_op, tail)


def halves(values):
    top = low(values)
    return top, low(values - top.astype(jnp.float32))


def iota(shape, axis):
    return lax.broadcasted_iota(jnp.int32, shape, axis)


def head_masks():
    lane = iota((CHUNK, PAIR), 1)
    return lane < SUBSPACE_SIZE


def stack_heads(values):
    first = iota(values.shape, 1) < SUBSPACE_SIZE
    zero = jnp.zeros_like(values)
    return jnp.concatenate(
        [jnp.where(first, values, zero), jnp.where(first, zero, values)], axis=0
    )


def fold_heads(values):
    first = iota((CHUNK, PAIR), 1) < SUBSPACE_SIZE
    return jnp.where(first, values[:CHUNK], values[CHUNK:])


def head_ones():
    return (
        iota((PAIR, PAIR), 0) // SUBSPACE_SIZE == iota((PAIR, PAIR), 1) // SUBSPACE_SIZE
    )


def head_sum(values, ones_op):
    top = low(values)
    rest = low(values - top.astype(jnp.float32))
    return dot_nn(top, ones_op) + dot_nn(rest, ones_op)


def lower_inverses(lower_parts):
    row = iota((CHUNK, PAIR), 0)
    col = iota((CHUNK, PAIR), 1) % CHUNK
    eye = jnp.where(row == col, 1.0, 0.0)

    def times(lefts, rights):
        return [
            dot_nn(low(left_op), stack_heads(low(right_op)))
            for left_op, right_op in zip(lefts, rights)
        ]

    def plus(*lists):
        return [sum(members[1:], members[0]) for members in zip(*lists)]

    near = row // 8 == col // 8
    base = [jnp.where(near, part, 0.0) for part in lower_parts]
    square = times(base, base)
    cube = times(base, square)
    fourth = times(square, square)
    accum = [eye + first + second + third for first, second, third in zip(base, square, cube)]
    accum = plus(accum, times(accum, fourth))
    width = 8
    while width < CHUNK:
        level = (row // (2 * width) == col // (2 * width)) & (row // width != col // width)
        off = [jnp.where(level, part, 0.0) for part in lower_parts]
        accum = plus(accum, times(times(accum, off), accum))
        width *= 2
    return accum


def prepare(r, k, dw, da, cols, live, tri_op, ones_op):
    sw = jax.nn.sigmoid(dw + cols[0:1])
    full_log = -DECAY_SCALE * sw
    log_decay = jnp.where(live, full_log, 0.0)
    rate = jax.nn.sigmoid(da + cols[1:2])
    scaled = k * cols[2:3]
    inv = lax.rsqrt(head_sum(scaled * scaled, ones_op) + 1e-06)
    unit = scaled * inv
    unit_live = jnp.where(live, unit, 0.0)
    lag_scale = 1.0 + (rate - 1.0) * cols[3:4]
    lagged = jnp.where(live, k * lag_scale, 0.0)
    running = split_dot(tri_op, log_decay)
    grown = jnp.exp(running)
    before = jnp.exp(running - log_decay)
    shrunk = jnp.exp(-running)
    last = running[CHUNK - 1 : CHUNK]
    til_end = jnp.exp(last - running)
    write = unit_live * rate
    return dict(
        sw=sw,
        full_log=full_log,
        rate=rate,
        inv=inv,
        unit=unit,
        unit_live=unit_live,
        lag_scale=lag_scale,
        lagged=lagged,
        grown=grown,
        before=before,
        shrunk=shrunk,
        til_end=til_end,
        final=jnp.exp(last),
        read_wide=r * grown,
        write_wide=write * shrunk,
        key_wide=lagged * shrunk,
        read_hat=low(r * grown),
        remove_hat=low(-unit_live * before),
        write_hat=low(write * shrunk),
        key_hat=low(lagged * shrunk),
        write_end=low(write * til_end),
        key_end=low(lagged * til_end),
    )


def tri_masks():
    row = iota((CHUNK, PAIR), 0)
    col = iota((CHUNK, PAIR), 1) % CHUNK
    return row > col, row >= col


def mixer_forward(
    steps_per_seq,
    length_ref,
    r_ref,
    k_ref,
    v_ref,
    dw_ref,
    da_ref,
    gate_ref,
    cols_ref,
    z_ref,
    y_ref,
    t_ref,
    u_ref,
    s_ref,
    lk_ref,
    reads_ref,
    state,
):
    step = pl.program_id(0)
    within_seq = lax.rem(step, steps_per_seq)
    length = length_ref[step // steps_per_seq]

    @pl.when(within_seq == 0)
    def _():
        state[...] = jnp.zeros_like(state)

    rows_each = r_ref.shape[0]
    chunks = rows_each // CHUNK
    pairs = r_ref.shape[1] // PAIR
    ones_mask = head_ones()
    ones_op = jnp.where(ones_mask, 1.0, 0.0).astype(jnp.bfloat16)
    tri_op = jnp.where(iota((CHUNK, CHUNK), 0) >= iota((CHUNK, CHUNK), 1), 1.0, 0.0).astype(jnp.bfloat16)
    strict, within = tri_masks()
    within_two = jnp.concatenate([within, within], axis=1)
    units = [(chunk, pair) for chunk in range(chunks) for pair in range(pairs)]

    def place_of(unit):
        chunk, pair = unit
        return slice(chunk * CHUNK, (chunk + 1) * CHUNK), slice(pair * PAIR, (pair + 1) * PAIR)

    prepared, scored, lower_parts = [], [], []
    for unit in units:
        rows, lanes = place_of(unit)
        live = within_seq * rows_each + unit[0] * CHUNK + iota((CHUNK, PAIR), 0) < length
        got = prepare(
            r_ref[rows, lanes],
            k_ref[rows, lanes],
            dw_ref[rows, lanes],
            da_ref[rows, lanes],
            cols_ref[:, lanes],
            live,
            tri_op,
            ones_op,
        )
        prepared.append(got)
    for unit, got in zip(units, prepared):
        got["both"] = jnp.concatenate([got["remove_hat"], got["read_hat"]], axis=0)
        past = jnp.concatenate([stack_heads(got["write_hat"]), stack_heads(got["key_hat"])], axis=0)
        scores = dot_nt(got["both"], past)
        past_rest = jnp.concatenate(
            [stack_heads(halves(got["write_wide"])[1]), stack_heads(halves(got["key_wide"])[1])], axis=0
        )
        got["read_rest"] = halves(got["read_wide"])[1]
        fine = scores[CHUNK:] + (dot_nt(got["read_rest"], past) + dot_nt(got["read_hat"], past_rest))
        lower_parts.append(jnp.where(strict, scores[:CHUNK, :PAIR], 0.0))
        lower_key = low(jnp.where(strict, scores[:CHUNK, PAIR:], 0.0))
        reads = low(jnp.where(within_two, fine, 0.0))
        scored.append((lower_key, reads))
    solves = [low(part) for part in lower_inverses(lower_parts)]
    for unit, solve in zip(units, solves):
        t_ref[place_of(unit)] = solve
    for chunk in range(chunks):
        group = [index for index, unit in enumerate(units) if unit[0] == chunk]
        lows = [low(v_ref[place_of(units[index])]) for index in group]
        stacks = [stack_heads(values) for values in lows]
        olds = [state[units[index][1]] for index in group]
        old_parts = [halves(old) for old in olds]
        from_state = [dot_nt(prepared[index]["both"], old[0]) for index, old in zip(group, old_parts)]
        read_state = [
            part[CHUNK:]
            + (dot_nt(prepared[index]["read_rest"], old[0]) + dot_nt(prepared[index]["read_hat"], old[1]))
            for index, part, old in zip(group, from_state, old_parts)
        ]
        right = [
            low(part[:CHUNK] + dot_nn(scored[index][0], stack))
            for index, part, stack in zip(group, from_state, stacks)
        ]
        removed = [low(dot_nn(solves[index], stack_heads(part))) for index, part in zip(group, right)]
        for slot, index in enumerate(group):
            pair = units[index][1]
            got = prepared[index]
            ends = jnp.concatenate([got["write_end"], got["key_end"]], axis=0)
            adds = dot_tn(jnp.concatenate([removed[slot], lows[slot]], axis=0), ends)
            state[pair] = olds[slot] * got["final"] + jnp.where(ones_mask, adds, 0.0)
            u_ref[place_of(units[index])] = removed[slot]
            rows, lanes = place_of(units[index])
            lk_ref[rows, lanes], reads_ref[rows, slice(2 * lanes.start, 2 * lanes.stop)] = scored[index]
            s_ref[chunk, pair] = olds[slot]
        outs = [
            read_state[slot]
            + dot_nn(scored[index][1], jnp.concatenate([stack_heads(removed[slot]), stacks[slot]], axis=0))
            for slot, index in enumerate(group)
        ]
        centred = [y - head_sum(y, ones_op) * (1.0 / SUBSPACE_SIZE) for y in outs]
        spread = [head_sum(part * part, ones_op) * (1.0 / SUBSPACE_SIZE) for part in centred]
        for slot, index in enumerate(group):
            rows, lanes = place_of(units[index])
            cols = cols_ref[:, lanes]
            normed = centred[slot] * lax.rsqrt(spread[slot] + group_eps)
            bonus = head_sum(r_ref[rows, lanes] * prepared[index]["lagged"] * cols[4:5], ones_op)
            mixed = normed * cols[5:6] + cols[6:7] + bonus * v_ref[rows, lanes]
            y_ref[rows, lanes] = outs[slot]
            z_ref[rows, lanes] = low(mixed * gate_ref[rows, lanes])


def mixer_backward(
    steps_per_seq,
    length_ref,
    r_ref,
    k_ref,
    v_ref,
    dw_ref,
    da_ref,
    gate_ref,
    cols_ref,
    y_ref,
    t_ref,
    u_ref,
    s_ref,
    lk_ref,
    reads_ref,
    dz_ref,
    dr_ref,
    dk_ref,
    dv_ref,
    ddw_ref,
    dda_ref,
    dgate_ref,
    dcols_ref,
    dstate,
):
    step = pl.num_programs(0) - 1 - pl.program_id(0)
    within_seq = lax.rem(step, steps_per_seq)
    length = length_ref[step // steps_per_seq]

    @pl.when(within_seq == steps_per_seq - 1)
    def _():
        dstate[...] = jnp.zeros_like(dstate)

    @pl.when(pl.program_id(0) == 0)
    def _():
        dcols_ref[...] = jnp.zeros_like(dcols_ref)

    rows_each = r_ref.shape[0]
    chunks = rows_each // CHUNK
    pairs = r_ref.shape[1] // PAIR
    ones_mask = head_ones()
    ones_op = jnp.where(ones_mask, 1.0, 0.0).astype(jnp.bfloat16)
    row = iota((CHUNK, CHUNK), 0)
    col = iota((CHUNK, CHUNK), 1)
    tri_op = jnp.where(row >= col, 1.0, 0.0).astype(jnp.bfloat16)
    suffix_op = jnp.where(row <= col, 1.0, 0.0).astype(jnp.bfloat16)
    prefix_op = jnp.where(row > col, 1.0, 0.0).astype(jnp.bfloat16)
    sums_op = jnp.concatenate([suffix_op, prefix_op], axis=1)
    strict, within = tri_masks()

    def add_col(index, lanes, values):
        part = values[0:8]
        for start in range(8, CHUNK, 8):
            part = part + values[start : start + 8]
        dcols_ref[index, :, lanes] += part

    strict_two = jnp.concatenate([strict, strict], axis=1)
    within_two = jnp.concatenate([within, within], axis=1)
    all_masks = jnp.concatenate([strict_two, within_two], axis=0)
    units = [(chunk, pair) for chunk in reversed(range(chunks)) for pair in range(pairs)]
    mean_of = 1.0 / SUBSPACE_SIZE
    known = []
    for chunk, pair in units:
        rows = slice(chunk * CHUNK, (chunk + 1) * CHUNK)
        lanes = slice(pair * PAIR, (pair + 1) * PAIR)
        live = within_seq * rows_each + chunk * CHUNK + iota((CHUNK, PAIR), 0) < length
        cols = cols_ref[:, lanes]
        got = prepare(
            r_ref[rows, lanes],
            k_ref[rows, lanes],
            dw_ref[rows, lanes],
            da_ref[rows, lanes],
            cols,
            live,
            tri_op,
            ones_op,
        )
        got.update(rows=rows, lanes=lanes, live=live, cols=cols, pair=pair, chunk=chunk)
        known.append(got)
    for got in known:
        y = y_ref[got["rows"], got["lanes"]]
        got["centred"] = y - head_sum(y, ones_op) * mean_of
    for got in known:
        spread = head_sum(got["centred"] * got["centred"], ones_op) * mean_of
        got["inv_y"] = lax.rsqrt(spread + group_eps)
    for got in known:
        rows, lanes, cols = got["rows"], got["lanes"], got["cols"]
        r, v, dz = r_ref[rows, lanes], v_ref[rows, lanes], dz_ref[rows, lanes]
        normed = got["centred"] * got["inv_y"]
        got["bonus"] = head_sum(r * got["lagged"] * cols[4:5], ones_op)
        mixed = normed * cols[5:6] + cols[6:7] + got["bonus"] * v
        dgate_ref[rows, lanes] = low(dz * mixed)
        dmix = dz * gate_ref[rows, lanes]
        add_col(5, lanes, dmix * normed)
        add_col(6, lanes, dmix)
        dnormed = dmix * cols[5:6]
        got["dbonus"] = head_sum(dmix * v, ones_op)
        mean_grad = head_sum(dnormed, ones_op) * mean_of
        mean_prod = head_sum(dnormed * normed, ones_op) * mean_of
        got["dy_low"], got["dy_rest"] = halves(got["inv_y"] * (dnormed - mean_grad - normed * mean_prod))
        got["dv"] = got["bonus"] * dmix
    for got in known:
        rows, lanes = got["rows"], got["lanes"]
        got["both"] = jnp.concatenate([got["remove_hat"], got["read_hat"]], axis=0)
        got["past"] = jnp.concatenate(
            [stack_heads(got["write_hat"]), stack_heads(got["key_hat"])], axis=0
        )
        got["lower_key"] = lk_ref[rows, lanes]
        reads = reads_ref[rows, slice(2 * lanes.start, 2 * lanes.stop)]
        got["from_y"] = dot_tn(reads, got["dy_low"])
        v_low = low(v_ref[rows, lanes])
        removed = u_ref[rows, lanes]
        got["sent"] = jnp.concatenate([removed, v_low], axis=0)
        got["stacks"] = jnp.concatenate([stack_heads(removed), stack_heads(v_low)], axis=0)
    for chunk in reversed(range(chunks)):
        group = [got for got in known if got["chunk"] == chunk]
        for got in group:
            got["later"] = dstate[got["pair"]]
            got["later_low"], got["later_rest"] = halves(got["later"])
            ends = jnp.concatenate([got["write_end"], got["key_end"]], axis=0)
            got["from_later"] = dot_nt(ends, got["later_low"])
        for got in group:
            dremoved = low(got["from_later"][:CHUNK] + fold_heads(got["from_y"][:PAIR]))
            got["dright"] = low(fold_heads(dot_tn(t_ref[got["rows"], got["lanes"]], dremoved)))
        for got in group:
            got["douts"] = jnp.concatenate([got["dright"], got["dy_low"]], axis=0)
            adds = dot_tn(got["douts"], got["both"]) + dot_tn(got["dy_rest"], got["read_hat"])
            adds = jnp.where(ones_mask, adds, 0.0)
            dstate[got["pair"]] = got["later"] * got["final"] + adds
    for got in known:
        dv = got["dv"] + got["from_later"][CHUNK:] + fold_heads(got["from_y"][PAIR:])
        dv = dv + fold_heads(dot_tn(got["lower_key"], got["dright"]))
        dv_ref[got["rows"], got["lanes"]] = low(dv)
        dscores = dot_nt(got["douts"], got["stacks"])
        fine = dscores[CHUNK:] + dot_nt(got["dy_rest"], got["stacks"])
        dscores = low(jnp.where(all_masks, jnp.concatenate([dscores[:CHUNK], fine], axis=0), 0.0))
        old_wide = s_ref[got["chunk"], got["pair"]]
        old_low, old_rest = halves(old_wide)
        from_old = dot_nn(got["douts"], old_low)
        fine = from_old[CHUNK:] + (dot_nn(got["dy_rest"], old_low) + dot_nn(got["dy_low"], old_rest))
        got["dboth"] = jnp.concatenate([from_old[:CHUNK], fine], axis=0) + dot_nn(dscores, got["past"])
        dpast = dot_tn(dscores, got["both"])
        got["dwrite_hat"] = fold_heads(dpast[:PAIR])
        got["dkey_hat"] = fold_heads(dpast[PAIR:])
        got["dends"] = dot_nn(got["sent"], got["later_low"]) + dot_nn(got["sent"], got["later_rest"])
        got["dfinal"] = jnp.sum(got["later"] * old_wide, axis=0, keepdims=True)
    for got in known:
        rows, lanes, cols, live = got["rows"], got["lanes"], got["cols"], got["live"]

        def wide(name):
            return got[name].astype(jnp.float32)

        r, k = r_ref[rows, lanes], k_ref[rows, lanes]
        dwrite_hat, dkey_hat = got["dwrite_hat"], got["dkey_hat"]
        dwrite_end, dkey_end = got["dends"][:CHUNK], got["dends"][CHUNK:]
        dremove_hat, dread_hat = got["dboth"][:CHUNK], got["dboth"][CHUNK:]
        dbonus, lagged = got["dbonus"], got["lagged"]
        bonus_lag = dbonus * lagged
        add_col(4, lanes, bonus_lag * r)
        dr_ref[rows, lanes] = low(bonus_lag * cols[4:5] + dread_hat * got["grown"])
        minus = wide("remove_hat") * dremove_hat
        plus = wide("read_hat") * dread_hat + minus
        plus = plus - wide("write_hat") * dwrite_hat - wide("key_hat") * dkey_hat
        ending = wide("write_end") * dwrite_end + wide("key_end") * dkey_end
        sums = split_dot(sums_op, jnp.concatenate([plus, ending], axis=0))
        dlog = sums - minus + got["final"] * got["dfinal"]
        ddw = jnp.where(live, dlog * got["full_log"] * (1.0 - got["sw"]), 0.0)
        add_col(0, lanes, ddw)
        ddw_ref[rows, lanes] = low(ddw)
        dwrite = dwrite_hat * got["shrunk"] + dwrite_end * got["til_end"]
        dlag = dbonus * r * cols[4:5] + dkey_hat * got["shrunk"] + dkey_end * got["til_end"]
        dlag = jnp.where(live, dlag, 0.0)
        rate = got["rate"]
        dunit = jnp.where(live, dwrite * rate - dremove_hat * got["before"], 0.0)
        lag_k = dlag * k
        drate = dwrite * got["unit_live"] + lag_k * cols[3:4]
        add_col(3, lanes, lag_k * (rate - 1.0))
        dscaled = got["inv"] * (dunit - got["unit"] * head_sum(dunit * got["unit"], ones_op))
        add_col(2, lanes, dscaled * k)
        dk_ref[rows, lanes] = low(dlag * got["lag_scale"] + dscaled * cols[2:3])
        dda = drate * rate * (1.0 - rate)
        add_col(1, lanes, dda)
        dda_ref[rows, lanes] = low(dda)


def run_mixer_forward(lengths, r, k, v, dw, da, gate, cols):
    positions, part_width = r.shape
    rows_each = CHUNKS_FWD * CHUNK
    steps = positions // rows_each
    steps_per_seq = SEQ_LEN // rows_each
    pairs = part_width // PAIR
    wide = pl.BlockSpec((rows_each, part_width), lambda i: (i, 0))
    shape = jax.ShapeDtypeStruct
    return pl.pallas_call(
        partial(mixer_forward, steps_per_seq),
        grid=(steps,),
        in_specs=[pl.BlockSpec(memory_space=pltpu.SMEM)]
        + [wide] * 6
        + [pl.BlockSpec((8, part_width), lambda i: (0, 0))],
        out_specs=[wide] * 4
        + [
            pl.BlockSpec((CHUNKS_FWD, pairs, PAIR, PAIR), lambda i: (i, 0, 0, 0)),
            wide,
            pl.BlockSpec((rows_each, 2 * part_width), lambda i: (i, 0)),
        ],
        out_shape=[
            shape((positions, part_width), jnp.bfloat16),
            shape((positions, part_width), jnp.float32),
            shape((positions, part_width), jnp.bfloat16),
            shape((positions, part_width), jnp.bfloat16),
            shape((positions // CHUNK, pairs, PAIR, PAIR), jnp.float32),
            shape((positions, part_width), jnp.bfloat16),
            shape((positions, 2 * part_width), jnp.bfloat16),
        ],
        scratch_shapes=[pltpu.VMEM((pairs, PAIR, PAIR), jnp.float32)],
        compiler_params=pltpu.CompilerParams(
            dimension_semantics=("arbitrary",), vmem_limit_bytes=40 * 1024 * 1024
        ),
        name="mixer_forward",
    )(lengths, r, k, v, dw, da, gate, cols)


def run_mixer_backward(lengths, r, k, v, dw, da, gate, cols, y, t, u, s, lk, reads, dz):
    positions, part_width = r.shape
    rows_each = CHUNKS_BWD * CHUNK
    steps = positions // rows_each
    steps_per_seq = SEQ_LEN // rows_each
    pairs = part_width // PAIR
    wide = pl.BlockSpec((rows_each, part_width), lambda i: (steps - 1 - i, 0))
    shape = jax.ShapeDtypeStruct
    return pl.pallas_call(
        partial(mixer_backward, steps_per_seq),
        grid=(steps,),
        in_specs=[pl.BlockSpec(memory_space=pltpu.SMEM)]
        + [wide] * 6
        + [pl.BlockSpec((8, part_width), lambda i: (0, 0))]
        + [wide] * 3
        + [
            pl.BlockSpec((CHUNKS_BWD, pairs, PAIR, PAIR), lambda i: (steps - 1 - i, 0, 0, 0)),
            wide,
            pl.BlockSpec((rows_each, 2 * part_width), lambda i: (steps - 1 - i, 0)),
            wide,
        ],
        out_specs=[wide] * 6 + [pl.BlockSpec((8, 8, part_width), lambda i: (0, 0, 0))],
        out_shape=[shape((positions, part_width), jnp.bfloat16)] * 6
        + [shape((8, 8, part_width), jnp.float32)],
        scratch_shapes=[pltpu.VMEM((pairs, PAIR, PAIR), jnp.float32)],
        compiler_params=pltpu.CompilerParams(
            dimension_semantics=("arbitrary",), vmem_limit_bytes=40 * 1024 * 1024
        ),
        name="mixer_backward",
    )(lengths, r, k, v, dw, da, gate, cols, y, t, u, s, lk, reads, dz)


LINE = "mp"
END_LAG = 4
MID_LAG = 2


def link_cost(elements):
    return elements * 2 * 2 * 40


def line_barrier(size):
    me = lax.axis_index(LINE)
    barrier = pltpu.get_barrier_semaphore()

    @pl.when(me > 0)
    def _():
        pl.semaphore_signal(barrier, inc=1, device_id={LINE: me - 1}, device_id_type=pl.DeviceIdType.MESH)

    @pl.when(me < size - 1)
    def _():
        pl.semaphore_signal(barrier, inc=1, device_id={LINE: me + 1}, device_id_type=pl.DeviceIdType.MESH)

    ends = jnp.where((me == 0) | (me == size - 1), 1, 2)
    pl.semaphore_wait(barrier, ends)


class Flow:
    def __init__(self, size, side):
        self.size = size
        self.side = side
        self.me = lax.axis_index(LINE)
        self.step = 1 - 2 * side
        self.target = self.me + self.step
        source = self.me - self.step
        self.has_source = (source >= 0) & (source < size)
        self.has_target = (self.target >= 0) & (self.target < size)

    def copy(self, source, place, send_sem, recv_sem):
        return pltpu.make_async_remote_copy(
            src_ref=source,
            dst_ref=place,
            send_sem=send_sem,
            recv_sem=recv_sem,
            device_id={LINE: self.target},
            device_id_type=pl.DeviceIdType.MESH,
        )


def two_flows(size):
    me = lax.axis_index(LINE)
    near = jnp.where(me < size // 2, 0, 1)
    return Flow(size, near), Flow(size, 1 - near)


def line_sum_kernel(size, chunk_rows, x_ref, out_ref, got, sent, send_sem, recv_sem):
    line_barrier(size)
    me = lax.axis_index(LINE)
    flows = two_flows(size)
    chunks = x_ref.shape[0] // chunk_rows

    def copy_of(flow, chunk, source):
        rows = pl.ds(pl.multiple_of(chunk * chunk_rows, chunk_rows), chunk_rows)
        return flow.copy(
            source.at[rows], got.at[flow.side, rows], send_sem.at[flow.side, chunk], recv_sem.at[flow.side, chunk]
        )

    def pass_on(flow, chunk):
        rows = pl.ds(pl.multiple_of(chunk * chunk_rows, chunk_rows), chunk_rows)

        @pl.when(flow.has_source)
        def _():
            copy_of(flow, chunk, x_ref).wait_recv()

        @pl.when(flow.has_source & flow.has_target)
        def _():
            total = got[flow.side, rows].astype(jnp.float32) + x_ref[rows].astype(jnp.float32)
            sent[flow.side, rows] = total.astype(sent.dtype)
            copy_of(flow, chunk, sent.at[flow.side]).start()

        @pl.when(jnp.logical_not(flow.has_source))
        def _():
            copy_of(flow, chunk, x_ref).start()

    is_end = (me == 0) | (me == size - 1)
    lag = jnp.where(is_end, END_LAG, MID_LAG)

    def step(turn, carry):
        @pl.when(turn < chunks)
        def _():
            pass_on(flows[0], turn)

        chunk = turn - lag

        @pl.when((chunk >= 0) & (chunk < chunks))
        def _():
            pass_on(flows[1], chunk)
            rows = pl.ds(pl.multiple_of(chunk * chunk_rows, chunk_rows), chunk_rows)

            @pl.when(is_end)
            def _():
                other = got[flows[1].side, rows].astype(jnp.float32)
                out_ref[rows] = (other + x_ref[rows].astype(jnp.float32)).astype(out_ref.dtype)

            @pl.when(jnp.logical_not(is_end))
            def _():
                other = got[0, rows].astype(jnp.float32) + got[1, rows].astype(jnp.float32)
                out_ref[rows] = (other + x_ref[rows].astype(jnp.float32)).astype(out_ref.dtype)

        return carry

    lax.fori_loop(0, chunks + END_LAG, step, 0)

    def drain(chunk, carry):
        for flow in flows:

            @pl.when(flow.has_target)
            def _():
                copy_of(flow, chunk, x_ref).wait_send()

        return carry

    lax.fori_loop(0, chunks, drain, 0)


def line_sum(x, size, collective_id, chunk_rows=64):
    rows, cols = x.shape
    chunks = rows // chunk_rows
    return pl.pallas_call(
        partial(line_sum_kernel, size, chunk_rows),
        out_shape=jax.ShapeDtypeStruct(x.shape, x.dtype),
        in_specs=[pl.BlockSpec(memory_space=pltpu.VMEM)],
        out_specs=pl.BlockSpec(memory_space=pltpu.VMEM),
        scratch_shapes=[
            pltpu.VMEM((2, rows, cols), x.dtype),
            pltpu.VMEM((2, rows, cols), x.dtype),
            pltpu.SemaphoreType.DMA((2, chunks)),
            pltpu.SemaphoreType.DMA((2, chunks)),
        ],
        compiler_params=pltpu.CompilerParams(
            collective_id=collective_id, has_side_effects=True, vmem_limit_bytes=48 * 1024 * 1024
        ),
        cost_estimate=pl.CostEstimate(flops=0, bytes_accessed=link_cost(rows * cols), transcendentals=0),
        name="line_sum",
    )(x)


def line_gather_kernel(size, chunk_rows, x_ref, out_ref, send_sem, recv_sem):
    line_barrier(size)
    me = lax.axis_index(LINE)
    flows = two_flows(size)
    width = x_ref.shape[1]
    chunks = x_ref.shape[0] // chunk_rows

    def place(block, chunk):
        rows = pl.ds(pl.multiple_of(chunk * chunk_rows, chunk_rows), chunk_rows)
        return out_ref.at[rows, pl.ds(pl.multiple_of(block * width, width), width)]

    def copy_of(flow, block, chunk):
        return flow.copy(
            place(block, chunk), place(block, chunk), send_sem.at[flow.side, block, chunk], recv_sem.at[flow.side, block, chunk]
        )

    def step(chunk, carry):
        rows = pl.ds(pl.multiple_of(chunk * chunk_rows, chunk_rows), chunk_rows)
        out_ref[rows, pl.ds(pl.multiple_of(me * width, width), width)] = x_ref[rows]
        for flow in flows:

            @pl.when(flow.has_target)
            def _():
                copy_of(flow, me, chunk).start()

        return carry

    lax.fori_loop(0, chunks, step, 0)
    for hop in range(1, size):

        def forward(chunk, carry):
            for flow in flows:
                block = me - hop * flow.step
                exists = (block >= 0) & (block < size)

                @pl.when(exists)
                def _():
                    copy_of(flow, block, chunk).wait_recv()

                @pl.when(exists & flow.has_target)
                def _():
                    copy_of(flow, block, chunk).start()

            return carry

        lax.fori_loop(0, chunks, forward, 0)
    for hop in range(size):

        def drain(chunk, carry):
            for flow in flows:
                block = me - hop * flow.step
                exists = (block >= 0) & (block < size)

                @pl.when(exists & flow.has_target)
                def _():
                    copy_of(flow, block, chunk).wait_send()

            return carry

        lax.fori_loop(0, chunks, drain, 0)


def line_gather(x, size, collective_id, chunk_rows=256):
    rows, cols = x.shape
    chunks = rows // chunk_rows
    return pl.pallas_call(
        partial(line_gather_kernel, size, chunk_rows),
        out_shape=jax.ShapeDtypeStruct((rows, size * cols), x.dtype),
        in_specs=[pl.BlockSpec(memory_space=pltpu.VMEM)],
        out_specs=pl.BlockSpec(memory_space=pltpu.VMEM),
        scratch_shapes=[
            pltpu.SemaphoreType.DMA((2, size, chunks)),
            pltpu.SemaphoreType.DMA((2, size, chunks)),
        ],
        compiler_params=pltpu.CompilerParams(
            collective_id=collective_id, has_side_effects=True, vmem_limit_bytes=48 * 1024 * 1024
        ),
        cost_estimate=pl.CostEstimate(flops=0, bytes_accessed=link_cost(3 * rows * cols), transcendentals=0),
        name="line_gather",
    )(x)


def line_scatter_kernel(size, chunk_rows, x_ref, out_ref, got, sent, send_sem, recv_sem):
    line_barrier(size)
    me = lax.axis_index(LINE)
    flows = two_flows(size)
    width = out_ref.shape[1]
    chunks = x_ref.shape[0] // chunk_rows

    def rows_of(chunk):
        return pl.ds(pl.multiple_of(chunk * chunk_rows, chunk_rows), chunk_rows)

    def cols_of(block):
        return pl.ds(pl.multiple_of(block * width, width), width)

    def copy_of(flow, block, chunk, source):
        return flow.copy(
            source,
            got.at[flow.side, rows_of(chunk), cols_of(block)],
            send_sem.at[flow.side, block, chunk],
            recv_sem.at[flow.side, block, chunk],
        )

    def own(block, chunk):
        return x_ref[rows_of(chunk), cols_of(block)].astype(jnp.float32)

    for hop in range(size - 1):

        def forward(chunk, carry):
            for flow in flows:
                block = jnp.where(flow.side == 0, size - 1 - hop, hop)
                ahead = (block - me) * flow.step > 0

                @pl.when(ahead & flow.has_source)
                def _():
                    source = x_ref.at[rows_of(chunk), cols_of(block)]
                    copy_of(flow, block, chunk, source).wait_recv()
                    total = got[flow.side, rows_of(chunk), cols_of(block)].astype(jnp.float32) + own(block, chunk)
                    sent[flow.side, rows_of(chunk), cols_of(block)] = total.astype(sent.dtype)
                    copy_of(flow, block, chunk, sent.at[flow.side, rows_of(chunk), cols_of(block)]).start()

                @pl.when(ahead & jnp.logical_not(flow.has_source))
                def _():
                    copy_of(flow, block, chunk, x_ref.at[rows_of(chunk), cols_of(block)]).start()

            return carry

        lax.fori_loop(0, chunks, forward, 0)

    def finish(chunk, carry):
        rows = rows_of(chunk)
        for flow in flows:

            @pl.when(flow.has_source)
            def _():
                copy_of(flow, me, chunk, x_ref.at[rows, cols_of(me)]).wait_recv()

        @pl.when(me == 0)
        def _():
            out_ref[rows] = (got[1, rows, cols_of(me)].astype(jnp.float32) + own(me, chunk)).astype(out_ref.dtype)

        @pl.when(me == size - 1)
        def _():
            out_ref[rows] = (got[0, rows, cols_of(me)].astype(jnp.float32) + own(me, chunk)).astype(out_ref.dtype)

        @pl.when((me > 0) & (me < size - 1))
        def _():
            other = got[0, rows, cols_of(me)].astype(jnp.float32) + got[1, rows, cols_of(me)].astype(jnp.float32)
            out_ref[rows] = (other + own(me, chunk)).astype(out_ref.dtype)

        return carry

    lax.fori_loop(0, chunks, finish, 0)
    for hop in range(size - 1):

        def drain(chunk, carry):
            for flow in flows:
                block = jnp.where(flow.side == 0, size - 1 - hop, hop)
                ahead = (block - me) * flow.step > 0

                @pl.when(ahead)
                def _():
                    copy_of(flow, block, chunk, x_ref.at[rows_of(chunk), cols_of(block)]).wait_send()

            return carry

        lax.fori_loop(0, chunks, drain, 0)


def line_scatter(x, size, collective_id, out_dtype=jnp.float32, chunk_rows=256):
    rows, cols = x.shape
    chunks = rows // chunk_rows
    return pl.pallas_call(
        partial(line_scatter_kernel, size, chunk_rows),
        out_shape=jax.ShapeDtypeStruct((rows, cols // size), out_dtype),
        in_specs=[pl.BlockSpec(memory_space=pltpu.VMEM)],
        out_specs=pl.BlockSpec(memory_space=pltpu.VMEM),
        scratch_shapes=[
            pltpu.VMEM((2, rows, cols), x.dtype),
            pltpu.VMEM((2, rows, cols), x.dtype),
            pltpu.SemaphoreType.DMA((2, size, chunks)),
            pltpu.SemaphoreType.DMA((2, size, chunks)),
        ],
        compiler_params=pltpu.CompilerParams(
            collective_id=collective_id, has_side_effects=True, vmem_limit_bytes=48 * 1024 * 1024
        ),
        cost_estimate=pl.CostEstimate(flops=0, bytes_accessed=link_cost(3 * rows * cols // size), transcendentals=0),
        name="line_scatter",
    )(x)


def matmul(left_op, right_op):
    return jnp.dot(left_op, right_op, preferred_element_type=jnp.float32)


def contract_rows(left_op, right_op):
    return jnp.einsum("tk,tn->kn", left_op, right_op, preferred_element_type=jnp.float32)


def against(grad_op, weight_op):
    return jnp.einsum("tn,kn->tk", grad_op, weight_op, preferred_element_type=jnp.float32)


def layer_norm(values, scale_in, offset):
    centre = jnp.mean(values, axis=-1, keepdims=True)
    centred = values - centre
    spread = jnp.mean(centred * centred, axis=-1, keepdims=True)
    return centred * lax.rsqrt(spread + norm_eps) * scale_in + offset


def shifted(values):
    grid_view = values.reshape(values.shape[0] // SEQ_LEN, SEQ_LEN, values.shape[1])
    earlier = jnp.concatenate([jnp.zeros_like(grid_view[:, :1]), grid_view[:, :-1]], axis=1)
    return earlier.reshape(values.shape)


def section_in(hidden, scale_in, offset, mix_rates):
    standardized_source = layer_norm(hidden, scale_in, offset)
    shift_diff = shifted(standardized_source) - standardized_source
    return tuple((standardized_source + shift_diff * mix_rates[:, column] for column in range(6)))


def section_out(residual, scale_in, offset, mix_rate):
    standardized_source = layer_norm(residual, scale_in, offset)
    return standardized_source + (shifted(standardized_source) - standardized_source) * mix_rate


def body(
    hidden,
    teacher,
    lengths,
    feature_params,
    decay_down,
    rate_down,
    gate_down,
    decay_up,
    rate_up,
    gate_up,
    receptance,
    key_proj,
    value_proj,
    output_proj,
    ffn_key,
    ffn_value,
):
    position_count, part_width = hidden.shape
    seq_dev = position_count // SEQ_LEN
    mp_index = lax.axis_index("mp")
    col_start = mp_index * part_width
    quarter = position_count // lax.axis_size("mp")
    row_start = mp_index * quarter
    own_lengths = lax.dynamic_slice_in_dim(lengths, lax.axis_index("dp") * seq_dev, seq_dev)
    places = jnp.arange(SEQ_LEN, dtype=jnp.int32)
    valid = (places[None, :] < own_lengths[:, None]).astype(jnp.float32).reshape(position_count)
    loss_scale = position_count * lax.axis_size("dp") / jnp.sum(lengths).astype(jnp.float32)
    line_size = lax.axis_size("mp")
    whole = line_gather(hidden, line_size, 1).astype(jnp.float32)
    low_rank = (decay_down.shape[1], rate_down.shape[1], gate_down.shape[1])
    narrow = jnp.concatenate([decay_down, rate_down, gate_down, feature_params], axis=1)
    narrow = jnp.pad(narrow, ((0, 0), (0, -narrow.shape[1] % 128)))
    narrow_w = lax.all_gather(narrow, "mp", axis=0, tiled=True)
    narrow_w = lax.all_gather(narrow_w, "dp", axis=0, tiled=True)
    decay_down_w = narrow_w[:, : low_rank[0]]
    rate_down_w = narrow_w[:, low_rank[0] : low_rank[0] + low_rank[1]]
    gate_down_w = narrow_w[:, low_rank[0] + low_rank[1] : sum(low_rank)]
    params_low = narrow_w[:, sum(low_rank) : sum(low_rank) + feature_params.shape[1]]
    three = lax.all_gather(
        jnp.concatenate([receptance, key_proj, value_proj], axis=1), "dp", axis=0, tiled=True
    )
    recept_w = three[:, :part_width]
    key_w = three[:, part_width : 2 * part_width]
    value_w = three[:, 2 * part_width :]
    up_rows = (decay_up.shape[0], rate_up.shape[0], gate_up.shape[0])
    ups = lax.all_gather(jnp.concatenate([decay_up, rate_up, gate_up], axis=0), "dp", axis=0)
    decay_up_w = ups[:, : up_rows[0]].reshape(-1, part_width)
    rate_up_w = ups[:, up_rows[0] : up_rows[0] + up_rows[1]].reshape(-1, part_width)
    gate_up_w = ups[:, up_rows[0] + up_rows[1] :].reshape(-1, part_width)
    output_w = lax.all_gather(output_proj, "dp", axis=1, tiled=True)
    ffn_key_w = lax.all_gather(ffn_key, "dp", axis=0, tiled=True)
    ffn_value_w = lax.all_gather(ffn_value, "dp", axis=1, tiled=True)
    params = params_low.astype(jnp.float32)
    model_width = whole.shape[1]
    mixed, back_in = jax.vjp(section_in, whole, params[:, 0], params[:, 1], params[:, 2:8])
    mix_r, mix_w, mix_k, mix_v, mix_a, mix_g = tuple(
        (member.astype(jnp.bfloat16) for member in mixed)
    )
    acceptance_matrix = matmul(mix_r, recept_w)
    keys_in = matmul(mix_k, key_w)
    payload_source = matmul(mix_v, value_w)
    decay_hid = jnp.tanh(matmul(mix_w, decay_down_w))
    decay_low = decay_hid.astype(jnp.bfloat16)
    rate_low = matmul(mix_a, rate_down_w).astype(jnp.bfloat16)
    gate_hid = jax.nn.sigmoid(matmul(mix_g, gate_down_w))
    gate_low = gate_hid.astype(jnp.bfloat16)
    decay_in = matmul(decay_low, decay_up_w)
    rate_in = matmul(rate_low, rate_up_w)
    sigmoid_source = matmul(gate_low, gate_up_w)
    columns = lax.dynamic_slice_in_dim(params, col_start, part_width, 0)[:, 8:15].T
    columns = jnp.pad(columns, ((0, 1), (0, 0)))
    mixer_args = (
        own_lengths,
        acceptance_matrix,
        keys_in,
        payload_source,
        decay_in,
        rate_in,
        sigmoid_source,
        columns,
    )
    gated_low, *kept = run_mixer_forward(*mixer_args)
    residual = whole + line_sum(matmul(gated_low, output_w).astype(jnp.bfloat16), line_size, 2).astype(
        jnp.float32
    )
    ffn_in, back_out = jax.vjp(section_out, residual, params[:, 15], params[:, 16], params[:, 17])
    ffn_low = ffn_in.astype(jnp.bfloat16)
    pre_act = matmul(ffn_low, ffn_key_w)
    active = jnp.maximum(pre_act, 0.0)
    squared = (active * active).astype(jnp.bfloat16)
    ffn_part = line_scatter(matmul(squared, ffn_value_w).astype(jnp.bfloat16), line_size, 3)
    result = lax.dynamic_slice_in_dim(residual, col_start, part_width, 1) + ffn_part
    grad_result = loss_scale * valid[:, None] * (result - teacher.astype(jnp.float32))
    grad_low = line_gather(grad_result.astype(jnp.bfloat16), line_size, 4)
    grad_ffn_value = contract_rows(squared, grad_low).astype(jnp.bfloat16)
    grad_low, grad_ffn_value = lax.optimization_barrier((grad_low, grad_ffn_value))
    grad_ffn_value = lax.psum_scatter(grad_ffn_value, "dp", scatter_dimension=1, tiled=True)
    grad_squared = against(grad_low, ffn_value_w)
    grad_pre = (grad_squared * 2.0 * active).astype(jnp.bfloat16)
    grad_ffn_key = contract_rows(ffn_low, grad_pre).astype(jnp.bfloat16)
    grad_pre, grad_ffn_key = lax.optimization_barrier((grad_pre, grad_ffn_key))
    grad_ffn_key = lax.psum_scatter(grad_ffn_key, "dp", scatter_dimension=0, tiled=True)
    d_resid_part, d_scale_two, d_offset_two, d_mix_two = back_out(against(grad_pre, ffn_key_w))
    d_residual = grad_low.astype(jnp.float32) + line_sum(
        d_resid_part.astype(jnp.bfloat16), line_size, 5
    ).astype(jnp.float32)
    d_low = d_residual.astype(jnp.bfloat16)
    grad_output_proj = contract_rows(gated_low, d_low).astype(jnp.bfloat16)
    d_low, grad_output_proj = lax.optimization_barrier((d_low, grad_output_proj))
    grad_output_proj = lax.psum_scatter(grad_output_proj, "dp", scatter_dimension=1, tiled=True)
    d_gated = against(d_low, output_w)
    d_gated, grad_ffn_value = lax.optimization_barrier((d_gated, grad_ffn_value))
    d_recept, d_keys, d_values, d_decay, d_rate, d_gate, d_columns = run_mixer_backward(
        *mixer_args, *kept, d_gated
    )
    d_columns = jnp.sum(d_columns, axis=1)[:7].T
    grad_three = jnp.concatenate(
        [
            contract_rows(mix_r, d_recept).astype(jnp.bfloat16),
            contract_rows(mix_k, d_keys).astype(jnp.bfloat16),
            contract_rows(mix_v, d_values).astype(jnp.bfloat16),
        ],
        axis=1,
    )
    d_recept, d_keys, d_values, grad_three = lax.optimization_barrier(
        (d_recept, d_keys, d_values, grad_three)
    )
    grad_three = lax.psum_scatter(grad_three, "dp", scatter_dimension=0, tiled=True)
    grad_decay_up = contract_rows(decay_low, d_decay)
    grad_rate_up = contract_rows(rate_low, d_rate)
    grad_gate_up = contract_rows(gate_low, d_gate)
    d_inner = jnp.concatenate(
        [against(d_decay, decay_up_w), against(d_rate, rate_up_w), against(d_gate, gate_up_w)], axis=1
    ).astype(jnp.bfloat16)
    d_inner = jnp.pad(d_inner, ((0, 0), (0, -d_inner.shape[1] % 128)))
    d_inner = line_sum(d_inner, line_size, 6)
    d_inner, grad_ffn_key = lax.optimization_barrier((d_inner, grad_ffn_key))
    d_inner = d_inner.astype(jnp.float32)
    d_decay_hid = d_inner[:, : low_rank[0]]
    d_rate_hid = d_inner[:, low_rank[0] : low_rank[0] + low_rank[1]]
    d_gate_hid = d_inner[:, low_rank[0] + low_rank[1] : sum(low_rank)]
    d_decay_pre = (d_decay_hid * (1.0 - decay_hid * decay_hid)).astype(jnp.bfloat16)
    d_rate_pre = d_rate_hid.astype(jnp.bfloat16)
    d_gate_pre = (d_gate_hid * gate_hid * (1.0 - gate_hid)).astype(jnp.bfloat16)

    def own_rows(values):
        return lax.dynamic_slice_in_dim(values, row_start, quarter, 0)

    def place_rows(values):
        return lax.dynamic_update_slice_in_dim(
            jnp.zeros((position_count, values.shape[1]), jnp.float32), values, row_start, 0
        )

    groups = lax.axis_size("dp")
    row_block = decay_down.shape[0]

    def own_features(values):
        split = values.reshape(position_count, groups, lax.axis_size("mp"), row_block)
        taken = lax.dynamic_index_in_dim(split, mp_index, 2, keepdims=False)
        return taken.reshape(position_count, groups * row_block)

    grad_downs = jnp.concatenate(
        [
            contract_rows(own_features(mix_w), d_decay_pre),
            contract_rows(own_features(mix_a), d_rate_pre),
            contract_rows(own_features(mix_g), d_gate_pre),
        ],
        axis=1,
    )
    cotangents = (
        against(d_recept, recept_w),
        place_rows(against(own_rows(d_decay_pre), decay_down_w)),
        against(d_keys, key_w),
        against(d_values, value_w),
        place_rows(against(own_rows(d_rate_pre), rate_down_w)),
        place_rows(against(own_rows(d_gate_pre), gate_down_w)),
    )
    d_in_part, d_scale_one, d_offset_one, d_mix_one = back_in(cotangents)
    d_in_part, grad_output_proj = lax.optimization_barrier((d_in_part.astype(jnp.bfloat16), grad_output_proj))
    grad_hidden = lax.dynamic_slice_in_dim(d_residual, col_start, part_width, 1) + line_scatter(
        d_in_part, line_size, 7
    )
    core_grads = lax.dynamic_update_slice_in_dim(
        jnp.zeros((model_width, 7), jnp.float32), d_columns, col_start, 0
    )
    grad_params = jnp.concatenate(
        [
            d_scale_one[:, None],
            d_offset_one[:, None],
            d_mix_one,
            core_grads,
            d_scale_two[:, None],
            d_offset_two[:, None],
            d_mix_two[:, None],
        ],
        axis=1,
    )
    param_parts = grad_params.reshape(groups, lax.axis_size("mp"), row_block, grad_params.shape[1])
    param_parts = lax.psum_scatter(
        param_parts.transpose(1, 0, 2, 3), "mp", scatter_dimension=0, tiled=True
    ).reshape(model_width // lax.axis_size("mp"), grad_params.shape[1])
    narrow_grads = lax.psum_scatter(
        jnp.concatenate([grad_downs, param_parts], axis=1), "dp", scatter_dimension=0, tiled=True
    )
    up_grads = jnp.concatenate(
        [member.reshape(groups, -1, part_width) for member in (grad_decay_up, grad_rate_up, grad_gate_up)],
        axis=1,
    ).astype(jnp.bfloat16)
    up_grads = lax.psum_scatter(up_grads, "dp", scatter_dimension=0, tiled=True)
    up_grads = up_grads.reshape(-1, part_width).astype(jnp.float32)
    first, second = low_rank[0], low_rank[0] + low_rank[1]
    return (
        result.astype(jnp.bfloat16),
        grad_hidden,
        narrow_grads[:, sum(low_rank) :],
        narrow_grads[:, :first],
        narrow_grads[:, first:second],
        narrow_grads[:, second : sum(low_rank)],
        up_grads[: up_rows[0]],
        up_grads[up_rows[0] : up_rows[0] + up_rows[1]],
        up_grads[up_rows[0] + up_rows[1] :],
        grad_three[:, :part_width].astype(jnp.float32),
        grad_three[:, part_width : 2 * part_width].astype(jnp.float32),
        grad_three[:, 2 * part_width :].astype(jnp.float32),
        grad_output_proj.astype(jnp.float32),
        grad_ffn_key.astype(jnp.float32),
        grad_ffn_value.astype(jnp.float32),
    )


def solution(mesh):
    in_specs = (
        P("dp", "mp"),
        P("dp", "mp"),
        P(),
        P(("dp", "mp"), None),
        P(("dp", "mp"), None),
        P(("dp", "mp"), None),
        P(("dp", "mp"), None),
        P("dp", "mp"),
        P("dp", "mp"),
        P("dp", "mp"),
        P("dp", "mp"),
        P("dp", "mp"),
        P("dp", "mp"),
        P("mp", "dp"),
        P("dp", "mp"),
        P("mp", "dp"),
    )
    out_specs = (
        P("dp", "mp"),
        P("dp", "mp"),
        P(("dp", "mp"), None),
        P(("dp", "mp"), None),
        P(("dp", "mp"), None),
        P(("dp", "mp"), None),
        P("dp", "mp"),
        P("dp", "mp"),
        P("dp", "mp"),
        P("dp", "mp"),
        P("dp", "mp"),
        P("dp", "mp"),
        P("mp", "dp"),
        P("dp", "mp"),
        P("mp", "dp"),
    )
    return jax.shard_map(body, mesh=mesh, in_specs=in_specs, out_specs=out_specs, check_vma=False)
```

time: 4000 us -> 1200 us (0.30)
  matrix products: 1550 us -> 201 us
  waiting for transfers between devices: 1370 us -> 69.8 us
  Pallas kernels: 0 us -> 630 us
  local copies, waits for them, and re-layouts: 413 us -> 108 us
  blocking collectives: 258 us -> 25.4 us
  other arithmetic: 335 us -> 135 us
    dot_general x1056 -> x0, matrix products: 1330 us -> none  [the longest x240 333 us: unit_lower_inverse(): accum = accum + product('bts,bsu->btu', accum, power)]
    reduce_scatter x12 -> x6, waiting for transfers between devices: 873 us -> 66.7 us  [the longest x1 55.2 us: body(): lax.psum_scatter(grad_three, 'dp', scatter_dimension=0, tiled=True)]
    pallas_call x0 -> x9, Pallas kernels: none -> 630 us  [the longest x3 269 us: line_sum(): pl.pallas_call(partial(line_sum_kernel, size, chunk_rows), out_shape=jax....]
    psum x3 -> x0, waiting for transfers between devices: 314 us -> none  [the longest x1 151 us: body(): lax.psum(matmul(gated_low, output_w).astype(jnp.bfloat16), 'mp')]
    all_gather x6 -> x2, blocking collectives: 241 us -> 25.4 us  [the longest x1 15.6 us: body(): narrow_w = lax.all_gather(narrow, 'mp', axis=0, tiled=True)]
    all_gather x9 -> x5, waiting for transfers between devices: 157 us -> 0.03 us  [the longest x1 0.02 us: body(): narrow_w = lax.all_gather(narrow_w, 'dp', axis=0, tiled=True)]
    dynamic_slice x112 -> x2, local copies, waits for them, and re-layouts: 115 us -> 5.36 us  [own_features(): taken = lax.dynamic_index_in_dim(split, mp_index, 2, keepdims=False)]
    dynamic_update_slice x49 -> x0, other arithmetic: 85.7 us -> none  [the longest x48 85.7 us: time_mixer(): final_state, outputs = lax.scan(block_step, start_state, arranged)]
  transfers between devices with their start and end apart: 29 -> 12, of which waited for: 18 -> 2; matrix products, arithmetic and copies ran while one was open for 24% -> 21% of each run, Pallas kernels for 0% -> 41%
where the time goes in v1:
time: 1200 us; the launch traced here: 1190 us
  Pallas kernels  630 us (52%)
  matrix products  201 us (17%)
  other arithmetic  135 us (11%)
  local copies, waits for them, and re-layouts  108 us (9%)
  waiting for transfers between devices  69.8 us (6%)
  blocking collectives  25.4 us (2%)
  between operations  16.9 us (1%)
    pallas_call x3, Pallas kernels, line_sum(): pl.pallas_call(partial(line_sum_kernel, size, chunk_rows), out_shape=jax....  269 us
    pallas_call x2, Pallas kernels, line_scatter(): pl.pallas_call(partial(line_scatter_kernel, size, chunk_rows), out_shape=...  142 us
    pallas_call x2, Pallas kernels, line_gather(): pl.pallas_call(partial(line_gather_kernel, size, chunk_rows), out_shape=j...  140 us
    dot_general x12, matrix products, against(): jnp.einsum('tn,kn->tk', grad_op, weight_op, preferred_element_type=jnp.fl...  93.3 us
    dot_general x12, matrix products, matmul(): return jnp.dot(left_op, right_op, preferred_element_type=jnp.float32)  57.3 us
    reduce_scatter x1, waiting for transfers between devices, body(): lax.psum_scatter(grad_three, 'dp', scatter_dimension=0, tiled=True)  55.2 us
    dot_general x12, matrix products, contract_rows(): jnp.einsum('tk,tn->kn', left_op, right_op, preferred_element_type=jnp.flo...  50.8 us
    unnamed x207, local copies, waits for them, and re-layouts  45.7 us
  transfers between devices with their start and end apart: 12, of which 2 were waited for; matrix products, arithmetic and copies ran while one was open for 21% of the time, Pallas kernels for 41%

profile of v1, /device:TPU:0, one launch (start us, length us, event | category | flops | bytes accessed | tf_op | source)
XLA Modules:
  0.0 1187.0 jit_solution(16696937643623155395)
XLA Ops:
  8.9 15.6 %all_gather.24 = bf16[256,512]{1,0:T(8,128)(2,1)S(1)} all-gather(bf16[64,512]{1,0:T(8,128)(2,1)S(1)} %fusion.70), channel_id=1, replica_groups=mesh['dp'=8,'mp'=4] {'mp'}, dimensions={0}, use_global_device_ids=true | all-gather | bytes 327680 | tf_op jit(solution)/shard_map/all_gather | solution.py:941
  30.7 68.8 %line_gather.2 = bf16[1024,2048]{1,0:T(8,128)(2,1)S(1)} custom-call(bf16[1024,512]{1,0:T(8,128)(2,1)S(1)} %copy-done.19), custom_call_target="tpu_custom_call" | custom-call | bytes 251658240 | tf_op jit(solution)/shard_map/line_gather/pallas_call | solution.py:746
  102.2 9.7 all-gather
  114.7 3.5 fusion.22
  119.5 3.5 fusion.14
  123.0 5.1 fusion.20
  128.2 9.3 fusion.19
  148.6 6.6 fusion.30.v_ref
  160.0 35.7 %mixer_forward.1 = (bf16[1024,512]{1,0:T(8,128)(2,1)S(1)}, f32[1024,512]{1,0:T(8,128)S(1)}, bf16[1024,512]{1,0:T(8,128)(2,1)S(1)}, bf16[1024,512]{1,0:T(8,128)(2...) custom-call(s32[1]{0:T(128)} %dynamic_slice.31.length_ref, ...), custom_call_target="tpu_custom_call" | custom-call | tf_op jit(solution)/shard_map/mixer_forward/pallas_call | solution.py:475
  202.5 6.3 convolution_convert_fusion.3.x_ref
  208.9 113.9 %line_sum.3 = bf16[1024,2048]{1,0:T(8,128)(2,1)S(1)} custom-call(bf16[1024,2048]{1,0:T(8,128)(2,1)} %convolution_convert_fusion.3.x_ref), custom_call_target="tpu_custom_call" | custom-call | bytes 335544320 | tf_op jit(solution)/shard_map/line_sum/pallas_call | solution.py:662
  322.8 4.5 convert_add_fusion
  335.0 6.5 add_convert_fusion.2
  341.6 14.4 %fusion.93 = f32[1024,2048]{1,0:T(8,128)} fusion(bf16[1024,2048]{1,0:T(8,128)(2,1)} %add_convert_fusion.2, bf16[2048,2048]{1,0:T(8,128)(2,1)} %all-gather.13.cloned.1.call-done), kind=kOutput, calls=%fused_computation.183 | convolution fusion | flops 8589934592 | bytes 20971520 | tf_op jit(solution)/shard_map/dot_general | solution.py:873
  356.0 15.4 %convolution_convert_fusion.2.x_ref = bf16[1024,2048]{1,0:T(8,128)(2,1)} fusion(bf16[2048,2048]{1,0:T(8,128)(2,1)} %all-gather.15.cloned.1.call-done, f32[1024,2048]{1,0:T(8,128)} %fusion.93), kind=kOutput, calls=%fused_computation.56 | convolution fusion | flops 8598323200 | bytes 20971520 | tf_op jit(solution)/shard_map/dot_general | solution.py:873
  371.5 69.9 %line_scatter.2 = f32[1024,512]{1,0:T(8,128)S(1)} custom-call(bf16[1024,2048]{1,0:T(8,128)(2,1)} %convolution_convert_fusion.2.x_ref), custom_call_target="tpu_custom_call" | custom-call | bytes 251658240 | tf_op jit(solution)/shard_map/line_scatter/pallas_call | solution.py:853
  444.3 71.4 %line_gather.3 = bf16[1024,2048]{1,0:T(8,128)(2,1)S(1)} custom-call(bf16[1024,512]{1,0:T(8,128)(2,1)S(1)} %get-tuple-element.163.x_ref), custom_call_target="tpu_custom_call" | custom-call | bytes 251658240 | tf_op jit(solution)/shard_map/line_gather/pallas_call | solution.py:746
  517.7 14.6 %convolution_convert_fusion.1 = bf16[2048,2048]{1,0:T(8,128)(2,1)} fusion(bf16[1024,2048]{1,0:T(8,128)(2,1)S(1)} %line_gather.3, f32[1024,2048]{1,0:T(8,128)} %fusion.93), kind=kOutput, calls=%fused_computation.53 | convolution fusion | flops 8600420352 | bytes 20971520 | tf_op jit(solution)/shard_map/tk,tn->kn/dot_general | solution.py:877
  532.4 14.8 %multiply_convert_fusion = bf16[1024,2048]{1,0:T(8,128)(2,1)S(1)} fusion(f32[1024,2048]{1,0:T(8,128)} %fusion.93, bf16[1024,2048]{1,0:T(8,128)(2,1)} %copy-done.7, bf16[2048,2048]{1,0:T(8,128)(2,1)} %all-gather.15.cloned.1.call-done), kind=kOutput, calls=%fused_computation.46 | convolution fusion | flops 8598323200 | bytes 25165824 | tf_op jit(solution)/shard_map/tn,kn->tk/dot_general | solution.py:881
  549.2 11.5 convolution_convert_fusion
  560.8 13.1 %fusion.94 = f32[1024,2048]{1,0:T(8,128)S(1)} fusion(bf16[1024,2048]{1,0:T(8,128)(2,1)} %copy-done.94, bf16[2048,2048]{1,0:T(8,128)(2,1)} %all-gather.13.cloned.1.call-done), kind=kOutput, calls=%fused_computation.184 | convolution fusion | flops 8589934592 | bytes 20971520 | tf_op jit(solution)/shard_map/tn,kn->tk/dot_general | solution.py:881
  578.9 5.2 split.8
  585.4 13.7 %multiply_reduce_fusion.1 = (f32[2048]{0:T(1024)S(1)}, f32[1024]{0:T(1024)S(1)}, f32[2048]{0:T(1024)S(1)}, f32[2048]{0:T(1024)S(1)}, f32[1024,2048]{1,0:T(8,128)S(1)}) fusion(f32[1024]{0:T(1024)S(1)} %fusion.79, f32[1024]{0:T(1024)S(1)} %broadcast_multiply_fusion, bf16[1024,2048]{1,0:T(8,128)(2,1)S(1)} %copy-done.6, bf16[1024,2048]{1,0:T(8,128)(2,1)S(1)} %copy-done.3, ...), kind=kLoop, calls=%fused_computation.33 | loop fusion | flops 41935872 | bytes 41988096 | tf_op jit(solution)/shard_map/transpose(jvp())/reduce_sum | solution.py:888
  599.1 5.4 fusion.87
  604.5 6.0 add_convert_fusion.1.x_ref
  610.5 110.5 %line_sum.4 = bf16[1024,2048]{1,0:T(8,128)(2,1)S(1)} custom-call(bf16[1024,2048]{1,0:T(8,128)(2,1)} %add_convert_fusion.1.x_ref), custom_call_target="tpu_custom_call" | custom-call | bytes 335544320 | tf_op jit(solution)/shard_map/line_sum/pallas_call | solution.py:662
  721.0 7.0 convert_add_fusion.1
  728.0 5.9 convolution_convert_fusion.7
  735.9 6.7 fusion.95.dz_ref
  747.9 43.3 %mixer_backward.1 = (bf16[1024,512]{1,0:T(8,128)(2,1)S(1)}, bf16[1024,512]{1,0:T(8,128)(2,1)S(1)}, bf16[1024,512]{1,0:T(8,128)(2,1)S(1)}, bf16[1024,512]{1,0:T(8...) custom-call(s32[1]{0:T(128)} %dynamic_slice.31.length_ref, ...), custom_call_target="tpu_custom_call" | custom-call | tf_op jit(solution)/shard_map/mixer_backward/pallas_call | solution.py:512
  799.9 44.3 %line_sum.5 = bf16[1024,512]{1,0:T(8,128)(2,1)S(1)} custom-call(bf16[1024,512]{1,0:T(8,128)(2,1)S(1)} %fusion.44.x_ref), custom_call_target="tpu_custom_call" | custom-call | bytes 83886080 | tf_op jit(solution)/shard_map/line_sum/pallas_call | solution.py:662
  849.9 4.0 copy.102
  864.6 11.6 pad_maximum_fusion
  876.2 7.6 fusion.28
  883.8 7.2 fusion.32
  891.1 4.4 broadcast.128.clone.1
  898.9 4.3 broadcast.128.clone.2
  903.2 4.3 add_dynamic-update-slice_fusion.1
  907.5 31.9 %multiply_reduce_fusion.7 = (f32[2048]{0:T(1024)S(1)}, f32[2048]{0:T(1024)S(1)}, f32[2048]{0:T(1024)S(1)}, f32[2048]{0:T(1024)S(1)}, f32[2048]{0:T(1024)S(1)}, /...) fusion(f32[1024,2048]{1,0:T(8,128)} %copy-done.37, ...), kind=kOutput, calls=%fused_computation.39 | convolution fusion | flops 2199900160 | bytes 87130112 | tf_op jit(solution)/shard_map/tn,kn->tk/dot_general | solution.py:881
  939.6 8.6 split.9
  951.6 17.6 %fusion.21 = (f32[2048]{0:T(1024)S(1)}, f32[1024]{0:T(1024)}, f32[2048]{0:T(1024)S(1)}, f32[1024,2048]{1,0:T(8,128)}) fusion(bf16[1024,2048]{1,0:T(8,128)(2,1)S(1)} %copy-done.4, f32[1024]{0:T(1024)S(1)} %copy-done.70, f32[1024]{0:T(1024)S(1)} %copy-done.67, f32[2048]{0:T(1024)S(1)} %bitcast.144, f32[1,1023,2048]{2,1,0:T(8,128)} %split.9, ...), kind=kLoop, calls=%fused_computation.26 | loop fusion | flops 27257856 | bytes 46166016 | tf_op jit(solution)/shard_map/transpose(jvp())/reduce_sum | solution.py:888
  971.2 6.4 copy.82
  977.6 6.5 copy.84
  984.1 6.5 copy.83
  1013.2 6.0 fusion.86
  1021.8 11.5 reduce-scatter.14.cloned.1.call-done
  1033.3 71.9 %line_scatter.3 = f32[1024,512]{1,0:T(8,128)S(1)} custom-call(bf16[1024,2048]{1,0:T(8,128)(2,1)} %add_convert_fusion.x_ref), custom_call_target="tpu_custom_call" | custom-call | bytes 251658240 | tf_op jit(solution)/shard_map/line_scatter/pallas_call | solution.py:853
  1120.2 55.2 %reduce-scatter.20.cloned.1.call-done = bf16[256,1536]{0,1:T(8,128)(2,1)} async-done(((bf16[2048,1536]{0,1:T(8,128)(2,1)}), bf16[256,1536]{0,1:T(8,128)(2,1)}) %reduce-scatter.20.cloned.1.call-update) | async-done | bytes 786448 | tf_op jit(solution)/shard_map/reduce_scatter | solution.py:1036
  (332 shorter events, 142.3 us)
Async XLA Ops:
  7.2 95.0 %copy-start.91 = (bf16[12,512]{1,0:T(8,128)(2,1)S(1)}, bf16[12,512]{1,0:T(8,128)(2,1)}, u32[]{:S(2)}) copy-start(bf16[12,512]{1,0:T(8,128)(2,1)} %param.23) | copy-start | bytes 36868
  7.2 95.0 %copy-start.90 = (bf16[12,512]{1,0:T(8,128)(2,1)S(1)}, bf16[12,512]{1,0:T(8,128)(2,1)}, u32[]{:S(2)}) copy-start(bf16[12,512]{1,0:T(8,128)(2,1)} %param.24) | copy-start | bytes 36868
  7.2 95.0 %copy-start.89 = (bf16[32,512]{1,0:T(8,128)(2,1)S(1)}, bf16[32,512]{1,0:T(8,128)(2,1)}, u32[]{:S(2)}) copy-start(bf16[32,512]{1,0:T(8,128)(2,1)} %param.25) | copy-start | bytes 98308
  7.2 104.8 %copy-start.93 = (s32[8]{0:T(128)S(1)}, s32[8]{0:T(128)}, u32[]{:S(2)}) copy-start(s32[8]{0:T(128)} %param.18) | copy-start | bytes 100
  7.2 111.0 %all-gather.7.cloned.1.call-start = ((), (), s32[]{:S(2)}) async-start(), calls=%async_computation.7 | async-start | bytes 2359296 | tf_op jit(solution)/shard_map/all_gather | solution.py:942
  25.4 123.1 %all-gather.9.cloned.1.call-start = ((), (), s32[]{:S(2)}) async-start(), calls=%async_computation.8 | async-start | bytes 7077888 | tf_op jit(solution)/shard_map/all_gather | solution.py:947
  27.6 175.0 %all-gather.11.cloned.1.call-start = ((), (), s32[]{:S(2)}) async-start(), calls=%async_computation.9 | async-start | bytes 2359296 | tf_op jit(solution)/shard_map/all_gather | solution.py:958
  28.3 313.3 %all-gather.13.cloned.1.call-start = ((), (), s32[]{:S(2)}) async-start(), calls=%async_computation.10 | async-start | bytes 9437184 | tf_op jit(solution)/shard_map/all_gather | solution.py:959
  28.9 327.2 %all-gather.15.cloned.1.call-start = ((), (), s32[]{:S(2)}) async-start(), calls=%async_computation.11 | async-start | bytes 9437184 | tf_op jit(solution)/shard_map/all_gather | solution.py:960
  29.5 713.2 %reduce-scatter.10.cloned.1.call-start = ((), (), s32[]{:S(2)}) async-start(), calls=%async_computation.12 | async-start | bytes 9437184 | tf_op jit(solution)/shard_map/reduce_scatter | solution.py:1005
  102.2 26.0 %copy-start.66 = (f32[1024]{0:T(1024)}, f32[1024]{0:T(1024)S(1)}, u32[]{:S(2)}) copy-start(f32[1024]{0:T(1024)S(1)} %broadcast_multiply_fusion.1) | copy-start | bytes 12292
  114.6 31.3 %copy-start.52 = (bf16[8,32,512]{2,1,0:T(8,128)(2,1)}, bf16[8,32,512]{2,1,0:T(8,128)(2,1)S(1)}, u32[]{:S(2)}) copy-start(bf16[8,32,512]{2,1,0:T(8,128)(2,1)S(1)} %slice.190) | copy-start | bytes 786436
  114.6 28.1 %copy-start.60 = (bf16[96,512]{1,0:T(8,128)(2,1)}, bf16[96,512]{1,0:T(8,128)(2,1)S(1)}, u32[]{:S(2)}) copy-start(bf16[96,512]{1,0:T(8,128)(2,1)S(1)} %reshape.236) | copy-start | bytes 294916
  114.7 24.3 %copy-start.59 = (bf16[96,512]{1,0:T(8,128)(2,1)}, bf16[96,512]{1,0:T(8,128)(2,1)S(1)}, u32[]{:S(2)}) copy-start(bf16[96,512]{1,0:T(8,128)(2,1)S(1)} %reshape.237) | copy-start | bytes 294916
  118.2 10.0 copy-start.69
  119.3 40.6 %copy-start.26 = (f32[8,512]{1,0:T(8,128)}, f32[8,512]{1,0:T(8,128)S(1)}, u32[]{:S(2)}) copy-start(f32[8,512]{1,0:T(8,128)S(1)} %pad.39.cols_ref) | copy-start | bytes 49156
  119.4 8.7 copy-start.63
  119.4 8.7 copy-start.74
  119.4 8.7 copy-start.76
  119.5 8.7 copy-start.78
  119.5 8.7 copy-start.80
  128.1 9.4 copy-start.37
  128.1 16.4 %copy-start.39 = (bf16[1024,2048]{1,0:T(8,128)(2,1)}, bf16[1024,2048]{1,0:T(8,128)(2,1)S(1)}, u32[]{:S(2)}) copy-start(bf16[1024,2048]{1,0:T(8,128)(2,1)S(1)} %get-tuple-element.154) | copy-start | bytes 12582916
  128.2 9.3 copy-start.54
  202.5 120.2 %copy-start.28 = (bf16[1024,512]{1,0:T(8,128)(2,1)}, bf16[1024,512]{1,0:T(8,128)(2,1)S(1)}, u32[]{:S(2)}) copy-start(bf16[1024,512]{1,0:T(8,128)(2,1)S(1)} %get-tuple-element.45) | copy-start | bytes 3145732
  202.5 120.3 %copy-start.2 = (bf16[1024,2048]{1,0:T(8,128)(2,1)S(1)}, bf16[1024,2048]{1,0:T(8,128)(2,1)}, u32[]{:S(2)}) copy-start(bf16[1024,2048]{1,0:T(8,128)(2,1)} %copy-done) | copy-start | bytes 12582916
  322.8 9.0 copy-start.5
  356.0 85.4 %copy-start.56 = (bf16[1024,512]{1,0:T(8,128)(2,1)S(1)}, bf16[1024,512]{1,0:T(8,128)(2,1)}, u32[]{:S(2)}) copy-start(bf16[1024,512]{1,0:T(8,128)(2,1)} %param.17) | copy-start | bytes 3145732
  532.4 311.9 %reduce-scatter.12.cloned.1.call-start = ((), (), s32[]{:S(2)}) async-start(), calls=%async_computation.13 | async-start | bytes 9437184 | tf_op jit(solution)/shard_map/reduce_scatter | solution.py:1010
  532.4 16.8 %copy-start.45 = (bf16[1024,2048]{1,0:T(8,128)(2,1)S(1)}, bf16[1024,2048]{1,0:T(8,128)(2,1)}, u32[]{:S(2)}) copy-start(bf16[1024,2048]{1,0:T(8,128)(2,1)} %add_convert_fusion.2) | copy-start | bytes 12582916
  560.8 449.4 %reduce-scatter.16.cloned.1.call-start = ((), (), s32[]{:S(2)}) async-start(), calls=%async_computation.15 | async-start | bytes 368640 | tf_op jit(solution)/shard_map/reduce_scatter | solution.py:1107
  604.5 116.5 %copy-start.8 = (bf16[1024,2048]{1,0:T(8,128)(2,1)S(1)}, bf16[1024,2048]{1,0:T(8,128)(2,1)}, u32[]{:S(2)}) copy-start(bf16[1024,2048]{1,0:T(8,128)(2,1)} %copy-done.7) | copy-start | bytes 12582916
  747.9 47.2 %copy-start.61 = (bf16[96,512]{1,0:T(8,128)(2,1)S(1)}, bf16[96,512]{1,0:T(8,128)(2,1)}, u32[]{:S(2)}) copy-start(bf16[96,512]{1,0:T(8,128)(2,1)} %copy-done.60) | copy-start | bytes 294916
  747.9 50.9 %copy-start.53 = (bf16[8,32,512]{2,1,0:T(8,128)(2,1)S(1)}, bf16[8,32,512]{2,1,0:T(8,128)(2,1)}, u32[]{:S(2)}) copy-start(bf16[8,32,512]{2,1,0:T(8,128)(2,1)} %copy-done.52) | copy-start | bytes 786436
  939.6 11.9 %copy-start.4 = (bf16[1024,2048]{1,0:T(8,128)(2,1)S(1)}, bf16[1024,2048]{1,0:T(8,128)(2,1)}, u32[]{:S(2)}) copy-start(bf16[1024,2048]{1,0:T(8,128)(2,1)} %copy-done) | copy-start | bytes 12582916
  939.6 11.9 %copy-start.64 = (f32[2048,1]{0,1:T(1,128)S(1)}, f32[2048,1]{0,1:T(1,128)}, u32[]{:S(2)}) copy-start(f32[2048,1]{0,1:T(1,128)} %copy-done.63) | copy-start | bytes 24580
  939.6 11.9 %copy-start.67 = (f32[1024]{0:T(1024)S(1)}, f32[1024]{0:T(1024)}, u32[]{:S(2)}) copy-start(f32[1024]{0:T(1024)} %copy-done.66) | copy-start | bytes 12292
  939.6 11.9 %copy-start.70 = (f32[1024]{0:T(1024)S(1)}, f32[1024]{0:T(1024)}, u32[]{:S(2)}) copy-start(f32[1024]{0:T(1024)} %copy-done.69) | copy-start | bytes 12292
  951.5 18.1 %copy-start.86 = (f32[8,4,64,1]{2,1,0,3:T(4,128)S(1)}, f32[8,4,64,1]{2,1,0,3:T(4,128)}, u32[]{:S(2)}) copy-start(f32[8,4,64,1]{2,1,0,3:T(4,128)} %concatenate.58) | copy-start | bytes 24580
  951.6 18.1 %copy-start.84 = (f32[8,4,64,1]{2,1,0,3:T(4,128)S(1)}, f32[8,4,64,1]{2,1,0,3:T(4,128)}, u32[]{:S(2)}) copy-start(f32[8,4,64,1]{2,1,0,3:T(4,128)} %concatenate.59) | copy-start | bytes 24580
  951.6 18.1 %copy-start.85 = (f32[8,4,64,1]{2,1,0,3:T(4,128)S(1)}, f32[8,4,64,1]{2,1,0,3:T(4,128)}, u32[]{:S(2)}) copy-start(f32[8,4,64,1]{2,1,0,3:T(4,128)} %concatenate.60) | copy-start | bytes 24580
  970.4 62.9 %reduce-scatter.14.cloned.1.call-start = ((), (), s32[]{:S(2)}) async-start(), calls=%async_computation.14 | async-start | bytes 2359296 | tf_op jit(solution)/shard_map/reduce_scatter | solution.py:1018
  971.2 142.3 %reduce-scatter.18.cloned.1.call-start = ((), (), s32[]{:S(2)}) async-start(), calls=%async_computation.16 | async-start | bytes 516096 | tf_op jit(solution)/shard_map/reduce_scatter | solution.py:1117
  984.1 15.2 %copy-start.14 = (bf16[1024,512]{1,0:T(8,128)(2,1)S(1)}, bf16[1024,512]{1,0:T(8,128)(2,1)}, u32[]{:S(2)}) copy-start(bf16[1024,512]{1,0:T(8,128)(2,1)} %copy-done.13) | copy-start | bytes 3145732
  1004.8 110.8 %reduce-scatter.22.cloned.1.call-start = ((), (), s32[]{:S(2)}) async-start(), calls=%async_computation.18 | async-start | bytes 1179648
  1012.6 162.8 %reduce-scatter.20.cloned.1.call-start = ((), (), s32[]{:S(2)}) async-start(), calls=%async_computation.17 | async-start | bytes 7077888 | tf_op jit(solution)/shard_map/reduce_scatter | solution.py:1036
  1019.3 87.8 %copy-start.58 = (bf16[256,2048]{1,0:T(8,128)(2,1)S(1)}, bf16[256,2048]{1,0:T(8,128)(2,1)}, u32[]{:S(2)}) copy-start(bf16[256,2048]{1,0:T(8,128)(2,1)} %reduce-scatter.12.cloned.1.call-done) | copy-start | bytes 3145732
  1019.3 89.3 %copy-start.57 = (bf16[2048,256]{1,0:T(8,128)(2,1)S(1)}, bf16[2048,256]{1,0:T(8,128)(2,1)}, u32[]{:S(2)}) copy-start(bf16[2048,256]{1,0:T(8,128)(2,1)} %reduce-scatter.10.cloned.1.call-done) | copy-start | bytes 3145732
  (61 other events, 278.7 us)
Sparse Core Ops, SparseCore 0:
  25.6 29.7 all-gather.6
  57.8 45.5 all-gather.8
  105.2 28.2 all-gather.10
  135.3 54.3 all-gather.12
  191.4 56.0 all-gather.14
  532.5 69.7 reduce-scatter.9
  606.1 71.2 reduce-scatter.11
  970.6 19.9 reduce-scatter.15
  993.8 39.4 reduce-scatter.13
  1037.1 33.9 reduce-scatter.17
  1074.3 36.0 reduce-scatter.21
  1113.6 61.7 reduce-scatter.19

commit v2 on v1

--- a/solution.py
+++ b/solution.py
@@ -1,5 +1,6 @@
 from functools import partial
 import math
+from types import SimpleNamespace
 
 import jax
 import jax.numpy as jnp
@@ -130,7 +131,7 @@
     last = running[CHUNK - 1 : CHUNK]
     til_end = jnp.exp(last - running)
     write = unit_live * rate
-    return dict(
+    return SimpleNamespace(
         sw=sw,
         full_log=full_log,
         rate=rate,
@@ -219,14 +220,14 @@
         )
         prepared.append(got)
     for unit, got in zip(units, prepared):
-        got["both"] = jnp.concatenate([got["remove_hat"], got["read_hat"]], axis=0)
-        past = jnp.concatenate([stack_heads(got["write_hat"]), stack_heads(got["key_hat"])], axis=0)
-        scores = dot_nt(got["both"], past)
+        got.both = jnp.concatenate([got.remove_hat, got.read_hat], axis=0)
+        past = jnp.concatenate([stack_heads(got.write_hat), stack_heads(got.key_hat)], axis=0)
+        scores = dot_nt(got.both, past)
         past_rest = jnp.concatenate(
-            [stack_heads(halves(got["write_wide"])[1]), stack_heads(halves(got["key_wide"])[1])], axis=0
+            [stack_heads(halves(got.write_wide)[1]), stack_heads(halves(got.key_wide)[1])], axis=0
         )
-        got["read_rest"] = halves(got["read_wide"])[1]
-        fine = scores[CHUNK:] + (dot_nt(got["read_rest"], past) + dot_nt(got["read_hat"], past_rest))
+        got.read_rest = halves(got.read_wide)[1]
+        fine = scores[CHUNK:] + (dot_nt(got.read_rest, past) + dot_nt(got.read_hat, past_rest))
         lower_parts.append(jnp.where(strict, scores[:CHUNK, :PAIR], 0.0))
         lower_key = low(jnp.where(strict, scores[:CHUNK, PAIR:], 0.0))
         reads = low(jnp.where(within_two, fine, 0.0))
@@ -240,10 +241,10 @@
         stacks = [stack_heads(values) for values in lows]
         olds = [state[units[index][1]] for index in group]
         old_parts = [halves(old) for old in olds]
-        from_state = [dot_nt(prepared[index]["both"], old[0]) for index, old in zip(group, old_parts)]
+        from_state = [dot_nt(prepared[index].both, old[0]) for index, old in zip(group, old_parts)]
         read_state = [
             part[CHUNK:]
-            + (dot_nt(prepared[index]["read_rest"], old[0]) + dot_nt(prepared[index]["read_hat"], old[1]))
+            + (dot_nt(prepared[index].read_rest, old[0]) + dot_nt(prepared[index].read_hat, old[1]))
             for index, part, old in zip(group, from_state, old_parts)
         ]
         right = [
@@ -254,9 +255,9 @@
         for slot, index in enumerate(group):
             pair = units[index][1]
             got = prepared[index]
-            ends = jnp.concatenate([got["write_end"], got["key_end"]], axis=0)
+            ends = jnp.concatenate([got.write_end, got.key_end], axis=0)
             adds = dot_tn(jnp.concatenate([removed[slot], lows[slot]], axis=0), ends)
-            state[pair] = olds[slot] * got["final"] + jnp.where(ones_mask, adds, 0.0)
+            state[pair] = olds[slot] * got.final + jnp.where(ones_mask, adds, 0.0)
             u_ref[place_of(units[index])] = removed[slot]
             rows, lanes = place_of(units[index])
             lk_ref[rows, lanes], reads_ref[rows, slice(2 * lanes.start, 2 * lanes.stop)] = scored[index]
@@ -272,7 +273,7 @@
             rows, lanes = place_of(units[index])
             cols = cols_ref[:, lanes]
             normed = centred[slot] * lax.rsqrt(spread[slot] + group_eps)
-            bonus = head_sum(r_ref[rows, lanes] * prepared[index]["lagged"] * cols[4:5], ones_op)
+            bonus = head_sum(r_ref[rows, lanes] * prepared[index].lagged * cols[4:5], ones_op)
             mixed = normed * cols[5:6] + cols[6:7] + bonus * v_ref[rows, lanes]
             y_ref[rows, lanes] = outs[slot]
             z_ref[rows, lanes] = low(mixed * gate_ref[rows, lanes])
@@ -356,109 +357,110 @@
             tri_op,
             ones_op,
         )
-        got.update(rows=rows, lanes=lanes, live=live, cols=cols, pair=pair, chunk=chunk)
+        got.rows, got.lanes, got.live, got.cols = rows, lanes, live, cols
+        got.pair, got.chunk = pair, chunk
         known.append(got)
     for got in known:
-        y = y_ref[got["rows"], got["lanes"]]
-        got["centred"] = y - head_sum(y, ones_op) * mean_of
+        y = y_ref[got.rows, got.lanes]
+        got.centred = y - head_sum(y, ones_op) * mean_of
     for got in known:
-        spread = head_sum(got["centred"] * got["centred"], ones_op) * mean_of
-        got["inv_y"] = lax.rsqrt(spread + group_eps)
+        spread = head_sum(got.centred * got.centred, ones_op) * mean_of
+        got.inv_y = lax.rsqrt(spread + group_eps)
     for got in known:
-        rows, lanes, cols = got["rows"], got["lanes"], got["cols"]
+        rows, lanes, cols = got.rows, got.lanes, got.cols
         r, v, dz = r_ref[rows, lanes], v_ref[rows, lanes], dz_ref[rows, lanes]
-        normed = got["centred"] * got["inv_y"]
-        got["bonus"] = head_sum(r * got["lagged"] * cols[4:5], ones_op)
-        mixed = normed * cols[5:6] + cols[6:7] + got["bonus"] * v
+        normed = got.centred * got.inv_y
+        got.bonus = head_sum(r * got.lagged * cols[4:5], ones_op)
+        mixed = normed * cols[5:6] + cols[6:7] + got.bonus * v
         dgate_ref[rows, lanes] = low(dz * mixed)
         dmix = dz * gate_ref[rows, lanes]
         add_col(5, lanes, dmix * normed)
         add_col(6, lanes, dmix)
         dnormed = dmix * cols[5:6]
-        got["dbonus"] = head_sum(dmix * v, ones_op)
+        got.dbonus = head_sum(dmix * v, ones_op)
         mean_grad = head_sum(dnormed, ones_op) * mean_of
         mean_prod = head_sum(dnormed * normed, ones_op) * mean_of
-        got["dy_low"], got["dy_rest"] = halves(got["inv_y"] * (dnormed - mean_grad - normed * mean_prod))
-        got["dv"] = got["bonus"] * dmix
+        got.dy_low, got.dy_rest = halves(got.inv_y * (dnormed - mean_grad - normed * mean_prod))
+        got.dv = got.bonus * dmix
     for got in known:
-        rows, lanes = got["rows"], got["lanes"]
-        got["both"] = jnp.concatenate([got["remove_hat"], got["read_hat"]], axis=0)
-        got["past"] = jnp.concatenate(
-            [stack_heads(got["write_hat"]), stack_heads(got["key_hat"])], axis=0
+        rows, lanes = got.rows, got.lanes
+        got.both = jnp.concatenate([got.remove_hat, got.read_hat], axis=0)
+        got.past = jnp.concatenate(
+            [stack_heads(got.write_hat), stack_heads(got.key_hat)], axis=0
         )
-        got["lower_key"] = lk_ref[rows, lanes]
+        got.lower_key = lk_ref[rows, lanes]
         reads = reads_ref[rows, slice(2 * lanes.start, 2 * lanes.stop)]
-        got["from_y"] = dot_tn(reads, got["dy_low"])
+        got.from_y = dot_tn(reads, got.dy_low)
         v_low = low(v_ref[rows, lanes])
         removed = u_ref[rows, lanes]
-        got["sent"] = jnp.concatenate([removed, v_low], axis=0)
-        got["stacks"] = jnp.concatenate([stack_heads(removed), stack_heads(v_low)], axis=0)
+        got.sent = jnp.concatenate([removed, v_low], axis=0)
+        got.stacks = jnp.concatenate([stack_heads(removed), stack_heads(v_low)], axis=0)
     for chunk in reversed(range(chunks)):
-        group = [got for got in known if got["chunk"] == chunk]
+        group = [got for got in known if got.chunk == chunk]
         for got in group:
-            got["later"] = dstate[got["pair"]]
-            got["later_low"], got["later_rest"] = halves(got["later"])
-            ends = jnp.concatenate([got["write_end"], got["key_end"]], axis=0)
-            got["from_later"] = dot_nt(ends, got["later_low"])
+            got.later = dstate[got.pair]
+            got.later_low, got.later_rest = halves(got.later)
+            ends = jnp.concatenate([got.write_end, got.key_end], axis=0)
+            got.from_later = dot_nt(ends, got.later_low)
         for got in group:
-            dremoved = low(got["from_later"][:CHUNK] + fold_heads(got["from_y"][:PAIR]))
-            got["dright"] = low(fold_heads(dot_tn(t_ref[got["rows"], got["lanes"]], dremoved)))
+            dremoved = low(got.from_later[:CHUNK] + fold_heads(got.from_y[:PAIR]))
+            got.dright = low(fold_heads(dot_tn(t_ref[got.rows, got.lanes], dremoved)))
         for got in group:
-            got["douts"] = jnp.concatenate([got["dright"], got["dy_low"]], axis=0)
-            adds = dot_tn(got["douts"], got["both"]) + dot_tn(got["dy_rest"], got["read_hat"])
+            got.douts = jnp.concatenate([got.dright, got.dy_low], axis=0)
+            adds = dot_tn(got.douts, got.both) + dot_tn(got.dy_rest, got.read_hat)
             adds = jnp.where(ones_mask, adds, 0.0)
-            dstate[got["pair"]] = got["later"] * got["final"] + adds
+            dstate[got.pair] = got.later * got.final + adds
     for got in known:
-        dv = got["dv"] + got["from_later"][CHUNK:] + fold_heads(got["from_y"][PAIR:])
-        dv = dv + fold_heads(dot_tn(got["lower_key"], got["dright"]))
-        dv_ref[got["rows"], got["lanes"]] = low(dv)
-        dscores = dot_nt(got["douts"], got["stacks"])
-        fine = dscores[CHUNK:] + dot_nt(got["dy_rest"], got["stacks"])
+        dv = got.dv + got.from_later[CHUNK:] + fold_heads(got.from_y[PAIR:])
+        dv = dv + fold_heads(dot_tn(got.lower_key, got.dright))
+        dv_ref[got.rows, got.lanes] = low(dv)
+        dscores = dot_nt(got.douts, got.stacks)
+        fine = dscores[CHUNK:] + dot_nt(got.dy_rest, got.stacks)
         dscores = low(jnp.where(all_masks, jnp.concatenate([dscores[:CHUNK], fine], axis=0), 0.0))
-        old_wide = s_ref[got["chunk"], got["pair"]]
+        old_wide = s_ref[got.chunk, got.pair]
         old_low, old_rest = halves(old_wide)
-        from_old = dot_nn(got["douts"], old_low)
-        fine = from_old[CHUNK:] + (dot_nn(got["dy_rest"], old_low) + dot_nn(got["dy_low"], old_rest))
-        got["dboth"] = jnp.concatenate([from_old[:CHUNK], fine], axis=0) + dot_nn(dscores, got["past"])
-        dpast = dot_tn(dscores, got["both"])
-        got["dwrite_hat"] = fold_heads(dpast[:PAIR])
-        got["dkey_hat"] = fold_heads(dpast[PAIR:])
-        got["dends"] = dot_nn(got["sent"], got["later_low"]) + dot_nn(got["sent"], got["later_rest"])
-        got["dfinal"] = jnp.sum(got["later"] * old_wide, axis=0, keepdims=True)
+        from_old = dot_nn(got.douts, old_low)
+        fine = from_old[CHUNK:] + (dot_nn(got.dy_rest, old_low) + dot_nn(got.dy_low, old_rest))
+        got.dboth = jnp.concatenate([from_old[:CHUNK], fine], axis=0) + dot_nn(dscores, got.past)
+        dpast = dot_tn(dscores, got.both)
+        got.dwrite_hat = fold_heads(dpast[:PAIR])
+        got.dkey_hat = fold_heads(dpast[PAIR:])
+        got.dends = dot_nn(got.sent, got.later_low) + dot_nn(got.sent, got.later_rest)
+        got.dfinal = jnp.sum(got.later * old_wide, axis=0, keepdims=True)
     for got in known:
-        rows, lanes, cols, live = got["rows"], got["lanes"], got["cols"], got["live"]
-
-        def wide(name):
-            return got[name].astype(jnp.float32)
+        rows, lanes, cols, live = got.rows, got.lanes, got.cols, got.live
+
+        def wide(values):
+            return values.astype(jnp.float32)
 
         r, k = r_ref[rows, lanes], k_ref[rows, lanes]
-        dwrite_hat, dkey_hat = got["dwrite_hat"], got["dkey_hat"]
-        dwrite_end, dkey_end = got["dends"][:CHUNK], got["dends"][CHUNK:]
-        dremove_hat, dread_hat = got["dboth"][:CHUNK], got["dboth"][CHUNK:]
-        dbonus, lagged = got["dbonus"], got["lagged"]
+        dwrite_hat, dkey_hat = got.dwrite_hat, got.dkey_hat
+        dwrite_end, dkey_end = got.dends[:CHUNK], got.dends[CHUNK:]
+        dremove_hat, dread_hat = got.dboth[:CHUNK], got.dboth[CHUNK:]
+        dbonus, lagged = got.dbonus, got.lagged
         bonus_lag = dbonus * lagged
         add_col(4, lanes, bonus_lag * r)
-        dr_ref[rows, lanes] = low(bonus_lag * cols[4:5] + dread_hat * got["grown"])
-        minus = wide("remove_hat") * dremove_hat
-        plus = wide("read_hat") * dread_hat + minus
-        plus = plus - wide("write_hat") * dwrite_hat - wide("key_hat") * dkey_hat
-        ending = wide("write_end") * dwrite_end + wide("key_end") * dkey_end
+        dr_ref[rows, lanes] = low(bonus_lag * cols[4:5] + dread_hat * got.grown)
+        minus = wide(got.remove_hat) * dremove_hat
+        plus = wide(got.read_hat) * dread_hat + minus
+        plus = plus - wide(got.write_hat) * dwrite_hat - wide(got.key_hat) * dkey_hat
+        ending = wide(got.write_end) * dwrite_end + wide(got.key_end) * dkey_end
         sums = split_dot(sums_op, jnp.concatenate([plus, ending], axis=0))
-        dlog = sums - minus + got["final"] * got["dfinal"]
-        ddw = jnp.where(live, dlog * got["full_log"] * (1.0 - got["sw"]), 0.0)
+        dlog = sums - minus + got.final * got.dfinal
+        ddw = jnp.where(live, dlog * got.full_log * (1.0 - got.sw), 0.0)
         add_col(0, lanes, ddw)
         ddw_ref[rows, lanes] = low(ddw)
-        dwrite = dwrite_hat * got["shrunk"] + dwrite_end * got["til_end"]
-        dlag = dbonus * r * cols[4:5] + dkey_hat * got["shrunk"] + dkey_end * got["til_end"]
+        dwrite = dwrite_hat * got.shrunk + dwrite_end * got.til_end
+        dlag = dbonus * r * cols[4:5] + dkey_hat * got.shrunk + dkey_end * got.til_end
         dlag = jnp.where(live, dlag, 0.0)
-        rate = got["rate"]
-        dunit = jnp.where(live, dwrite * rate - dremove_hat * got["before"], 0.0)
+        rate = got.rate
+        dunit = jnp.where(live, dwrite * rate - dremove_hat * got.before, 0.0)
         lag_k = dlag * k
-        drate = dwrite * got["unit_live"] + lag_k * cols[3:4]
+        drate = dwrite * got.unit_live + lag_k * cols[3:4]
         add_col(3, lanes, lag_k * (rate - 1.0))
-        dscaled = got["inv"] * (dunit - got["unit"] * head_sum(dunit * got["unit"], ones_op))
+        dscaled = got.inv * (dunit - got.unit * head_sum(dunit * got.unit, ones_op))
         add_col(2, lanes, dscaled * k)
-        dk_ref[rows, lanes] = low(dlag * got["lag_scale"] + dscaled * cols[2:3])
+        dk_ref[rows, lanes] = low(dlag * got.lag_scale + dscaled * cols[2:3])
         dda = drate * rate * (1.0 - rate)
         add_col(1, lanes, dda)
         dda_ref[rows, lanes] = low(dda)
@@ -869,6 +871,172 @@
     )(x)
 
 
+def input_backward_kernel(
+    seq_len, splits, whole_ref, dr_ref, dk_ref, dv_ref, dl_ref, three_ref, down_ref, params_ref, din_ref, gparams_ref, gdown_ref, carry, kept
+):
+    step = pl.program_id(0)
+    tile = pl.num_programs(0) - 1 - step
+    rows_each = dr_ref.shape[0]
+    part = dr_ref.shape[1]
+    width = whole_ref.shape[1]
+    start = tile * rows_each
+    at_start = lax.rem(start, seq_len) == 0
+    at_end = lax.rem(start + rows_each, seq_len) == 0
+
+    @pl.when(step == 0)
+    def _():
+        gparams_ref[...] = jnp.zeros_like(gparams_ref)
+        gdown_ref[...] = jnp.zeros_like(gdown_ref)
+
+    @pl.when(at_end)
+    def _():
+        carry[...] = jnp.zeros_like(carry)
+
+    edge = 16
+    rows = pl.ds(pl.multiple_of(start, rows_each), rows_each)
+    edge_rows = pl.ds(pl.multiple_of(jnp.maximum(start - edge, 0), edge), edge)
+    inverse_width = 1.0 / width
+
+    def moments(place):
+        values = whole_ref[place, :].astype(jnp.float32)
+        centre = jnp.sum(values, axis=1, keepdims=True) * inverse_width
+        values = values - centre
+        spread = jnp.sum(values * values, axis=1, keepdims=True) * inverse_width
+        return centre, lax.rsqrt(spread + norm_eps)
+
+    centre, inv = moments(rows)
+    edge_centre, edge_inv = moments(edge_rows)
+    block_cols = 256
+    row_index = iota((rows_each, block_cols), 0)
+    dl = dl_ref[...]
+    lane = iota(dl.shape, 1)
+    zero = jnp.zeros_like(dl)
+    first, second = splits
+    dls = (
+        jnp.where(lane < first, dl, zero),
+        jnp.where((lane >= first) & (lane < second), dl, zero),
+        jnp.where(lane >= second, dl, zero),
+    )
+    down_row = iota((dl.shape[1], block_cols), 0)
+    sum_grad = jnp.zeros((rows_each, 1), jnp.float32)
+    sum_prod = jnp.zeros((rows_each, 1), jnp.float32)
+
+    def add_param(index, cols, values):
+        total = values[0:8]
+        for place in range(8, rows_each, 8):
+            total = total + values[place : place + 8]
+        gparams_ref[index, :, cols] += total
+
+    for block in range(width // block_cols):
+        cols = slice(block * block_cols, (block + 1) * block_cols)
+        gain, bias = params_ref[0:1, cols], params_ref[1:2, cols]
+        unit = (whole_ref[rows, cols].astype(jnp.float32) - centre) * inv
+        normed = unit * gain + bias
+        edge_unit = (whole_ref[edge_rows, cols].astype(jnp.float32) - edge_centre) * edge_inv
+        edge_normed = (edge_unit * gain + bias)[edge - 1 : edge]
+        edge_normed = jnp.where(at_start, 0.0, edge_normed)
+        before = jnp.where(row_index == 0, edge_normed, pltpu.roll(normed, 1, 0))
+        shift = before - normed
+        down = down_ref[cols, :]
+        weights = three_ref[cols, :]
+        grads = (
+            dot_nt(dr_ref[...], weights[:, :part]),
+            dot_nt(dls[0], down),
+            dot_nt(dk_ref[...], weights[:, part : 2 * part]),
+            dot_nt(dv_ref[...], weights[:, 2 * part :]),
+            dot_nt(dls[1], down),
+            dot_nt(dls[2], down),
+        )
+        total = grads[0]
+        for grad in grads[1:]:
+            total = total + grad
+        mixed = None
+        for index, grad in enumerate(grads):
+            rate = params_ref[2 + index : 3 + index, cols]
+            mixed = grad * rate if mixed is None else mixed + grad * rate
+            add_param(2 + index, cols, grad * shift)
+        after = jnp.where(row_index == rows_each - 1, carry[0:1, cols], pltpu.roll(mixed, rows_each - 1, 0))
+        carry[0:1, cols] = mixed[0:1]
+        dnormed = total - mixed + after
+        add_param(0, cols, dnormed * unit)
+        add_param(1, cols, dnormed)
+        dunit = dnormed * gain
+        kept[:, cols] = dunit
+        sum_grad = sum_grad + jnp.sum(dunit, axis=1, keepdims=True)
+        sum_prod = sum_prod + jnp.sum(dunit * unit, axis=1, keepdims=True)
+        outs = [
+            dot_tn(dl, low(normed + shift * params_ref[index : index + 1, cols])) for index in (3, 6, 7)
+        ]
+        gdown_ref[:, cols] += jnp.where(
+            down_row < first, outs[0], jnp.where(down_row < second, outs[1], outs[2])
+        )
+    sum_grad = sum_grad * inverse_width
+    sum_prod = sum_prod * inverse_width
+    for block in range(width // block_cols):
+        cols = slice(block * block_cols, (block + 1) * block_cols)
+        unit = (whole_ref[rows, cols].astype(jnp.float32) - centre) * inv
+        din_ref[:, cols] = low(inv * (kept[:, cols] - sum_grad - unit * sum_prod))
+
+
+def input_backward(whole, dr, dk, dv, dl, splits, three, down, params):
+    positions, width = whole.shape
+    part = dr.shape[1]
+    rows_each = 256
+    steps = positions // rows_each
+    tile = lambda cols: pl.BlockSpec((rows_each, cols), lambda i: (steps - 1 - i, 0))
+    full = pl.BlockSpec(memory_space=pltpu.VMEM)
+    shape = jax.ShapeDtypeStruct
+    return pl.pallas_call(
+        partial(input_backward_kernel, SEQ_LEN, splits),
+        grid=(steps,),
+        in_specs=[full, tile(part), tile(part), tile(part), tile(dl.shape[1]), full, full, full],
+        out_specs=[
+            tile(width),
+            pl.BlockSpec((8, 8, width), lambda i: (0, 0, 0)),
+            pl.BlockSpec((dl.shape[1], width), lambda i: (0, 0)),
+        ],
+        out_shape=[
+            shape((positions, width), jnp.bfloat16),
+            shape((8, 8, width), jnp.float32),
+            shape((dl.shape[1], width), jnp.float32),
+        ],
+        scratch_shapes=[pltpu.VMEM((8, width), jnp.float32), pltpu.VMEM((rows_each, width), jnp.float32)],
+        compiler_params=pltpu.CompilerParams(
+            dimension_semantics=("arbitrary",), vmem_limit_bytes=48 * 1024 * 1024
+        ),
+        name="input_backward",
+    )(whole, dr, dk, dv, dl, three, down, params)
+
+
+def weight_grads_kernel(left_refs, right_refs, out_ref):
+    part = right_refs[0].shape[1]
+    for index, (left_ref, right_ref) in enumerate(zip(left_refs, right_refs)):
+        out_ref[:, index * part : (index + 1) * part] = low(dot_tn(left_ref[...], right_ref[...]))
+
+
+def weight_grads(lefts, rights):
+    positions, width = lefts[0].shape
+    part = rights[0].shape[1]
+    count = len(lefts)
+    block = 512
+
+    def kernel(*refs):
+        weight_grads_kernel(refs[:count], refs[count : 2 * count], refs[2 * count])
+
+    return pl.pallas_call(
+        kernel,
+        grid=(width // block,),
+        in_specs=[pl.BlockSpec((positions, block), lambda i: (0, i))] * count
+        + [pl.BlockSpec((positions, part), lambda i: (0, 0))] * count,
+        out_specs=pl.BlockSpec((block, count * part), lambda i: (i, 0)),
+        out_shape=jax.ShapeDtypeStruct((width, count * part), jnp.bfloat16),
+        compiler_params=pltpu.CompilerParams(
+            dimension_semantics=("arbitrary",), vmem_limit_bytes=40 * 1024 * 1024
+        ),
+        name="weight_grads",
+    )(*lefts, *rights)
+
+
 def matmul(left_op, right_op):
     return jnp.dot(left_op, right_op, preferred_element_type=jnp.float32)
 
@@ -927,14 +1095,14 @@
     seq_dev = position_count // SEQ_LEN
     mp_index = lax.axis_index("mp")
     col_start = mp_index * part_width
-    quarter = position_count // lax.axis_size("mp")
-    row_start = mp_index * quarter
+    groups = lax.axis_size("dp")
     own_lengths = lax.dynamic_slice_in_dim(lengths, lax.axis_index("dp") * seq_dev, seq_dev)
     places = jnp.arange(SEQ_LEN, dtype=jnp.int32)
     valid = (places[None, :] < own_lengths[:, None]).astype(jnp.float32).reshape(position_count)
     loss_scale = position_count * lax.axis_size("dp") / jnp.sum(lengths).astype(jnp.float32)
     line_size = lax.axis_size("mp")
-    whole = line_gather(hidden, line_size, 1).astype(jnp.float32)
+    whole_low = line_gather(hidden, line_size, 1)
+    whole = whole_low.astype(jnp.float32)
     low_rank = (decay_down.shape[1], rate_down.shape[1], gate_down.shape[1])
     narrow = jnp.concatenate([decay_down, rate_down, gate_down, feature_params], axis=1)
     narrow = jnp.pad(narrow, ((0, 0), (0, -narrow.shape[1] % 128)))
@@ -960,7 +1128,7 @@
     ffn_value_w = lax.all_gather(ffn_value, "dp", axis=1, tiled=True)
     params = params_low.astype(jnp.float32)
     model_width = whole.shape[1]
-    mixed, back_in = jax.vjp(section_in, whole, params[:, 0], params[:, 1], params[:, 2:8])
+    mixed = section_in(whole, params[:, 0], params[:, 1], params[:, 2:8])
     mix_r, mix_w, mix_k, mix_v, mix_a, mix_g = tuple(
         (member.astype(jnp.bfloat16) for member in mixed)
     )
@@ -1021,109 +1189,97 @@
     d_recept, d_keys, d_values, d_decay, d_rate, d_gate, d_columns = run_mixer_backward(
         *mixer_args, *kept, d_gated
     )
-    d_columns = jnp.sum(d_columns, axis=1)[:7].T
-    grad_three = jnp.concatenate(
+    d_columns = jnp.sum(d_columns, axis=1)[:7]
+    grad_three = weight_grads((mix_r, mix_k, mix_v), (d_recept, d_keys, d_values))
+    d_decay, d_rate, d_gate, grad_three = lax.optimization_barrier((d_decay, d_rate, d_gate, grad_three))
+    grad_three = lax.psum_scatter(grad_three, "dp", scatter_dimension=0, tiled=True)
+    shares = [rank // line_size for rank in low_rank]
+    starts = (0, shares[0], shares[0] + shares[1])
+    own_rank = sum(shares) + -sum(shares) % 128
+
+    def spread_rows(weight, share, start):
+        grouped = weight.reshape(line_size, share, part_width)
+        grouped = jnp.pad(grouped, ((0, 0), (start, own_rank - start - share), (0, 0)))
+        return grouped.reshape(line_size * own_rank, part_width)
+
+    def own_columns(values, share):
+        return lax.dynamic_slice_in_dim(values, mp_index * share, share, 1)
+
+    def own_group(members):
+        taken = jnp.concatenate(
+            [own_columns(member, share) for member, share in zip(members, shares)], axis=1
+        )
+        return jnp.pad(taken, ((0, 0), (0, own_rank - sum(shares))))
+
+    d_inner = (
+        against(d_decay, spread_rows(decay_up_w, shares[0], starts[0]))
+        + against(d_rate, spread_rows(rate_up_w, shares[1], starts[1]))
+        + against(d_gate, spread_rows(gate_up_w, shares[2], starts[2]))
+    ).astype(jnp.bfloat16)
+    d_own = line_scatter(d_inner, line_size, 6)
+    d_own, grad_ffn_key, grad_output_proj = lax.optimization_barrier(
+        (d_own, grad_ffn_key, grad_output_proj)
+    )
+    slope = own_group(
+        (
+            1.0 - decay_hid * decay_hid,
+            jnp.ones((position_count, low_rank[1]), jnp.float32),
+            gate_hid * (1.0 - gate_hid),
+        )
+    )
+    d_own_pre = (d_own * slope).astype(jnp.bfloat16)
+    down_own = own_group((decay_down_w, rate_down_w, gate_down_w))
+    params_rows = jnp.pad(params.T, ((0, -params.shape[1] % 8), (0, 0)))
+    d_in_part, d_params_in, d_down = input_backward(
+        whole_low, d_recept, d_keys, d_values, d_own_pre, starts[1:], three, down_own, params_rows
+    )
+    up_grads = jnp.concatenate(
         [
-            contract_rows(mix_r, d_recept).astype(jnp.bfloat16),
-            contract_rows(mix_k, d_keys).astype(jnp.bfloat16),
-            contract_rows(mix_v, d_values).astype(jnp.bfloat16),
+            contract_rows(low_part, grad).reshape(groups, -1, part_width)
+            for low_part, grad in ((decay_low, d_decay), (rate_low, d_rate), (gate_low, d_gate))
         ],
         axis=1,
-    )
-    d_recept, d_keys, d_values, grad_three = lax.optimization_barrier(
-        (d_recept, d_keys, d_values, grad_three)
-    )
-    grad_three = lax.psum_scatter(grad_three, "dp", scatter_dimension=0, tiled=True)
-    grad_decay_up = contract_rows(decay_low, d_decay)
-    grad_rate_up = contract_rows(rate_low, d_rate)
-    grad_gate_up = contract_rows(gate_low, d_gate)
-    d_inner = jnp.concatenate(
-        [against(d_decay, decay_up_w), against(d_rate, rate_up_w), against(d_gate, gate_up_w)], axis=1
     ).astype(jnp.bfloat16)
-    d_inner = jnp.pad(d_inner, ((0, 0), (0, -d_inner.shape[1] % 128)))
-    d_inner = line_sum(d_inner, line_size, 6)
-    d_inner, grad_ffn_key = lax.optimization_barrier((d_inner, grad_ffn_key))
-    d_inner = d_inner.astype(jnp.float32)
-    d_decay_hid = d_inner[:, : low_rank[0]]
-    d_rate_hid = d_inner[:, low_rank[0] : low_rank[0] + low_rank[1]]
-    d_gate_hid = d_inner[:, low_rank[0] + low_rank[1] : sum(low_rank)]
-    d_decay_pre = (d_decay_hid * (1.0 - decay_hid * decay_hid)).astype(jnp.bfloat16)
-    d_rate_pre = d_rate_hid.astype(jnp.bfloat16)
-    d_gate_pre = (d_gate_hid * gate_hid * (1.0 - gate_hid)).astype(jnp.bfloat16)
-
-    def own_rows(values):
-        return lax.dynamic_slice_in_dim(values, row_start, quarter, 0)
-
-    def place_rows(values):
-        return lax.dynamic_update_slice_in_dim(
-            jnp.zeros((position_count, values.shape[1]), jnp.float32), values, row_start, 0
-        )
-
-    groups = lax.axis_size("dp")
-    row_block = decay_down.shape[0]
-
-    def own_features(values):
-        split = values.reshape(position_count, groups, lax.axis_size("mp"), row_block)
-        taken = lax.dynamic_index_in_dim(split, mp_index, 2, keepdims=False)
-        return taken.reshape(position_count, groups * row_block)
-
-    grad_downs = jnp.concatenate(
+    d_in_part, grad_three, up_grads = lax.optimization_barrier((d_in_part, grad_three, up_grads))
+    up_grads = lax.psum_scatter(up_grads, "dp", scatter_dimension=0, tiled=True)
+    up_grads = up_grads.reshape(-1, part_width).astype(jnp.float32)
+    core_grads = lax.dynamic_update_slice_in_dim(
+        jnp.zeros((7, model_width), jnp.float32), d_columns, col_start, 1
+    )
+    param_rows = jnp.concatenate(
         [
-            contract_rows(own_features(mix_w), d_decay_pre),
-            contract_rows(own_features(mix_a), d_rate_pre),
-            contract_rows(own_features(mix_g), d_gate_pre),
+            jnp.sum(d_params_in, axis=1),
+            core_grads,
+            d_scale_two[None],
+            d_offset_two[None],
+            d_mix_two[None],
         ],
-        axis=1,
-    )
-    cotangents = (
-        against(d_recept, recept_w),
-        place_rows(against(own_rows(d_decay_pre), decay_down_w)),
-        against(d_keys, key_w),
-        against(d_values, value_w),
-        place_rows(against(own_rows(d_rate_pre), rate_down_w)),
-        place_rows(against(own_rows(d_gate_pre), gate_down_w)),
-    )
-    d_in_part, d_scale_one, d_offset_one, d_mix_one = back_in(cotangents)
-    d_in_part, grad_output_proj = lax.optimization_barrier((d_in_part.astype(jnp.bfloat16), grad_output_proj))
+        axis=0,
+    )
+    param_count = param_rows.shape[0]
+    narrow_grads = jnp.pad(
+        jnp.concatenate([d_down, param_rows], axis=0), ((0, -(own_rank + param_count) % 8), (0, 0))
+    )
+    d_in_part, narrow_grads = lax.optimization_barrier((d_in_part, narrow_grads))
+    narrow_grads = lax.psum_scatter(narrow_grads, "dp", scatter_dimension=1, tiled=True)
     grad_hidden = lax.dynamic_slice_in_dim(d_residual, col_start, part_width, 1) + line_scatter(
         d_in_part, line_size, 7
     )
-    core_grads = lax.dynamic_update_slice_in_dim(
-        jnp.zeros((model_width, 7), jnp.float32), d_columns, col_start, 0
-    )
-    grad_params = jnp.concatenate(
-        [
-            d_scale_one[:, None],
-            d_offset_one[:, None],
-            d_mix_one,
-            core_grads,
-            d_scale_two[:, None],
-            d_offset_two[:, None],
-            d_mix_two[:, None],
-        ],
-        axis=1,
-    )
-    param_parts = grad_params.reshape(groups, lax.axis_size("mp"), row_block, grad_params.shape[1])
-    param_parts = lax.psum_scatter(
-        param_parts.transpose(1, 0, 2, 3), "mp", scatter_dimension=0, tiled=True
-    ).reshape(model_width // lax.axis_size("mp"), grad_params.shape[1])
-    narrow_grads = lax.psum_scatter(
-        jnp.concatenate([grad_downs, param_parts], axis=1), "dp", scatter_dimension=0, tiled=True
-    )
-    up_grads = jnp.concatenate(
-        [member.reshape(groups, -1, part_width) for member in (grad_decay_up, grad_rate_up, grad_gate_up)],
-        axis=1,
-    ).astype(jnp.bfloat16)
-    up_grads = lax.psum_scatter(up_grads, "dp", scatter_dimension=0, tiled=True)
-    up_grads = up_grads.reshape(-1, part_width).astype(jnp.float32)
-    first, second = low_rank[0], low_rank[0] + low_rank[1]
+    row_block = decay_down.shape[0]
+    narrow_grads = lax.all_gather(narrow_grads, "mp", axis=0)
+    narrow_grads = lax.dynamic_slice_in_dim(narrow_grads, mp_index * row_block, row_block, 2)
+
+    def down_grad(start, share):
+        return narrow_grads[:, start : start + share].reshape(line_size * share, row_block).T
+
+    grad_params = jnp.sum(narrow_grads[:, own_rank : own_rank + param_count], axis=0).T
     return (
         result.astype(jnp.bfloat16),
         grad_hidden,
-        narrow_grads[:, sum(low_rank) :],
-        narrow_grads[:, :first],
-        narrow_grads[:, first:second],
-        narrow_grads[:, second : sum(low_rank)],
+        grad_params,
+        down_grad(starts[0], shares[0]),
+        down_grad(starts[1], shares[1]),
+        down_grad(starts[2], shares[2]),
         up_grads[: up_rows[0]],
         up_grads[up_rows[0] : up_rows[0] + up_rows[1]],
         up_grads[up_rows[0] + up_rows[1] :],

time: 1200 us -> 1040 us (0.87)
  matrix products: 201 us -> 136 us
  local copies, waits for them, and re-layouts: 108 us -> 61.5 us
  waiting for transfers between devices: 69.8 us -> 28 us
  other arithmetic: 135 us -> 95.1 us
  Pallas kernels: 630 us -> 649 us
  blocking collectives: 25.4 us -> 44.4 us
    dot_general x12 -> x6, matrix products: 93.3 us -> 38 us  [against(): jnp.einsum('tn,kn->tk', grad_op, weight_op, preferred_element_type=jnp.fl...]
    pallas_call x3 -> x2, Pallas kernels: 269 us -> 222 us  [line_sum(): pl.pallas_call(partial(line_sum_kernel, size, chunk_rows), out_shape=jax....]
    pallas_call x0 -> x2, Pallas kernels: none -> 40.8 us  [the longest x1 30.2 us: input_backward(): pl.pallas_call(partial(input_backward_kernel, SEQ_LEN, splits), grid=(ste...]
    reduce_scatter x1, waiting for transfers between devices: 55.2 us -> 23.5 us  [body(): lax.psum_scatter(grad_three, 'dp', scatter_dimension=0, tiled=True)]
    pallas_call x2 -> x3, Pallas kernels: 142 us -> 164 us  [line_scatter(): pl.pallas_call(partial(line_scatter_kernel, size, chunk_rows), out_shape=...]
    convert_element_type x3 -> x0, local copies, waits for them, and re-layouts: 19.4 us -> none  [body(): member.astype(jnp.bfloat16)]
    all_gather x0 -> x1, blocking collectives: none -> 18 us  [body(): narrow_grads = lax.all_gather(narrow_grads, 'mp', axis=0)]
    reduce_sum x2 -> x1, other arithmetic: 31.3 us -> 14.5 us  [layer_norm(): return centred * lax.rsqrt(spread + norm_eps) * scale_in + offset]
  transfers between devices with their start and end apart: 12 -> 11, of which waited for: 2 -> 2; matrix products, arithmetic and copies ran while one was open for 21% -> 21% of each run, Pallas kernels for 41% -> 49%
where the time goes in v2:
time: 1040 us; the launch traced here: 1030 us
  Pallas kernels  649 us (62%)
  matrix products  136 us (13%)
  other arithmetic  95.1 us (9%)
  local copies, waits for them, and re-layouts  61.5 us (6%)
  blocking collectives  44.4 us (4%)
  waiting for transfers between devices  28 us (3%)
  between operations  15.9 us (2%)
    pallas_call x2, Pallas kernels, line_sum(): pl.pallas_call(partial(line_sum_kernel, size, chunk_rows), out_shape=jax....  222 us
    pallas_call x3, Pallas kernels, line_scatter(): pl.pallas_call(partial(line_scatter_kernel, size, chunk_rows), out_shape=...  164 us
    pallas_call x2, Pallas kernels, line_gather(): pl.pallas_call(partial(line_gather_kernel, size, chunk_rows), out_shape=j...  143 us
    dot_general x12, matrix products, matmul(): return jnp.dot(left_op, right_op, preferred_element_type=jnp.float32)  62.4 us
    pallas_call x1, Pallas kernels, run_mixer_backward(): pl.pallas_call(partial(mixer_backward, steps_per_seq), grid=(steps,), in_...  43.2 us
    unnamed x130, local copies, waits for them, and re-layouts  40.3 us
    dot_general x6, matrix products, against(): jnp.einsum('tn,kn->tk', grad_op, weight_op, preferred_element_type=jnp.fl...  38 us
    pallas_call x1, Pallas kernels, run_mixer_forward(): pl.pallas_call(partial(mixer_forward, steps_per_seq), grid=(steps,), in_s...  35.6 us
  transfers between devices with their start and end apart: 11, of which 2 were waited for; matrix products, arithmetic and copies ran while one was open for 21% of the time, Pallas kernels for 49%

profile of v2, /device:TPU:0, one launch (start us, length us, event | category | flops | bytes accessed | tf_op | source)
XLA Modules:
  0.0 1030.2 jit_solution(1073739410833734450)
XLA Ops:
  9.0 15.6 %all_gather.30 = bf16[256,512]{1,0:T(8,128)(2,1)S(1)} all-gather(bf16[64,512]{1,0:T(8,128)(2,1)S(1)} %fusion.64), channel_id=1, replica_groups=mesh['dp'=8,'mp'=4] {'mp'}, dimensions={0}, use_global_device_ids=true | all-gather | bytes 327680 | tf_op jit(solution)/shard_map/all_gather | solution.py:1109
  30.3 10.7 %all-gather = bf16[448,512]{1,0:T(8,128)(2,1)S(1)} all-gather(bf16[56,512]{1,0:T(8,128)(2,1)S(1)} %pad_maximum_fusion.4), channel_id=2, replica_groups=mesh['dp'=8,'mp'=4] {'dp'}, dimensions={0}, use_global_device_ids=true | all-gather | bytes 516096 | tf_op jit(solution)/shard_map/all_gather | solution.py:1122
  44.4 71.4 %line_gather.2.whole_ref = bf16[1024,2048]{1,0:T(8,128)(2,1)S(1)} custom-call(bf16[1024,512]{1,0:T(8,128)(2,1)S(1)} %copy-done.31), custom_call_target="tpu_custom_call" | custom-call | bytes 251658240 | tf_op jit(solution)/shard_map/line_gather/pallas_call | solution.py:748
  119.1 3.4 fusion.2
  124.4 3.9 fusion.12
  128.4 3.2 fusion.47
  133.4 3.1 fusion.44
  138.2 3.2 fusion.41
  144.2 9.2 fusion.15
  153.5 5.3 fusion.30.r_ref
  159.4 2.3 fusion.28.k_ref
  161.9 3.7 fusion.26.v_ref
  165.6 35.6 %mixer_forward.1 = (bf16[1024,512]{1,0:T(8,128)(2,1)S(1)}, f32[1024,512]{1,0:T(8,128)S(1)}, bf16[1024,512]{1,0:T(8,128)(2,1)S(1)}, bf16[1024,512]{1,0:T(8,128)(2...) custom-call(s32[1]{0:T(128)} %dynamic_slice.33.length_ref, ...), custom_call_target="tpu_custom_call" | custom-call | tf_op jit(solution)/shard_map/mixer_forward/pallas_call | solution.py:477
  205.9 6.4 convolution_convert_fusion.3.x_ref
  212.3 112.6 %line_sum.2 = bf16[1024,2048]{1,0:T(8,128)(2,1)S(1)} custom-call(bf16[1024,2048]{1,0:T(8,128)(2,1)} %convolution_convert_fusion.3.x_ref), custom_call_target="tpu_custom_call" | custom-call | bytes 335544320 | tf_op jit(solution)/shard_map/line_sum/pallas_call | solution.py:664
  326.1 4.3 convert_add_fusion
  330.5 2.3 fusion.19
  332.7 3.2 copy-done.40
  336.0 6.5 add_convert_fusion.1
  342.5 14.6 %fusion.83 = f32[1024,2048]{1,0:T(8,128)} fusion(bf16[1024,2048]{1,0:T(8,128)(2,1)} %add_convert_fusion.1, bf16[2048,2048]{1,0:T(8,128)(2,1)} %all-gather.14.cloned.1.call-done), kind=kOutput, calls=%fused_computation.126 | convolution fusion | flops 8589934592 | bytes 20971520 | tf_op jit(solution)/shard_map/dot_general | solution.py:1041
  357.1 15.3 %convolution_convert_fusion.2.x_ref = bf16[1024,2048]{1,0:T(8,128)(2,1)} fusion(bf16[2048,2048]{1,0:T(8,128)(2,1)} %all-gather.16.cloned.1.call-done, f32[1024,2048]{1,0:T(8,128)} %fusion.83), kind=kOutput, calls=%fused_computation.42 | convolution fusion | flops 8598323200 | bytes 20971520 | tf_op jit(solution)/shard_map/dot_general | solution.py:1041
  372.4 69.2 %line_scatter.3 = f32[1024,512]{1,0:T(8,128)S(1)} custom-call(bf16[1024,2048]{1,0:T(8,128)(2,1)} %convolution_convert_fusion.2.x_ref), custom_call_target="tpu_custom_call" | custom-call | bytes 251658240 | tf_op jit(solution)/shard_map/line_scatter/pallas_call | solution.py:855
  441.6 2.9 multiply_convert_fusion.2
  444.5 71.3 %line_gather.3 = bf16[1024,2048]{1,0:T(8,128)(2,1)S(1)} custom-call(bf16[1024,512]{1,0:T(8,128)(2,1)S(1)} %get-tuple-element.129.x_ref), custom_call_target="tpu_custom_call" | custom-call | bytes 251658240 | tf_op jit(solution)/shard_map/line_gather/pallas_call | solution.py:748
  517.8 14.6 %convolution_convert_fusion.1 = bf16[2048,2048]{1,0:T(8,128)(2,1)} fusion(bf16[1024,2048]{1,0:T(8,128)(2,1)S(1)} %line_gather.3, f32[1024,2048]{1,0:T(8,128)} %fusion.83), kind=kOutput, calls=%fused_computation.37 | convolution fusion | flops 8600420352 | bytes 20971520 | tf_op jit(solution)/shard_map/tk,tn->kn/dot_general | solution.py:1045
  532.5 15.1 %multiply_convert_fusion = bf16[1024,2048]{1,0:T(8,128)(2,1)S(1)} fusion(f32[1024,2048]{1,0:T(8,128)} %fusion.83, bf16[1024,2048]{1,0:T(8,128)(2,1)} %copy-done.6, bf16[2048,2048]{1,0:T(8,128)(2,1)} %all-gather.16.cloned.1.call-done), kind=kOutput, calls=%fused_computation.30 | convolution fusion | flops 8598323200 | bytes 25165824 | tf_op jit(solution)/shard_map/tn,kn->tk/dot_general | solution.py:1049
  547.6 2.1 copy-done.60
  549.7 11.4 %convolution_convert_fusion = bf16[2048,2048]{1,0:T(8,128)(2,1)} fusion(bf16[1024,2048]{1,0:T(8,128)(2,1)S(1)} %copy-done.46, bf16[1024,2048]{1,0:T(8,128)(2,1)S(1)} %multiply_convert_fusion), kind=kOutput, calls=%fused_computation.36 | convolution fusion | flops 8594128896 | bytes 16777216 | tf_op jit(solution)/shard_map/tk,tn->kn/dot_general | solution.py:1045
  561.1 13.0 %fusion.84 = f32[1024,2048]{1,0:T(8,128)S(1)} fusion(bf16[1024,2048]{1,0:T(8,128)(2,1)} %copy-done.60, bf16[2048,2048]{1,0:T(8,128)(2,1)} %all-gather.14.cloned.1.call-done), kind=kOutput, calls=%fused_computation.127 | convolution fusion | flops 8589934592 | bytes 20971520 | tf_op jit(solution)/shard_map/tn,kn->tk/dot_general | solution.py:1049
  574.2 3.3 copy-done.41
  579.2 5.2 split.4
  585.7 14.5 %multiply_reduce_fusion.1 = (f32[2048]{0:T(1024)S(1)}, f32[1024]{0:T(1024)S(1)}, f32[2048]{0:T(1024)S(1)}, f32[2048]{0:T(1024)}, f32[1024,2048]{1,0:T(8,128)S(1)}) fusion(f32[1024]{0:T(1024)S(1)} %fusion.67, f32[1024]{0:T(1024)S(1)} %broadcast_multiply_fusion, bf16[1024,2048]{1,0:T(8,128)(2,1)S(1)} %copy-done.5, bf16[1024,2048]{1,0:T(8,128)(2,1)S(1)} %copy-done.3, ...), kind=kLoop, calls=%fused_computation.26 | loop fusion | flops 41935872 | bytes 41988096 | tf_op jit(solution)/shard_map/transpose(jvp())/reduce_sum | solution.py:1056
  600.2 5.4 fusion.78
  605.6 6.1 add_convert_fusion.x_ref
  611.7 109.4 %line_sum.3 = bf16[1024,2048]{1,0:T(8,128)(2,1)S(1)} custom-call(bf16[1024,2048]{1,0:T(8,128)(2,1)} %add_convert_fusion.x_ref), custom_call_target="tpu_custom_call" | custom-call | bytes 335544320 | tf_op jit(solution)/shard_map/line_sum/pallas_call | solution.py:664
  721.2 6.7 convert_add_fusion.1
  727.9 5.9 convolution_convert_fusion.4
  734.8 6.7 fusion.85.dz_ref
  745.8 43.2 %mixer_backward.1 = (bf16[1024,512]{1,0:T(8,128)(2,1)S(1)}, bf16[1024,512]{1,0:T(8,128)(2,1)S(1)}, bf16[1024,512]{1,0:T(8,128)(2,1)S(1)}, bf16[1024,512]{1,0:T(8...) custom-call(s32[1]{0:T(128)} %dynamic_slice.33.length_ref, ...), custom_call_target="tpu_custom_call" | custom-call | tf_op jit(solution)/shard_map/mixer_backward/pallas_call | solution.py:514
  791.9 10.5 %weight_grads.1 = bf16[2048,1536]{1,0:T(8,128)(2,1)} custom-call(bf16[1024,2048]{1,0:T(8,128)(2,1)S(1)} %copy-done.8, bf16[1024,2048]{1,0:T(8,128)(2,1)S(1)} %copy-done.10, bf16[1024,2048]{1,0:T(8,128)(2,1)} %get-tuple-element.126.refs_2_, bf16[1024,512]{1,0:T(8,128)(2,1)S(1)} %get-tuple-element.64.refs_3_.dr_ref, ...), custom_call_target="tpu_custom_call" | custom-call | tf_op jit(solution)/shard_map/weight_grads/pallas_call | solution.py:1026
  813.8 2.1 pad.48.clone.down_ref
  823.7 23.4 %line_scatter.4 = f32[1024,128]{1,0:T(8,128)S(1)} custom-call(bf16[1024,512]{1,0:T(8,128)(2,1)S(1)} %add_convert_fusion.2.x_ref), custom_call_target="tpu_custom_call" | custom-call | bytes 62914560 | tf_op jit(solution)/shard_map/line_scatter/pallas_call | solution.py:855
  860.3 30.2 %input_backward.1 = (bf16[1024,2048]{1,0:T(8,128)(2,1)}, f32[8,8,2048]{2,1,0:T(8,128)S(1)}, f32[128,2048]{1,0:T(8,128)S(1)}) custom-call(bf16[1024,2048]{1,0:T(8,128)(2,1)} %copy-done, bf16[1024,512]{1,0:T(8,128)(2,1)S(1)} %copy-done.22, bf16[1024,512]{1,0:T(8,128)(2,1)S(1)} %copy-done.24, bf16[1024,512]{1,0:T(8,128)(2,1)S(1)} %copy-done.26, ...), custom_call_target="tpu_custom_call" | custom-call | tf_op jit(solution)/shard_map/input_backward/pallas_call | solution.py:989
  891.9 23.5 %reduce-scatter.13.cloned.1.call-done = bf16[256,1536]{1,0:T(8,128)(2,1)} async-done(((bf16[2048,1536]{1,0:T(8,128)(2,1)}), bf16[256,1536]{1,0:T(8,128)(2,1)}) %reduce-scatter.13.cloned.1.call-update) | async-done | bytes 786448 | tf_op jit(solution)/shard_map/reduce_scatter | solution.py:1195
  919.6 2.8 convert_element_type.171
  923.9 71.6 %line_scatter.5 = f32[1024,512]{1,0:T(8,128)S(1)} custom-call(bf16[1024,2048]{1,0:T(8,128)(2,1)} %get-tuple-element.82.x_ref), custom_call_target="tpu_custom_call" | custom-call | bytes 251658240 | tf_op jit(solution)/shard_map/line_scatter/pallas_call | solution.py:855
  996.7 3.4 dynamic-slice_add_fusion
  1002.2 18.0 %all-gather.1 = f32[608,256]{1,0:T(8,128)S(1)} all-gather(f32[152,256]{1,0:T(8,128)} %reduce-scatter.15.cloned.1.call-done), channel_id=3, replica_groups=mesh['dp'=8,'mp'=4] {'mp'}, dimensions={0}, use_global_device_ids=true | all-gather | bytes 778240 | tf_op jit(solution)/shard_map/all_gather | solution.py:1269
  (229 shorter events, 86.6 us)
Async XLA Ops:
  7.2 37.2 %copy-start.31 = (bf16[1024,512]{1,0:T(8,128)(2,1)S(1)}, bf16[1024,512]{1,0:T(8,128)(2,1)}, u32[]{:S(2)}) copy-start(bf16[1024,512]{1,0:T(8,128)(2,1)} %x_ref.1) | copy-start | bytes 3145732
  7.2 115.4 %all-gather.8.cloned.1.call-start = ((), (), s32[]{:S(2)}) async-start(), calls=%async_computation.6 | async-start | bytes 2359296 | tf_op jit(solution)/shard_map/all_gather | solution.py:1110
  25.5 128.0 %all-gather.10.cloned.1.call-start = ((), (), s32[]{:S(2)}) async-start(), calls=%async_computation.7 | async-start | bytes 7077888 | tf_op jit(solution)/shard_map/all_gather | solution.py:1115
  27.6 178.3 %all-gather.12.cloned.1.call-start = ((), (), s32[]{:S(2)}) async-start(), calls=%async_computation.8 | async-start | bytes 2359296 | tf_op jit(solution)/shard_map/all_gather | solution.py:1126
  28.3 314.2 %all-gather.14.cloned.1.call-start = ((), (), s32[]{:S(2)}) async-start(), calls=%async_computation.9 | async-start | bytes 9437184 | tf_op jit(solution)/shard_map/all_gather | solution.py:1127
  28.9 328.2 %all-gather.16.cloned.1.call-start = ((), (), s32[]{:S(2)}) async-start(), calls=%async_computation.10 | async-start | bytes 9437184 | tf_op jit(solution)/shard_map/all_gather | solution.py:1128
  29.5 712.0 %reduce-scatter.7.cloned.1.call-start = ((), (), s32[]{:S(2)}) async-start(), calls=%async_computation.11 | async-start | bytes 9437184 | tf_op jit(solution)/shard_map/reduce_scatter | solution.py:1173
  41.1 87.3 %copy-start.52 = (bf16[8,12,512]{2,1,0:T(8,128)(2,1)}, bf16[8,12,512]{2,1,0:T(8,128)(2,1)S(1)}, u32[]{:S(2)}) copy-start(bf16[8,12,512]{2,1,0:T(8,128)(2,1)S(1)} %get-tuple-element.144) | copy-start | bytes 294916
  41.1 87.3 %copy-start.54 = (bf16[8,12,512]{2,1,0:T(8,128)(2,1)}, bf16[8,12,512]{2,1,0:T(8,128)(2,1)S(1)}, u32[]{:S(2)}) copy-start(bf16[8,12,512]{2,1,0:T(8,128)(2,1)S(1)} %get-tuple-element.145) | copy-start | bytes 294916
  41.1 100.3 %copy-start.47 = (bf16[8,32,512]{2,1,0:T(8,128)(2,1)}, bf16[8,32,512]{2,1,0:T(8,128)(2,1)S(1)}, u32[]{:S(2)}) copy-start(bf16[8,32,512]{2,1,0:T(8,128)(2,1)S(1)} %slice.177) | copy-start | bytes 786436
  122.6 5.8 copy-start.1
  122.6 5.8 copy-start.51
  124.4 41.3 %copy-start.36 = (f32[8,512]{1,0:T(8,128)}, f32[8,512]{1,0:T(8,128)S(1)}, u32[]{:S(2)}) copy-start(f32[8,512]{1,0:T(8,128)S(1)} %pad.42.cols_ref) | copy-start | bytes 49156
  131.6 4.9 copy-start.59
  136.5 4.9 copy-start.45
  153.5 5.4 copy-start.9
  153.5 5.4 slice-start
  153.5 5.9 slice-start.1
  158.8 6.8 copy-start.11
  205.9 119.0 %copy-start.38 = (bf16[1024,512]{1,0:T(8,128)(2,1)}, bf16[1024,512]{1,0:T(8,128)(2,1)S(1)}, u32[]{:S(2)}) copy-start(bf16[1024,512]{1,0:T(8,128)(2,1)S(1)} %get-tuple-element.52) | copy-start | bytes 3145732
  205.9 119.0 %copy-start.2 = (bf16[1024,2048]{1,0:T(8,128)(2,1)S(1)}, bf16[1024,2048]{1,0:T(8,128)(2,1)}, u32[]{:S(2)}) copy-start(bf16[1024,2048]{1,0:T(8,128)(2,1)} %copy-done) | copy-start | bytes 12582916
  325.0 7.8 copy-start.4
  357.1 84.5 %copy-start.56 = (bf16[1024,512]{1,0:T(8,128)(2,1)S(1)}, bf16[1024,512]{1,0:T(8,128)(2,1)}, u32[]{:S(2)}) copy-start(bf16[1024,512]{1,0:T(8,128)(2,1)} %param.17) | copy-start | bytes 3145732
  532.5 315.5 %reduce-scatter.11.cloned.1.call-start = ((), (), s32[]{:S(2)}) async-start(), calls=%async_computation.13 | async-start | bytes 2359296 | tf_op jit(solution)/shard_map/reduce_scatter | solution.py:1186
  532.5 17.2 %copy-start.46 = (bf16[1024,2048]{1,0:T(8,128)(2,1)S(1)}, bf16[1024,2048]{1,0:T(8,128)(2,1)}, u32[]{:S(2)}) copy-start(bf16[1024,2048]{1,0:T(8,128)(2,1)} %add_convert_fusion.1) | copy-start | bytes 12582916
  579.1 5.3 copy-start.3
  579.1 6.5 copy-start.5
  605.6 115.6 %copy-start.7 = (bf16[1024,2048]{1,0:T(8,128)(2,1)S(1)}, bf16[1024,2048]{1,0:T(8,128)(2,1)}, u32[]{:S(2)}) copy-start(bf16[1024,2048]{1,0:T(8,128)(2,1)} %copy-done.6) | copy-start | bytes 12582916
  721.2 6.7 copy-start.39
  733.8 116.1 %reduce-scatter.9.cloned.1.call-start = ((), (), s32[]{:S(2)}) async-start(), calls=%async_computation.12 | async-start | bytes 9437184 | tf_op jit(solution)/shard_map/reduce_scatter | solution.py:1178
  734.6 6.9 copy-start.12
  734.6 6.9 copy-start.37
  734.6 180.8 %reduce-scatter.13.cloned.1.call-start = ((), (), s32[]{:S(2)}) async-start(), calls=%async_computation.14 | async-start | bytes 7077888 | tf_op jit(solution)/shard_map/reduce_scatter | solution.py:1195
  745.8 46.2 %copy-start.8 = (bf16[1024,2048]{1,0:T(8,128)(2,1)S(1)}, bf16[1024,2048]{1,0:T(8,128)(2,1)}, u32[]{:S(2)}) copy-start(bf16[1024,2048]{1,0:T(8,128)(2,1)} %get-tuple-element.127.refs_0_) | copy-start | bytes 12582916
  745.8 46.2 %copy-start.10 = (bf16[1024,2048]{1,0:T(8,128)(2,1)S(1)}, bf16[1024,2048]{1,0:T(8,128)(2,1)}, u32[]{:S(2)}) copy-start(bf16[1024,2048]{1,0:T(8,128)(2,1)} %get-tuple-element.128.refs_1_) | copy-start | bytes 12582916
  791.9 13.5 %copy-start.55 = (bf16[8,12,512]{2,1,0:T(8,128)(2,1)S(1)}, bf16[8,12,512]{2,1,0:T(8,128)(2,1)}, u32[]{:S(2)}) copy-start(bf16[8,12,512]{2,1,0:T(8,128)(2,1)} %copy-done.54) | copy-start | bytes 294916
  791.9 13.6 %copy-start.53 = (bf16[8,12,512]{2,1,0:T(8,128)(2,1)S(1)}, bf16[8,12,512]{2,1,0:T(8,128)(2,1)}, u32[]{:S(2)}) copy-start(bf16[8,12,512]{2,1,0:T(8,128)(2,1)} %copy-done.52) | copy-start | bytes 294916
  791.9 15.3 %copy-start.48 = (bf16[8,32,512]{2,1,0:T(8,128)(2,1)S(1)}, bf16[8,32,512]{2,1,0:T(8,128)(2,1)}, u32[]{:S(2)}) copy-start(bf16[8,32,512]{2,1,0:T(8,128)(2,1)} %copy-done.47) | copy-start | bytes 786436
  805.4 15.0 %copy-start.16 = (bf16[1024,512]{1,0:T(8,128)(2,1)S(1)}, bf16[1024,512]{1,0:T(8,128)(2,1)}, u32[]{:S(2)}) copy-start(bf16[1024,512]{1,0:T(8,128)(2,1)} %copy-done.15) | copy-start | bytes 3145732
  805.4 194.7 %reduce-scatter.17.cloned.1.call-start = ((), (), s32[]{:S(2)}) async-start(), calls=%async_computation.16 | async-start | bytes 516096 | tf_op jit(solution)/shard_map/reduce_scatter | solution.py:1244
  806.4 15.8 %copy-start.18 = (bf16[1024,512]{1,0:T(8,128)(2,1)S(1)}, bf16[1024,512]{1,0:T(8,128)(2,1)}, u32[]{:S(2)}) copy-start(bf16[1024,512]{1,0:T(8,128)(2,1)} %copy-done.17) | copy-start | bytes 3145732
  809.4 13.5 %copy-start.20 = (bf16[1024,512]{1,0:T(8,128)(2,1)S(1)}, bf16[1024,512]{1,0:T(8,128)(2,1)}, u32[]{:S(2)}) copy-start(bf16[1024,512]{1,0:T(8,128)(2,1)} %copy-done.19) | copy-start | bytes 3145732
  813.8 8.4 copy-start.49
  813.8 9.2 copy-start.50
  854.1 36.5 %copy-start.44 = (f32[1024,256]{1,0:T(8,128)S(1)}, f32[1024,256]{1,0:T(8,128)}, u32[]{:S(2)}) copy-start(f32[1024,256]{1,0:T(8,128)} %copy-done.43) | copy-start | bytes 3145732
  891.0 31.4 %copy-start.57 = (bf16[2048,256]{1,0:T(8,128)(2,1)S(1)}, bf16[2048,256]{1,0:T(8,128)(2,1)}, u32[]{:S(2)}) copy-start(bf16[2048,256]{1,0:T(8,128)(2,1)} %reduce-scatter.7.cloned.1.call-done) | copy-start | bytes 3145732
  915.4 86.8 %reduce-scatter.15.cloned.1.call-start = ((), (), s32[]{:S(2)}) async-start(), calls=%async_computation.15 | async-start | bytes 1400832 | tf_op jit(solution)/shard_map/reduce_scatter | solution.py:1264
  916.7 78.9 %copy-start.58 = (bf16[256,1536]{1,0:T(8,128)(2,1)S(1)}, bf16[256,1536]{1,0:T(8,128)(2,1)}, u32[]{:S(2)}) copy-start(bf16[256,1536]{1,0:T(8,128)(2,1)} %reduce-scatter.13.cloned.1.call-done) | copy-start | bytes 2359300
  (26 other events, 40.9 us)
Sparse Core Ops, SparseCore 0:
  25.6 30.9 all-gather.7
  59.0 45.5 all-gather.9
  106.5 28.1 all-gather.11
  136.5 54.3 all-gather.13
  192.6 55.9 all-gather.15
  532.6 69.6 reduce-scatter.6
  733.9 41.1 reduce-scatter.10
  778.6 71.2 reduce-scatter.8
  853.6 61.7 reduce-scatter.12
  918.3 33.9 reduce-scatter.16
  955.9 37.0 reduce-scatter.14

commit v3 on v2

--- a/solution.py
+++ b/solution.py
@@ -536,8 +536,8 @@
 
 
 LINE = "mp"
-END_LAG = 4
-MID_LAG = 2
+END_LAG = 3
+MID_LAG = 1
 
 
 def link_cost(elements):
@@ -1037,6 +1037,369 @@
     )(*lefts, *rights)
 
 
+def line_error_kernel(
+    size, chunk_rows, x_ref, base_ref, teacher_ref, weight_ref, state_ref, error_ref, got, sent, send_sem, recv_sem, out_send_sem, out_recv_sem
+):
+    line_barrier(size)
+    me = lax.axis_index(LINE)
+    flows = two_flows(size)
+    width = base_ref.shape[1]
+    chunks = x_ref.shape[0] // chunk_rows
+    is_end = (me == 0) | (me == size - 1)
+    lag = jnp.where(is_end, END_LAG, MID_LAG)
+
+    def rows_of(chunk):
+        return pl.ds(pl.multiple_of(chunk * chunk_rows, chunk_rows), chunk_rows)
+
+    def cols_of(block):
+        return pl.ds(pl.multiple_of(block * width, width), width)
+
+    def part_copy(flow, block, chunk, source):
+        place = (rows_of(chunk), cols_of(block))
+        return flow.copy(
+            source.at[place],
+            got.at[(flow.side,) + place],
+            send_sem.at[flow.side, block, chunk],
+            recv_sem.at[flow.side, block, chunk],
+        )
+
+    def error_copy(flow, block, chunk):
+        place = error_ref.at[rows_of(chunk), cols_of(block)]
+        return flow.copy(
+            place, place, out_send_sem.at[flow.side, block, chunk], out_recv_sem.at[flow.side, block, chunk]
+        )
+
+    def target_of(flow, hop):
+        block = jnp.where(flow.side == 0, size - 1 - hop, hop)
+        return block, (block - me) * flow.step > 0
+
+    def reduce_part(flow, chunk):
+        for hop in range(size - 1):
+            block, ahead = target_of(flow, hop)
+
+            @pl.when(ahead & flow.has_source)
+            def _():
+                part_copy(flow, block, chunk, x_ref).wait_recv()
+                place = (rows_of(chunk), cols_of(block))
+                total = got[(flow.side,) + place].astype(jnp.float32) + x_ref[place].astype(jnp.float32)
+                sent[(flow.side,) + place] = total.astype(sent.dtype)
+                part_copy(flow, block, chunk, sent.at[flow.side]).start()
+
+            @pl.when(ahead & jnp.logical_not(flow.has_source))
+            def _():
+                part_copy(flow, block, chunk, x_ref).start()
+
+    def finish(chunk):
+        rows = rows_of(chunk)
+        for flow in flows:
+
+            @pl.when(flow.has_source)
+            def _():
+                part_copy(flow, me, chunk, x_ref).wait_recv()
+
+        def write(others):
+            result = base_ref[rows] + (others + x_ref[rows, cols_of(me)].astype(jnp.float32))
+            state_ref[rows] = result.astype(state_ref.dtype)
+            error = weight_ref[rows, 0:1] * (result - teacher_ref[rows].astype(jnp.float32))
+            error_ref[rows, cols_of(me)] = error.astype(error_ref.dtype)
+
+        @pl.when(is_end)
+        def _():
+            write(got[flows[1].side, rows, cols_of(me)].astype(jnp.float32))
+
+        @pl.when(jnp.logical_not(is_end))
+        def _():
+            write(
+                got[0, rows, cols_of(me)].astype(jnp.float32) + got[1, rows, cols_of(me)].astype(jnp.float32)
+            )
+
+        for flow in flows:
+
+            @pl.when(flow.has_target)
+            def _():
+                error_copy(flow, me, chunk).start()
+
+    def forward(hop, chunk):
+        for flow in flows:
+            block = me - hop * flow.step
+            exists = (block >= 0) & (block < size)
+
+            @pl.when(exists)
+            def _():
+                error_copy(flow, block, chunk).wait_recv()
+
+            @pl.when(exists & flow.has_target)
+            def _():
+                error_copy(flow, block, chunk).start()
+
+    def at(chunk, action):
+        @pl.when((chunk >= 0) & (chunk < chunks))
+        def _():
+            action(chunk)
+
+    def step(turn, carry):
+        at(turn, lambda chunk: reduce_part(flows[0], chunk))
+        at(turn - lag, lambda chunk: reduce_part(flows[1], chunk))
+        at(turn - lag - 1, finish)
+        for hop in range(1, size):
+            at(turn - lag - 1 - 2 * hop, partial(forward, hop))
+        return carry
+
+    lax.fori_loop(0, chunks + END_LAG + 1 + 2 * (size - 1), step, 0)
+
+    def drain(chunk, carry):
+        for flow in flows:
+            for hop in range(size - 1):
+                block, ahead = target_of(flow, hop)
+
+                @pl.when(ahead)
+                def _():
+                    part_copy(flow, block, chunk, x_ref).wait_send()
+
+            for hop in range(size):
+                source = me - hop * flow.step
+                exists = (source >= 0) & (source < size)
+
+                @pl.when(exists & flow.has_target)
+                def _():
+                    error_copy(flow, source, chunk).wait_send()
+
+        return carry
+
+    lax.fori_loop(0, chunks, drain, 0)
+
+
+def line_error(x, base, teacher, weight, size, collective_id, chunk_rows=64):
+    rows, cols = x.shape
+    chunks = rows // chunk_rows
+    sems = pltpu.SemaphoreType.DMA((2, size, chunks))
+    return pl.pallas_call(
+        partial(line_error_kernel, size, chunk_rows),
+        out_shape=[
+            jax.ShapeDtypeStruct(base.shape, jnp.bfloat16),
+            jax.ShapeDtypeStruct(x.shape, jnp.bfloat16),
+        ],
+        in_specs=[pl.BlockSpec(memory_space=pltpu.VMEM)] * 4,
+        out_specs=[pl.BlockSpec(memory_space=pltpu.VMEM)] * 2,
+        scratch_shapes=[
+            pltpu.VMEM((2, rows, cols), x.dtype),
+            pltpu.VMEM((2, rows, cols), x.dtype),
+            sems,
+            sems,
+            sems,
+            sems,
+        ],
+        compiler_params=pltpu.CompilerParams(
+            collective_id=collective_id, has_side_effects=True, vmem_limit_bytes=48 * 1024 * 1024
+        ),
+        cost_estimate=pl.CostEstimate(flops=0, bytes_accessed=link_cost(rows * cols), transcendentals=0),
+        name="line_error",
+    )(x, base, teacher, weight)
+
+
+def output_backward_kernel(
+    seq_len, whole_ref, delta_ref, dpre_ref, weight_ref, params_ref, dres_ref, gparams_ref, carry, kept
+):
+    step = pl.program_id(0)
+    tile = pl.num_programs(0) - 1 - step
+    rows_each = dpre_ref.shape[0]
+    width = whole_ref.shape[1]
+    start = tile * rows_each
+    at_start = lax.rem(start, seq_len) == 0
+    at_end = lax.rem(start + rows_each, seq_len) == 0
+
+    @pl.when(step == 0)
+    def _():
+        gparams_ref[...] = jnp.zeros_like(gparams_ref)
+
+    @pl.when(at_end)
+    def _():
+        carry[...] = jnp.zeros_like(carry)
+
+    edge = 16
+    rows = pl.ds(pl.multiple_of(start, rows_each), rows_each)
+    edge_rows = pl.ds(pl.multiple_of(jnp.maximum(start - edge, 0), edge), edge)
+    inverse_width = 1.0 / width
+
+    def residual(place, cols):
+        return whole_ref[place, cols].astype(jnp.float32) + delta_ref[place, cols].astype(jnp.float32)
+
+    def moments(place):
+        values = residual(place, slice(0, width))
+        centre = jnp.sum(values, axis=1, keepdims=True) * inverse_width
+        values = values - centre
+        spread = jnp.sum(values * values, axis=1, keepdims=True) * inverse_width
+        return centre, lax.rsqrt(spread + norm_eps)
+
+    centre, inv = moments(rows)
+    edge_centre, edge_inv = moments(edge_rows)
+    block_cols = 256
+    row_index = iota((rows_each, block_cols), 0)
+    sum_grad = jnp.zeros((rows_each, 1), jnp.float32)
+    sum_prod = jnp.zeros((rows_each, 1), jnp.float32)
+
+    def add_param(index, cols, values):
+        total = values[0:8]
+        for place in range(8, rows_each, 8):
+            total = total + values[place : place + 8]
+        gparams_ref[index, :, cols] += total
+
+    for block in range(width // block_cols):
+        cols = slice(block * block_cols, (block + 1) * block_cols)
+        gain, bias, rate = params_ref[0:1, cols], params_ref[1:2, cols], params_ref[2:3, cols]
+        unit = (residual(rows, cols) - centre) * inv
+        normed = unit * gain + bias
+        edge_unit = (residual(edge_rows, cols) - edge_centre) * edge_inv
+        edge_normed = (edge_unit * gain + bias)[edge - 1 : edge]
+        edge_normed = jnp.where(at_start, 0.0, edge_normed)
+        before = jnp.where(row_index == 0, edge_normed, pltpu.roll(normed, 1, 0))
+        grad = dot_nt(dpre_ref[...], weight_ref[cols, :])
+        add_param(2, cols, grad * (before - normed))
+        mixed = grad * rate
+        after = jnp.where(row_index == rows_each - 1, carry[0:1, cols], pltpu.roll(mixed, rows_each - 1, 0))
+        carry[0:1, cols] = mixed[0:1]
+        dnormed = grad - mixed + after
+        add_param(0, cols, dnormed * unit)
+        add_param(1, cols, dnormed)
+        dunit = dnormed * gain
+        kept[:, cols] = dunit
+        sum_grad = sum_grad + jnp.sum(dunit, axis=1, keepdims=True)
+        sum_prod = sum_prod + jnp.sum(dunit * unit, axis=1, keepdims=True)
+    sum_grad = sum_grad * inverse_width
+    sum_prod = sum_prod * inverse_width
+    for block in range(width // block_cols):
+        cols = slice(block * block_cols, (block + 1) * block_cols)
+        unit = (residual(rows, cols) - centre) * inv
+        dres_ref[:, cols] = low(inv * (kept[:, cols] - sum_grad - unit * sum_prod))
+
+
+def output_backward(whole, delta, dpre, weight, params):
+    positions, width = whole.shape
+    rows_each = 256
+    steps = positions // rows_each
+    tile = lambda cols: pl.BlockSpec((rows_each, cols), lambda i: (steps - 1 - i, 0))
+    full = pl.BlockSpec(memory_space=pltpu.VMEM)
+    return pl.pallas_call(
+        partial(output_backward_kernel, SEQ_LEN),
+        grid=(steps,),
+        in_specs=[full, full, tile(dpre.shape[1]), full, full],
+        out_specs=[tile(width), pl.BlockSpec((8, 8, width), lambda i: (0, 0, 0))],
+        out_shape=[
+            jax.ShapeDtypeStruct((positions, width), jnp.bfloat16),
+            jax.ShapeDtypeStruct((8, 8, width), jnp.float32),
+        ],
+        scratch_shapes=[pltpu.VMEM((8, width), jnp.float32), pltpu.VMEM((rows_each, width), jnp.float32)],
+        compiler_params=pltpu.CompilerParams(
+            dimension_semantics=("arbitrary",), vmem_limit_bytes=48 * 1024 * 1024
+        ),
+        name="output_backward",
+    )(whole, delta, dpre, weight, params)
+
+
+def input_forward_kernel(
+    seq_len,
+    tanh_end,
+    plain_end,
+    whole_ref,
+    three_ref,
+    down_ref,
+    ups_ref,
+    params_ref,
+    r_ref,
+    k_ref,
+    v_ref,
+    dw_ref,
+    da_ref,
+    gate_ref,
+    mr_ref,
+    mk_ref,
+    mv_ref,
+    inner_ref,
+):
+    tile = pl.program_id(0)
+    rows_each = r_ref.shape[0]
+    part = r_ref.shape[1]
+    width = whole_ref.shape[1]
+    start = tile * rows_each
+    at_start = lax.rem(start, seq_len) == 0
+    edge = 16
+    rows = pl.ds(pl.multiple_of(start, rows_each), rows_each)
+    edge_rows = pl.ds(pl.multiple_of(jnp.maximum(start - edge, 0), edge), edge)
+    inverse_width = 1.0 / width
+
+    def moments(place):
+        values = whole_ref[place, :].astype(jnp.float32)
+        centre = jnp.sum(values, axis=1, keepdims=True) * inverse_width
+        values = values - centre
+        spread = jnp.sum(values * values, axis=1, keepdims=True) * inverse_width
+        return centre, lax.rsqrt(spread + norm_eps)
+
+    centre, inv = moments(rows)
+    edge_centre, edge_inv = moments(edge_rows)
+    block_cols = 256
+    row_index = iota((rows_each, block_cols), 0)
+    lane = iota((rows_each, down_ref.shape[1]), 1)
+    r = k = v = inner_w = inner_a = inner_g = 0.0
+    for block in range(width // block_cols):
+        cols = slice(block * block_cols, (block + 1) * block_cols)
+        gain, bias = params_ref[0:1, cols], params_ref[1:2, cols]
+        normed = (whole_ref[rows, cols].astype(jnp.float32) - centre) * inv * gain + bias
+        edge_unit = (whole_ref[edge_rows, cols].astype(jnp.float32) - edge_centre) * edge_inv
+        edge_normed = (edge_unit * gain + bias)[edge - 1 : edge]
+        edge_normed = jnp.where(at_start, 0.0, edge_normed)
+        before = jnp.where(row_index == 0, edge_normed, pltpu.roll(normed, 1, 0))
+        shift = before - normed
+
+        def mix(index):
+            return low(normed + shift * params_ref[index : index + 1, cols])
+
+        mix_r, mix_k, mix_v = mix(2), mix(4), mix(5)
+        mr_ref[:, cols], mk_ref[:, cols], mv_ref[:, cols] = mix_r, mix_k, mix_v
+        weights = three_ref[cols, :]
+        r = r + dot_nn(mix_r, weights[:, :part])
+        k = k + dot_nn(mix_k, weights[:, part : 2 * part])
+        v = v + dot_nn(mix_v, weights[:, 2 * part :])
+        down = down_ref[cols, :]
+        inner_w = inner_w + dot_nn(mix(3), down)
+        inner_a = inner_a + dot_nn(mix(6), down)
+        inner_g = inner_g + dot_nn(mix(7), down)
+    r_ref[...], k_ref[...], v_ref[...] = r, k, v
+    inner = jnp.where(
+        lane < tanh_end,
+        jnp.tanh(inner_w),
+        jnp.where(lane < plain_end, inner_a, jax.nn.sigmoid(inner_g)),
+    )
+    inner_ref[...] = inner
+    inner_low = low(inner)
+    zero = jnp.zeros_like(inner_low)
+    ups = ups_ref[...]
+    dw_ref[...] = dot_nn(jnp.where(lane < tanh_end, inner_low, zero), ups)
+    da_ref[...] = dot_nn(jnp.where((lane >= tanh_end) & (lane < plain_end), inner_low, zero), ups)
+    gate_ref[...] = dot_nn(jnp.where(lane >= plain_end, inner_low, zero), ups)
+
+
+def input_forward(whole, three, down, ups, ends, params):
+    positions, width = whole.shape
+    part = ups.shape[1]
+    rows_each = 256
+    tile = lambda cols: pl.BlockSpec((rows_each, cols), lambda i: (i, 0))
+    full = pl.BlockSpec(memory_space=pltpu.VMEM)
+    shape = jax.ShapeDtypeStruct
+    return pl.pallas_call(
+        partial(input_forward_kernel, SEQ_LEN, *ends),
+        grid=(positions // rows_each,),
+        in_specs=[full] * 5,
+        out_specs=[tile(part)] * 6 + [tile(width)] * 3 + [tile(down.shape[1])],
+        out_shape=[shape((positions, part), jnp.float32)] * 6
+        + [shape((positions, width), jnp.bfloat16)] * 3
+        + [shape((positions, down.shape[1]), jnp.float32)],
+        compiler_params=pltpu.CompilerParams(
+            dimension_semantics=("arbitrary",), vmem_limit_bytes=52 * 1024 * 1024
+        ),
+        name="input_forward",
+    )(whole, three, down, ups, params)
+
+
 def matmul(left_op, right_op):
     return jnp.dot(left_op, right_op, preferred_element_type=jnp.float32)
 
@@ -1060,12 +1423,6 @@
     grid_view = values.reshape(values.shape[0] // SEQ_LEN, SEQ_LEN, values.shape[1])
     earlier = jnp.concatenate([jnp.zeros_like(grid_view[:, :1]), grid_view[:, :-1]], axis=1)
     return earlier.reshape(values.shape)
-
-
-def section_in(hidden, scale_in, offset, mix_rates):
-    standardized_source = layer_norm(hidden, scale_in, offset)
-    shift_diff = shifted(standardized_source) - standardized_source
-    return tuple((standardized_source + shift_diff * mix_rates[:, column] for column in range(6)))
 
 
 def section_out(residual, scale_in, offset, mix_rate):
@@ -1102,7 +1459,6 @@
     loss_scale = position_count * lax.axis_size("dp") / jnp.sum(lengths).astype(jnp.float32)
     line_size = lax.axis_size("mp")
     whole_low = line_gather(hidden, line_size, 1)
-    whole = whole_low.astype(jnp.float32)
     low_rank = (decay_down.shape[1], rate_down.shape[1], gate_down.shape[1])
     narrow = jnp.concatenate([decay_down, rate_down, gate_down, feature_params], axis=1)
     narrow = jnp.pad(narrow, ((0, 0), (0, -narrow.shape[1] % 128)))
@@ -1115,9 +1471,6 @@
     three = lax.all_gather(
         jnp.concatenate([receptance, key_proj, value_proj], axis=1), "dp", axis=0, tiled=True
     )
-    recept_w = three[:, :part_width]
-    key_w = three[:, part_width : 2 * part_width]
-    value_w = three[:, 2 * part_width :]
     up_rows = (decay_up.shape[0], rate_up.shape[0], gate_up.shape[0])
     ups = lax.all_gather(jnp.concatenate([decay_up, rate_up, gate_up], axis=0), "dp", axis=0)
     decay_up_w = ups[:, : up_rows[0]].reshape(-1, part_width)
@@ -1127,24 +1480,31 @@
     ffn_key_w = lax.all_gather(ffn_key, "dp", axis=0, tiled=True)
     ffn_value_w = lax.all_gather(ffn_value, "dp", axis=1, tiled=True)
     params = params_low.astype(jnp.float32)
-    model_width = whole.shape[1]
-    mixed = section_in(whole, params[:, 0], params[:, 1], params[:, 2:8])
-    mix_r, mix_w, mix_k, mix_v, mix_a, mix_g = tuple(
-        (member.astype(jnp.bfloat16) for member in mixed)
-    )
-    acceptance_matrix = matmul(mix_r, recept_w)
-    keys_in = matmul(mix_k, key_w)
-    payload_source = matmul(mix_v, value_w)
-    decay_hid = jnp.tanh(matmul(mix_w, decay_down_w))
-    decay_low = decay_hid.astype(jnp.bfloat16)
-    rate_low = matmul(mix_a, rate_down_w).astype(jnp.bfloat16)
-    gate_hid = jax.nn.sigmoid(matmul(mix_g, gate_down_w))
-    gate_low = gate_hid.astype(jnp.bfloat16)
-    decay_in = matmul(decay_low, decay_up_w)
-    rate_in = matmul(rate_low, rate_up_w)
-    sigmoid_source = matmul(gate_low, gate_up_w)
-    columns = lax.dynamic_slice_in_dim(params, col_start, part_width, 0)[:, 8:15].T
-    columns = jnp.pad(columns, ((0, 1), (0, 0)))
+    model_width = whole_low.shape[1]
+    params_rows = jnp.pad(params.T, ((0, -params.shape[1] % 8), (0, 0)))
+    up_all = jnp.concatenate([decay_up_w, rate_up_w, gate_up_w], axis=0)
+    up_all = jnp.pad(up_all, ((0, narrow_w.shape[1] - up_all.shape[0]), (0, 0)))
+    (
+        acceptance_matrix,
+        keys_in,
+        payload_source,
+        decay_in,
+        rate_in,
+        sigmoid_source,
+        mix_r,
+        mix_k,
+        mix_v,
+        inner_hid,
+    ) = input_forward(
+        whole_low, three, narrow_w, up_all, (low_rank[0], low_rank[0] + low_rank[1]), params_rows
+    )
+    inner_low = inner_hid.astype(jnp.bfloat16)
+    decay_hid = inner_hid[:, : low_rank[0]]
+    gate_hid = inner_hid[:, low_rank[0] + low_rank[1] : sum(low_rank)]
+    decay_low = inner_low[:, : low_rank[0]]
+    rate_low = inner_low[:, low_rank[0] : low_rank[0] + low_rank[1]]
+    gate_low = inner_low[:, low_rank[0] + low_rank[1] : sum(low_rank)]
+    columns = lax.dynamic_slice(params_rows, (8, col_start), (8, part_width))
     mixer_args = (
         own_lengths,
         acceptance_matrix,
@@ -1156,18 +1516,17 @@
         columns,
     )
     gated_low, *kept = run_mixer_forward(*mixer_args)
-    residual = whole + line_sum(matmul(gated_low, output_w).astype(jnp.bfloat16), line_size, 2).astype(
-        jnp.float32
-    )
-    ffn_in, back_out = jax.vjp(section_out, residual, params[:, 15], params[:, 16], params[:, 17])
+    delta_low = line_sum(matmul(gated_low, output_w).astype(jnp.bfloat16), line_size, 2)
+    residual = whole_low.astype(jnp.float32) + delta_low.astype(jnp.float32)
+    ffn_in = section_out(residual, params[:, 15], params[:, 16], params[:, 17])
     ffn_low = ffn_in.astype(jnp.bfloat16)
     pre_act = matmul(ffn_low, ffn_key_w)
     active = jnp.maximum(pre_act, 0.0)
     squared = (active * active).astype(jnp.bfloat16)
-    ffn_part = line_scatter(matmul(squared, ffn_value_w).astype(jnp.bfloat16), line_size, 3)
-    result = lax.dynamic_slice_in_dim(residual, col_start, part_width, 1) + ffn_part
-    grad_result = loss_scale * valid[:, None] * (result - teacher.astype(jnp.float32))
-    grad_low = line_gather(grad_result.astype(jnp.bfloat16), line_size, 4)
+    ffn_part = matmul(squared, ffn_value_w).astype(jnp.bfloat16)
+    own_residual = lax.dynamic_slice_in_dim(residual, col_start, part_width, 1)
+    error_scale = jnp.broadcast_to((loss_scale * valid)[:, None], (position_count, 128))
+    out_state, grad_low = line_error(ffn_part, own_residual, teacher, error_scale, line_size, 3)
     grad_ffn_value = contract_rows(squared, grad_low).astype(jnp.bfloat16)
     grad_low, grad_ffn_value = lax.optimization_barrier((grad_low, grad_ffn_value))
     grad_ffn_value = lax.psum_scatter(grad_ffn_value, "dp", scatter_dimension=1, tiled=True)
@@ -1176,16 +1535,18 @@
     grad_ffn_key = contract_rows(ffn_low, grad_pre).astype(jnp.bfloat16)
     grad_pre, grad_ffn_key = lax.optimization_barrier((grad_pre, grad_ffn_key))
     grad_ffn_key = lax.psum_scatter(grad_ffn_key, "dp", scatter_dimension=0, tiled=True)
-    d_resid_part, d_scale_two, d_offset_two, d_mix_two = back_out(against(grad_pre, ffn_key_w))
-    d_residual = grad_low.astype(jnp.float32) + line_sum(
-        d_resid_part.astype(jnp.bfloat16), line_size, 5
-    ).astype(jnp.float32)
+    d_resid_part, d_params_out = output_backward(
+        whole_low, delta_low, grad_pre, ffn_key_w, params_rows[15:23]
+    )
+    d_residual = grad_low.astype(jnp.float32) + line_sum(d_resid_part, line_size, 5).astype(jnp.float32)
     d_low = d_residual.astype(jnp.bfloat16)
     grad_output_proj = contract_rows(gated_low, d_low).astype(jnp.bfloat16)
     d_low, grad_output_proj = lax.optimization_barrier((d_low, grad_output_proj))
     grad_output_proj = lax.psum_scatter(grad_output_proj, "dp", scatter_dimension=1, tiled=True)
     d_gated = against(d_low, output_w)
-    d_gated, grad_ffn_value = lax.optimization_barrier((d_gated, grad_ffn_value))
+    d_gated, grad_ffn_value, grad_ffn_key = lax.optimization_barrier(
+        (d_gated, grad_ffn_value, grad_ffn_key)
+    )
     d_recept, d_keys, d_values, d_decay, d_rate, d_gate, d_columns = run_mixer_backward(
         *mixer_args, *kept, d_gated
     )
@@ -1217,9 +1578,7 @@
         + against(d_gate, spread_rows(gate_up_w, shares[2], starts[2]))
     ).astype(jnp.bfloat16)
     d_own = line_scatter(d_inner, line_size, 6)
-    d_own, grad_ffn_key, grad_output_proj = lax.optimization_barrier(
-        (d_own, grad_ffn_key, grad_output_proj)
-    )
+    d_own, grad_output_proj = lax.optimization_barrier((d_own, grad_output_proj))
     slope = own_group(
         (
             1.0 - decay_hid * decay_hid,
@@ -1229,7 +1588,6 @@
     )
     d_own_pre = (d_own * slope).astype(jnp.bfloat16)
     down_own = own_group((decay_down_w, rate_down_w, gate_down_w))
-    params_rows = jnp.pad(params.T, ((0, -params.shape[1] % 8), (0, 0)))
     d_in_part, d_params_in, d_down = input_backward(
         whole_low, d_recept, d_keys, d_values, d_own_pre, starts[1:], three, down_own, params_rows
     )
@@ -1250,9 +1608,7 @@
         [
             jnp.sum(d_params_in, axis=1),
             core_grads,
-            d_scale_two[None],
-            d_offset_two[None],
-            d_mix_two[None],
+            jnp.sum(d_params_out, axis=1)[:3],
         ],
         axis=0,
     )
@@ -1266,15 +1622,19 @@
         d_in_part, line_size, 7
     )
     row_block = decay_down.shape[0]
-    narrow_grads = lax.all_gather(narrow_grads, "mp", axis=0)
+    narrow_grads = jnp.pad(narrow_grads, ((0, 0), (0, -narrow_grads.shape[1] % 128)))
+    narrow_rows = narrow_grads.shape[0]
+    narrow_grads = line_gather(narrow_grads, line_size, 4, chunk_rows=narrow_rows)
+    narrow_grads = narrow_grads.reshape(narrow_rows, line_size, -1)
     narrow_grads = lax.dynamic_slice_in_dim(narrow_grads, mp_index * row_block, row_block, 2)
 
     def down_grad(start, share):
-        return narrow_grads[:, start : start + share].reshape(line_size * share, row_block).T
-
-    grad_params = jnp.sum(narrow_grads[:, own_rank : own_rank + param_count], axis=0).T
+        taken = narrow_grads[start : start + share].transpose(1, 0, 2)
+        return taken.reshape(line_size * share, row_block).T
+
+    grad_params = jnp.sum(narrow_grads[own_rank : own_rank + param_count], axis=1).T
     return (
-        result.astype(jnp.bfloat16),
+        out_state,
         grad_hidden,
         grad_params,
         down_grad(starts[0], shares[0]),

time: 1040 us -> 934 us (0.90)
  other arithmetic: 95.1 us -> 47 us
  matrix products: 136 us -> 94.8 us
  waiting for transfers between devices: 28 us -> 1.92 us
  Pallas kernels: 649 us -> 675 us
  blocking collectives: 44.4 us -> 26.7 us
    pallas_call x0 -> x3, Pallas kernels: none -> 170 us  [the longest x1 118 us: line_error(): pl.pallas_call(partial(line_error_kernel, size, chunk_rows), out_shape=[j...]
    pallas_call x3 -> x2, Pallas kernels: 164 us -> 86.7 us  [line_scatter(): pl.pallas_call(partial(line_scatter_kernel, size, chunk_rows), out_shape=...]
    pallas_call x2, Pallas kernels: 143 us -> 86.4 us  [line_gather(): pl.pallas_call(partial(line_gather_kernel, size, chunk_rows), out_shape=j...]
    dot_general x12 -> x3, matrix products: 62.4 us -> 36.2 us  [matmul(): return jnp.dot(left_op, right_op, preferred_element_type=jnp.float32)]
    reduce_scatter x1, waiting for transfers between devices: 23.5 us -> 0.01 us  [body(): lax.psum_scatter(grad_three, 'dp', scatter_dimension=0, tiled=True)]
    reduce_sum x5 -> x2, other arithmetic: 22.4 us -> 1.88 us  [the longest x1 1.17 us: body(): jnp.sum(d_params_out, axis=1)[:3]]
    convert_element_type x3 -> x1, other arithmetic: 18.2 us -> 0.13 us  [body(): inner_low = inner_hid.astype(jnp.bfloat16)]
    all_gather x1 -> x0, blocking collectives: 18 us -> none  [body(): narrow_grads = lax.all_gather(narrow_grads, 'mp', axis=0)]
  transfers between devices with their start and end apart: 11 -> 11, of which waited for: 2 -> 0; matrix products, arithmetic and copies ran while one was open for 21% -> 14% of each run, Pallas kernels for 49% -> 59%
where the time goes in v3:
time: 934 us; the launch traced here: 924 us
  Pallas kernels  675 us (72%)
  matrix products  94.8 us (10%)
  local copies, waits for them, and re-layouts  61.6 us (7%)
  other arithmetic  47 us (5%)
  blocking collectives  26.7 us (3%)
  between operations  15.9 us (2%)
    pallas_call x2, Pallas kernels, line_sum(): pl.pallas_call(partial(line_sum_kernel, size, chunk_rows), out_shape=jax....  214 us
    pallas_call x1, Pallas kernels, line_error(): pl.pallas_call(partial(line_error_kernel, size, chunk_rows), out_shape=[j...  118 us
    pallas_call x2, Pallas kernels, line_scatter(): pl.pallas_call(partial(line_scatter_kernel, size, chunk_rows), out_shape=...  86.7 us
    pallas_call x2, Pallas kernels, line_gather(): pl.pallas_call(partial(line_gather_kernel, size, chunk_rows), out_shape=j...  86.4 us
    pallas_call x1, Pallas kernels, run_mixer_backward(): pl.pallas_call(partial(mixer_backward, steps_per_seq), grid=(steps,), in_...  43.1 us
    unnamed x144, local copies, waits for them, and re-layouts  38.6 us
    dot_general x3, matrix products, matmul(): return jnp.dot(left_op, right_op, preferred_element_type=jnp.float32)  36.2 us
    pallas_call x1, Pallas kernels, run_mixer_forward(): pl.pallas_call(partial(mixer_forward, steps_per_seq), grid=(steps,), in_s...  35.5 us
  transfers between devices with their start and end apart: 11, of which 0 were waited for; matrix products, arithmetic and copies ran while one was open for 14% of the time, Pallas kernels for 59%

profile of v3, /device:TPU:0, one launch (start us, length us, event | category | flops | bytes accessed | tf_op | source)
XLA Modules:
  0.0 923.6 jit_solution(6903548063757124872)
XLA Ops:
  9.0 15.6 %all_gather.25 = bf16[256,512]{1,0:T(8,128)(2,1)S(1)} all-gather(bf16[64,512]{1,0:T(8,128)(2,1)S(1)} %fusion.19), channel_id=1, replica_groups=mesh['dp'=8,'mp'=4] {'mp'}, dimensions={0}, use_global_device_ids=true | all-gather | bytes 327680 | tf_op jit(solution)/shard_map/all_gather | solution.py:1465
  25.6 2.0 pad_maximum_fusion
  31.5 11.1 %all-gather = bf16[448,512]{1,0:T(8,128)(2,1)S(1)} all-gather(bf16[56,512]{1,0:T(8,128)(2,1)S(1)} %pad_maximum_fusion.4), channel_id=2, replica_groups=mesh['dp'=8,'mp'=4] {'dp'}, dimensions={0}, use_global_device_ids=true | all-gather | bytes 516096 | tf_op jit(solution)/shard_map/all_gather | solution.py:1475
  42.8 71.0 %line_gather.2.whole_ref = bf16[1024,2048]{1,0:T(8,128)(2,1)S(1)} custom-call(bf16[1024,512]{1,0:T(8,128)(2,1)S(1)} %copy-done.24), custom_call_target="tpu_custom_call" | custom-call | bytes 251658240 | tf_op jit(solution)/shard_map/line_gather/pallas_call | solution.py:748
  113.8 2.0 copy-done
  117.5 4.0 copy.50.down_ref
  121.6 27.0 %input_forward.1 = (f32[1024,512]{1,0:T(8,128)}, f32[1024,512]{1,0:T(8,128)}, f32[1024,512]{1,0:T(8,128)}, f32[1024,512]{1,0:T(8,128)}, f32[1024,512]{1,0:T(8,12...) custom-call(bf16[1024,2048]{1,0:T(8,128)(2,1)} %copy-done, ...), custom_call_target="tpu_custom_call" | custom-call | tf_op jit(solution)/shard_map/input_forward/pallas_call | solution.py:1388
  148.6 1.6 copy-done.3
  150.2 1.6 copy-done.5
  151.7 35.5 %mixer_forward.1 = (bf16[1024,512]{1,0:T(8,128)(2,1)S(1)}, f32[1024,512]{1,0:T(8,128)S(1)}, bf16[1024,512]{1,0:T(8,128)(2,1)S(1)}, bf16[1024,512]{1,0:T(8,128)(2...) custom-call(s32[1]{0:T(128)} %dynamic_slice.33.length_ref, ...), custom_call_target="tpu_custom_call" | custom-call | tf_op jit(solution)/shard_map/mixer_forward/pallas_call | solution.py:477
  192.9 6.3 convolution_convert_fusion.3.x_ref
  199.2 109.6 %line_sum.2.delta_ref = bf16[1024,2048]{1,0:T(8,128)(2,1)S(1)} custom-call(bf16[1024,2048]{1,0:T(8,128)(2,1)} %convolution_convert_fusion.3.x_ref), custom_call_target="tpu_custom_call" | custom-call | bytes 335544320 | tf_op jit(solution)/shard_map/line_sum/pallas_call | solution.py:664
  308.8 4.6 convert_add_fusion.1
  313.4 1.8 constant_dynamic-slice_fusion.6.base_ref
  315.1 2.2 multiply_reduce_fusion
  317.3 2.3 fusion.3
  319.6 6.5 fusion.2
  326.2 14.6 %fusion.29 = f32[1024,2048]{1,0:T(8,128)} fusion(bf16[1024,2048]{1,0:T(8,128)(2,1)} %fusion.2, bf16[2048,2048]{1,0:T(8,128)(2,1)} %all-gather.13.cloned.1.call-done.weight_ref), kind=kOutput, calls=%fused_computation.81 | convolution fusion | flops 8589934592 | bytes 20971520 | tf_op jit(solution)/shard_map/dot_general | solution.py:1404
  340.7 15.3 %convolution_convert_fusion.2.x_ref = bf16[1024,2048]{1,0:T(8,128)(2,1)} fusion(bf16[2048,2048]{1,0:T(8,128)(2,1)} %all-gather.15.cloned.1.call-done, f32[1024,2048]{1,0:T(8,128)} %fusion.29), kind=kOutput, calls=%fused_computation.13 | convolution fusion | flops 8598323200 | bytes 20971520 | tf_op jit(solution)/shard_map/dot_general | solution.py:1404
  356.3 117.6 %line_error.1 = (bf16[1024,512]{1,0:T(8,128)(2,1)S(1)}, bf16[1024,2048]{1,0:T(8,128)(2,1)}) custom-call(bf16[1024,2048]{1,0:T(8,128)(2,1)} %convolution_convert_fusion.2.x_ref, f32[1024,512]{1,0:T(8,128)S(1)} %constant_dynamic-slice_fusion.6.base_ref, bf16[1024,512]{1,0:T(8,128)(2,1)S(1)} %copy-done.25, f32[1024,128]{1,0:T(8,128)S(1)} %broadcast_in_dim.4.weight_ref), custom_call_target="tpu_custom_call" | custom-call | bytes 335544320 | tf_op jit(solution)/shard_map/line_error/pallas_call | solution.py:1176
  474.8 13.4 %convolution_convert_fusion.1 = bf16[2048,2048]{1,0:T(8,128)(2,1)} fusion(bf16[1024,2048]{1,0:T(8,128)(2,1)} %get-tuple-element.75, f32[1024,2048]{1,0:T(8,128)S(1)} %copy-done.67), kind=kOutput, calls=%fused_computation.11 | convolution fusion | flops 8600420352 | bytes 20971520 | tf_op jit(solution)/shard_map/tk,tn->kn/dot_general | solution.py:1408
  488.3 15.2 %multiply_convert_fusion.dpre_ref = bf16[1024,2048]{1,0:T(8,128)(2,1)S(1)} fusion(f32[1024,2048]{1,0:T(8,128)} %fusion.29, bf16[1024,2048]{1,0:T(8,128)(2,1)} %get-tuple-element.75, bf16[2048,2048]{1,0:T(8,128)(2,1)} %all-gather.15.cloned.1.call-done), kind=kOutput, calls=%fused_computation.5 | convolution fusion | flops 8598323200 | bytes 25165824 | tf_op jit(solution)/shard_map/tn,kn->tk/dot_general | solution.py:1412
  503.5 2.1 copy-done.47
  505.6 11.4 %convolution_convert_fusion = bf16[2048,2048]{1,0:T(8,128)(2,1)} fusion(bf16[1024,2048]{1,0:T(8,128)(2,1)S(1)} %copy-done.46, bf16[1024,2048]{1,0:T(8,128)(2,1)S(1)} %multiply_convert_fusion.dpre_ref), kind=kOutput, calls=%fused_computation.10 | convolution fusion | flops 8594128896 | bytes 16777216 | tf_op jit(solution)/shard_map/tk,tn->kn/dot_general | solution.py:1408
  517.1 26.0 %output_backward.1 = (bf16[1024,2048]{1,0:T(8,128)(2,1)S(1)}, f32[8,8,2048]{2,1,0:T(8,128)S(1)}) custom-call(bf16[1024,2048]{1,0:T(8,128)(2,1)} %copy-done, bf16[1024,2048]{1,0:T(8,128)(2,1)} %copy-done.2, bf16[1024,2048]{1,0:T(8,128)(2,1)} %copy-done.47, bf16[2048,2048]{1,0:T(8,128)(2,1)} %all-gather.13.cloned.1.call-done.weight_ref, ...), custom_call_target="tpu_custom_call" | custom-call | tf_op jit(solution)/shard_map/output_backward/pallas_call | solution.py:1282
  543.0 2.0 copy-done.9
  545.8 104.5 %line_sum.3 = bf16[1024,2048]{1,0:T(8,128)(2,1)S(1)} custom-call(bf16[1024,2048]{1,0:T(8,128)(2,1)} %copy-done.9), custom_call_target="tpu_custom_call" | custom-call | bytes 335544320 | tf_op jit(solution)/shard_map/line_sum/pallas_call | solution.py:664
  650.4 6.8 convert_add_fusion
  657.2 5.9 convolution_convert_fusion.4
  663.1 6.7 fusion.30.dz_ref
  669.8 1.7 copy-done.6
  675.3 43.1 %mixer_backward.1 = (bf16[1024,512]{1,0:T(8,128)(2,1)S(1)}, bf16[1024,512]{1,0:T(8,128)(2,1)S(1)}, bf16[1024,512]{1,0:T(8,128)(2,1)S(1)}, bf16[1024,512]{1,0:T(8...) custom-call(s32[1]{0:T(128)} %dynamic_slice.33.length_ref, ...), custom_call_target="tpu_custom_call" | custom-call | tf_op jit(solution)/shard_map/mixer_backward/pallas_call | solution.py:514
  720.4 2.2 copy-done.11
  722.6 10.2 %weight_grads.1 = bf16[2048,1536]{1,0:T(8,128)(2,1)} custom-call(bf16[1024,2048]{1,0:T(8,128)(2,1)S(1)} %copy-done.10, bf16[1024,2048]{1,0:T(8,128)(2,1)S(1)} %copy-done.11, bf16[1024,2048]{1,0:T(8,128)(2,1)} %get-tuple-element.96.refs_2_, bf16[1024,512]{1,0:T(8,128)(2,1)S(1)} %get-tuple-element.88.refs_3_.dr_ref, ...), custom_call_target="tpu_custom_call" | custom-call | tf_op jit(solution)/shard_map/weight_grads/pallas_call | solution.py:1026
  735.7 1.7 reshape_reshape.9
  737.5 1.6 reshape_reshape.10
  739.0 1.7 pad.41
  740.8 1.7 pad.40
  745.5 2.1 copy.62
  747.6 2.2 pad.44.clone.down_ref
  756.5 2.1 add_convert_fusion.x_ref
  758.7 22.9 %line_scatter.2 = f32[1024,128]{1,0:T(8,128)S(1)} custom-call(bf16[1024,512]{1,0:T(8,128)(2,1)S(1)} %add_convert_fusion.x_ref), custom_call_target="tpu_custom_call" | custom-call | bytes 62914560 | tf_op jit(solution)/shard_map/line_scatter/pallas_call | solution.py:855
  784.9 28.9 %input_backward.1 = (bf16[1024,2048]{1,0:T(8,128)(2,1)}, f32[8,8,2048]{2,1,0:T(8,128)S(1)}, f32[128,2048]{1,0:T(8,128)S(1)}) custom-call(bf16[1024,2048]{1,0:T(8,128)(2,1)} %copy-done, bf16[1024,512]{1,0:T(8,128)(2,1)S(1)} %copy-done.13, bf16[1024,512]{1,0:T(8,128)(2,1)S(1)} %copy-done.15, bf16[1024,512]{1,0:T(8,128)(2,1)S(1)} %copy-done.17, ...), custom_call_target="tpu_custom_call" | custom-call | tf_op jit(solution)/shard_map/input_backward/pallas_call | solution.py:989
  819.0 2.4 select_maximum_fusion
  822.3 1.6 convert_element_type.123
  825.3 63.9 %line_scatter.3 = f32[1024,512]{1,0:T(8,128)S(1)} custom-call(bf16[1024,2048]{1,0:T(8,128)(2,1)} %get-tuple-element.110.x_ref), custom_call_target="tpu_custom_call" | custom-call | bytes 251658240 | tf_op jit(solution)/shard_map/line_scatter/pallas_call | solution.py:855
  890.4 3.5 dynamic-slice_add_fusion
  896.9 15.3 %line_gather.3 = f32[152,1024]{1,0:T(8,128)S(1)} custom-call(f32[152,256]{1,0:T(8,128)S(1)} %copy-done.39), custom_call_target="tpu_custom_call" | custom-call | bytes 18677760 | tf_op jit(solution)/shard_map/line_gather/pallas_call | solution.py:748
  (229 shorter events, 53.2 us)
Async XLA Ops:
  7.2 22.4 %copy-start.66 = (s32[8]{0:T(128)S(1)}, s32[8]{0:T(128)}, u32[]{:S(2)}) copy-start(s32[8]{0:T(128)} %param.18) | copy-start | bytes 100
  7.2 24.3 %copy-start.63 = (bf16[32,512]{1,0:T(8,128)(2,1)S(1)}, bf16[32,512]{1,0:T(8,128)(2,1)}, u32[]{:S(2)}) copy-start(bf16[32,512]{1,0:T(8,128)(2,1)} %param.25) | copy-start | bytes 98308
  7.2 24.3 %copy-start.64 = (bf16[12,512]{1,0:T(8,128)(2,1)S(1)}, bf16[12,512]{1,0:T(8,128)(2,1)}, u32[]{:S(2)}) copy-start(bf16[12,512]{1,0:T(8,128)(2,1)} %param.24) | copy-start | bytes 36868
  7.2 24.3 %copy-start.65 = (bf16[12,512]{1,0:T(8,128)(2,1)S(1)}, bf16[12,512]{1,0:T(8,128)(2,1)}, u32[]{:S(2)}) copy-start(bf16[12,512]{1,0:T(8,128)(2,1)} %param.23) | copy-start | bytes 36868
  7.2 35.5 %copy-start.24 = (bf16[1024,512]{1,0:T(8,128)(2,1)S(1)}, bf16[1024,512]{1,0:T(8,128)(2,1)}, u32[]{:S(2)}) copy-start(bf16[1024,512]{1,0:T(8,128)(2,1)} %x_ref.1) | copy-start | bytes 3145732
  7.2 109.3 %all-gather.9.cloned.1.call-start = ((), (), s32[]{:S(2)}) async-start(), calls=%async_computation.7 | async-start | bytes 2359296 | tf_op jit(solution)/shard_map/all_gather | solution.py:1466
  25.5 96.1 %all-gather.7.cloned.1.call-start = ((), (), s32[]{:S(2)}) async-start(), calls=%async_computation.6 | async-start | bytes 7077888 | tf_op jit(solution)/shard_map/all_gather | solution.py:1471
  27.6 165.2 %all-gather.11.cloned.1.call-start = ((), (), s32[]{:S(2)}) async-start(), calls=%async_computation.8 | async-start | bytes 2359296 | tf_op jit(solution)/shard_map/all_gather | solution.py:1479
  28.4 297.8 %all-gather.13.cloned.1.call-start = ((), (), s32[]{:S(2)}) async-start(), calls=%async_computation.9 | async-start | bytes 9437184 | tf_op jit(solution)/shard_map/all_gather | solution.py:1480
  29.0 311.8 %all-gather.15.cloned.1.call-start = ((), (), s32[]{:S(2)}) async-start(), calls=%async_computation.10 | async-start | bytes 9437184 | tf_op jit(solution)/shard_map/all_gather | solution.py:1481
  29.5 640.2 %reduce-scatter.7.cloned.1.call-start = ((), (), s32[]{:S(2)}) async-start(), calls=%async_computation.11 | async-start | bytes 9437184 | tf_op jit(solution)/shard_map/reduce_scatter | solution.py:1532
  42.6 78.9 %copy-start.50 = (bf16[8,32,512]{2,1,0:T(8,128)(2,1)}, bf16[8,32,512]{2,1,0:T(8,128)(2,1)S(1)}, u32[]{:S(2)}) copy-start(bf16[8,32,512]{2,1,0:T(8,128)(2,1)S(1)} %slice.130) | copy-start | bytes 786436
  42.7 78.8 %copy-start.55 = (bf16[8,12,512]{2,1,0:T(8,128)(2,1)}, bf16[8,12,512]{2,1,0:T(8,128)(2,1)S(1)}, u32[]{:S(2)}) copy-start(bf16[8,12,512]{2,1,0:T(8,128)(2,1)S(1)} %get-tuple-element.161) | copy-start | bytes 294916
  42.7 78.8 %copy-start.56 = (bf16[8,12,512]{2,1,0:T(8,128)(2,1)}, bf16[8,12,512]{2,1,0:T(8,128)(2,1)S(1)}, u32[]{:S(2)}) copy-start(bf16[8,12,512]{2,1,0:T(8,128)(2,1)S(1)} %get-tuple-element.160) | copy-start | bytes 294916
  117.5 31.1 %copy-start.22 = (f32[24,2048]{1,0:T(8,128)}, f32[24,2048]{1,0:T(8,128)S(1)}, u32[]{:S(2)}) copy-start(f32[24,2048]{1,0:T(8,128)S(1)} %pad.39.params_ref) | copy-start | bytes 589828
  192.8 6.3 copy-start.40
  199.2 109.6 %copy-start.1 = (bf16[1024,2048]{1,0:T(8,128)(2,1)S(1)}, bf16[1024,2048]{1,0:T(8,128)(2,1)}, u32[]{:S(2)}) copy-start(bf16[1024,2048]{1,0:T(8,128)(2,1)} %copy-done) | copy-start | bytes 12582916
  308.8 10.8 %copy-start.2 = (bf16[1024,2048]{1,0:T(8,128)(2,1)}, bf16[1024,2048]{1,0:T(8,128)(2,1)S(1)}, u32[]{:S(2)}) copy-start(bf16[1024,2048]{1,0:T(8,128)(2,1)S(1)} %line_sum.2.delta_ref) | copy-start | bytes 12582916
  340.7 15.5 %copy-start.25 = (bf16[1024,512]{1,0:T(8,128)(2,1)S(1)}, bf16[1024,512]{1,0:T(8,128)(2,1)}, u32[]{:S(2)}) copy-start(bf16[1024,512]{1,0:T(8,128)(2,1)} %teacher_ref.1) | copy-start | bytes 3145732
  356.0 118.8 %copy-start.67 = (f32[1024,2048]{1,0:T(8,128)S(1)}, f32[1024,2048]{1,0:T(8,128)}, u32[]{:S(2)}) copy-start(f32[1024,2048]{1,0:T(8,128)} %fusion.29) | copy-start | bytes 25165828
  488.2 181.6 %reduce-scatter.9.cloned.1.call-start = ((), (), s32[]{:S(2)}) async-start(), calls=%async_computation.12 | async-start | bytes 9437184 | tf_op jit(solution)/shard_map/reduce_scatter | solution.py:1537
  488.3 17.3 %copy-start.46 = (bf16[1024,2048]{1,0:T(8,128)(2,1)S(1)}, bf16[1024,2048]{1,0:T(8,128)(2,1)}, u32[]{:S(2)}) copy-start(bf16[1024,2048]{1,0:T(8,128)(2,1)} %fusion.2) | copy-start | bytes 12582916
  517.0 265.4 %reduce-scatter.11.cloned.1.call-start = ((), (), s32[]{:S(2)}) async-start(), calls=%async_computation.13 | async-start | bytes 2359296 | tf_op jit(solution)/shard_map/reduce_scatter | solution.py:1545
  545.8 104.5 %copy-start.45 = (bf16[1024,2048]{1,0:T(8,128)(2,1)S(1)}, bf16[1024,2048]{1,0:T(8,128)(2,1)}, u32[]{:S(2)}) copy-start(bf16[1024,2048]{1,0:T(8,128)(2,1)} %get-tuple-element.75) | copy-start | bytes 12582916
  650.4 6.8 copy-start.41
  663.1 6.7 copy-start.4
  663.1 153.3 %reduce-scatter.13.cloned.1.call-start = ((), (), s32[]{:S(2)}) async-start(), calls=%async_computation.14 | async-start | bytes 7077888 | tf_op jit(solution)/shard_map/reduce_scatter | solution.py:1556
  675.3 45.1 %copy-start.10 = (bf16[1024,2048]{1,0:T(8,128)(2,1)S(1)}, bf16[1024,2048]{1,0:T(8,128)(2,1)}, u32[]{:S(2)}) copy-start(bf16[1024,2048]{1,0:T(8,128)(2,1)} %get-tuple-element.94.refs_0_) | copy-start | bytes 12582916
  735.7 6.8 copy-start.51
  735.7 7.8 copy-start.42
  735.7 158.2 %reduce-scatter.17.cloned.1.call-start = ((), (), s32[]{:S(2)}) async-start(), calls=%async_computation.16 | async-start | bytes 516096 | tf_op jit(solution)/shard_map/reduce_scatter | solution.py:1602
  743.5 6.3 copy-start.43
  750.0 5.0 copy-start.53
  750.8 4.9 copy-start.52
  756.5 27.2 %copy-start.13 = (bf16[1024,512]{1,0:T(8,128)(2,1)S(1)}, bf16[1024,512]{1,0:T(8,128)(2,1)}, u32[]{:S(2)}) copy-start(bf16[1024,512]{1,0:T(8,128)(2,1)} %copy-done.12) | copy-start | bytes 3145732
  756.5 27.2 %copy-start.15 = (bf16[1024,512]{1,0:T(8,128)(2,1)S(1)}, bf16[1024,512]{1,0:T(8,128)(2,1)}, u32[]{:S(2)}) copy-start(bf16[1024,512]{1,0:T(8,128)(2,1)} %copy-done.14) | copy-start | bytes 3145732
  756.5 27.2 %copy-start.17 = (bf16[1024,512]{1,0:T(8,128)(2,1)S(1)}, bf16[1024,512]{1,0:T(8,128)(2,1)}, u32[]{:S(2)}) copy-start(bf16[1024,512]{1,0:T(8,128)(2,1)} %copy-done.16) | copy-start | bytes 3145732
  756.5 27.2 %copy-start.23 = (f32[24,2048]{1,0:T(8,128)S(1)}, f32[24,2048]{1,0:T(8,128)}, u32[]{:S(2)}) copy-start(f32[24,2048]{1,0:T(8,128)} %copy-done.22) | copy-start | bytes 589828
  784.9 29.9 %copy-start.36 = (bf16[1024,512]{1,0:T(8,128)(2,1)S(1)}, bf16[1024,512]{1,0:T(8,128)(2,1)}, u32[]{:S(2)}) copy-start(bf16[1024,512]{1,0:T(8,128)(2,1)} %copy-done.35) | copy-start | bytes 3145732
  784.9 29.9 %copy-start.49 = (bf16[1024,512]{1,0:T(8,128)(2,1)S(1)}, bf16[1024,512]{1,0:T(8,128)(2,1)}, u32[]{:S(2)}) copy-start(bf16[1024,512]{1,0:T(8,128)(2,1)} %copy-done.48) | copy-start | bytes 3145732
  784.9 30.7 %copy-start.60 = (bf16[8,12,512]{2,1,0:T(8,128)(2,1)S(1)}, bf16[8,12,512]{2,1,0:T(8,128)(2,1)}, u32[]{:S(2)}) copy-start(bf16[8,12,512]{2,1,0:T(8,128)(2,1)} %reshape.119) | copy-start | bytes 294916
  784.9 30.7 %copy-start.61 = (bf16[8,12,512]{2,1,0:T(8,128)(2,1)S(1)}, bf16[8,12,512]{2,1,0:T(8,128)(2,1)}, u32[]{:S(2)}) copy-start(bf16[8,12,512]{2,1,0:T(8,128)(2,1)} %reshape.120) | copy-start | bytes 294916
  814.7 6.7 copy-start.62
  815.5 6.8 copy-start.58
  816.4 79.6 %reduce-scatter.15.cloned.1.call-start = ((), (), s32[]{:S(2)}) async-start(), calls=%async_computation.15 | async-start | bytes 1400832 | tf_op jit(solution)/shard_map/reduce_scatter | solution.py:1620
  817.7 6.2 copy-start.57
  823.9 65.3 %copy-start.59 = (bf16[256,1536]{1,0:T(8,128)(2,1)S(1)}, bf16[256,1536]{1,0:T(8,128)(2,1)}, u32[]{:S(2)}) copy-start(bf16[256,1536]{1,0:T(8,128)(2,1)} %reduce-scatter.13.cloned.1.call-done) | copy-start | bytes 2359300
  890.4 25.3 %copy-start.34 = (bf16[1024,512]{1,0:T(8,128)(2,1)S(1)}, bf16[1024,512]{1,0:T(8,128)(2,1)}, u32[]{:S(2)}) copy-start(bf16[1024,512]{1,0:T(8,128)(2,1)} %copy-done.33) | copy-start | bytes 3145732
  (32 other events, 43.8 us)
Sparse Core Ops, SparseCore 0:
  25.6 31.0 all-gather.8
  59.2 45.5 all-gather.6
  106.7 28.1 all-gather.10
  136.6 54.4 all-gather.12
  192.9 55.9 all-gather.14
  488.3 69.1 reduce-scatter.6
  561.4 71.2 reduce-scatter.8
  663.2 39.4 reduce-scatter.10
  735.8 60.0 reduce-scatter.12
  816.5 34.4 reduce-scatter.16
  854.6 37.0 reduce-scatter.14

commit v4 on v3

--- a/solution.py
+++ b/solution.py
@@ -15,7 +15,7 @@
 group_eps = 0.00064
 CHUNK = 64
 PAIR = 2 * SUBSPACE_SIZE
-CHUNKS_FWD = 2
+CHUNKS_FWD = 4
 CHUNKS_BWD = 2
 DECAY_SCALE = math.exp(-0.5)
 
@@ -536,6 +536,7 @@
 
 
 LINE = "mp"
+GROUP = "dp"
 END_LAG = 3
 MID_LAG = 1
 
@@ -1400,6 +1401,266 @@
     )(whole, three, down, ups, params)
 
 
+def start_gather_kernel(
+    size,
+    groups,
+    chunk_rows,
+    x_ref,
+    narrow_ref,
+    ups_ref,
+    out_ref,
+    narrow_out,
+    ups_out,
+    send_sem,
+    recv_sem,
+    line_send,
+    line_recv,
+    group_send,
+    group_recv,
+):
+    me = lax.axis_index(LINE)
+    mine = lax.axis_index(GROUP)
+    barrier = pltpu.get_barrier_semaphore()
+    for offset in range(1, groups):
+        peer = lax.rem(mine + offset, groups)
+        pl.semaphore_signal(barrier, inc=1, device_id={GROUP: peer}, device_id_type=pl.DeviceIdType.MESH)
+
+    @pl.when(me > 0)
+    def _():
+        pl.semaphore_signal(barrier, inc=1, device_id={LINE: me - 1}, device_id_type=pl.DeviceIdType.MESH)
+
+    @pl.when(me < size - 1)
+    def _():
+        pl.semaphore_signal(barrier, inc=1, device_id={LINE: me + 1}, device_id_type=pl.DeviceIdType.MESH)
+
+    ends = jnp.where((me == 0) | (me == size - 1), 1, 2)
+    pl.semaphore_wait(barrier, ends + groups - 1)
+    flows = two_flows(size)
+    width = x_ref.shape[1]
+    chunks = x_ref.shape[0] // chunk_rows
+
+    def place(block, chunk):
+        rows = pl.ds(pl.multiple_of(chunk * chunk_rows, chunk_rows), chunk_rows)
+        return out_ref.at[rows, pl.ds(pl.multiple_of(block * width, width), width)]
+
+    def copy_of(flow, block, chunk):
+        return flow.copy(
+            place(block, chunk), place(block, chunk), send_sem.at[flow.side, block, chunk], recv_sem.at[flow.side, block, chunk]
+        )
+
+    def narrow_copy(flow, block):
+        spot = narrow_out.at[mine, block]
+        return flow.copy(spot, spot, line_send.at[flow.side, block], line_recv.at[flow.side, block])
+
+    def group_copy(kind, out, peer, slot):
+        return pltpu.make_async_remote_copy(
+            src_ref=out.at[slot],
+            dst_ref=out.at[slot],
+            send_sem=group_send.at[kind, peer],
+            recv_sem=group_recv.at[kind, slot],
+            device_id={GROUP: peer},
+            device_id_type=pl.DeviceIdType.MESH,
+        )
+
+    narrow_out[mine, me] = narrow_ref[...]
+    for flow in flows:
+
+        @pl.when(flow.has_target)
+        def _():
+            narrow_copy(flow, me).start()
+
+    def first(chunk, carry):
+        rows = pl.ds(pl.multiple_of(chunk * chunk_rows, chunk_rows), chunk_rows)
+        out_ref[rows, pl.ds(pl.multiple_of(me * width, width), width)] = x_ref[rows]
+        for flow in flows:
+
+            @pl.when(flow.has_target)
+            def _():
+                copy_of(flow, me, chunk).start()
+
+        return carry
+
+    lax.fori_loop(0, chunks, first, 0)
+    ups_out[mine] = ups_ref[...]
+    for offset in range(1, groups):
+        group_copy(0, ups_out, lax.rem(mine + offset, groups), mine).start()
+    for hop in range(1, size):
+        for flow in flows:
+            block = me - hop * flow.step
+            exists = (block >= 0) & (block < size)
+
+            @pl.when(exists)
+            def _():
+                narrow_copy(flow, block).wait_recv()
+
+            @pl.when(exists & flow.has_target)
+            def _():
+                narrow_copy(flow, block).start()
+
+        if hop == size - 1:
+            for offset in range(1, groups):
+                group_copy(1, narrow_out, lax.rem(mine + offset, groups), mine).start()
+
+        def forward(chunk, carry):
+            for flow in flows:
+                block = me - hop * flow.step
+                exists = (block >= 0) & (block < size)
+
+                @pl.when(exists)
+                def _():
+                    copy_of(flow, block, chunk).wait_recv()
+
+                @pl.when(exists & flow.has_target)
+                def _():
+                    copy_of(flow, block, chunk).start()
+
+            return carry
+
+        lax.fori_loop(0, chunks, forward, 0)
+    for offset in range(1, groups):
+        peer = lax.rem(mine + offset, groups)
+        for kind, out in ((0, ups_out), (1, narrow_out)):
+            group_copy(kind, out, peer, peer).wait_recv()
+            group_copy(kind, out, peer, mine).wait_send()
+    for hop in range(size):
+
+        def drain(chunk, carry):
+            for flow in flows:
+                block = me - hop * flow.step
+                exists = (block >= 0) & (block < size)
+
+                @pl.when(exists & flow.has_target)
+                def _():
+                    copy_of(flow, block, chunk).wait_send()
+
+            return carry
+
+        lax.fori_loop(0, chunks, drain, 0)
+        for flow in flows:
+            block = me - hop * flow.step
+            exists = (block >= 0) & (block < size)
+
+            @pl.when(exists & flow.has_target)
+            def _():
+                narrow_copy(flow, block).wait_send()
+
+
+def start_gather(x, narrow, ups, size, groups, collective_id, chunk_rows=256):
+    rows, cols = x.shape
+    chunks = rows // chunk_rows
+    shape = jax.ShapeDtypeStruct
+    dma = pltpu.SemaphoreType.DMA
+    return pl.pallas_call(
+        partial(start_gather_kernel, size, groups, chunk_rows),
+        out_shape=[
+            shape((rows, size * cols), x.dtype),
+            shape((groups, size) + narrow.shape, x.dtype),
+            shape((groups,) + ups.shape, x.dtype),
+        ],
+        in_specs=[pl.BlockSpec(memory_space=pltpu.VMEM)] * 3,
+        out_specs=[pl.BlockSpec(memory_space=pltpu.VMEM)] * 3,
+        scratch_shapes=[
+            dma((2, size, chunks)),
+            dma((2, size, chunks)),
+            dma((2, size)),
+            dma((2, size)),
+            dma((2, groups)),
+            dma((2, groups)),
+        ],
+        compiler_params=pltpu.CompilerParams(
+            collective_id=collective_id, has_side_effects=True, vmem_limit_bytes=48 * 1024 * 1024
+        ),
+        cost_estimate=pl.CostEstimate(flops=0, bytes_accessed=link_cost(3 * rows * cols), transcendentals=0),
+        name="start_gather",
+    )(x, narrow, ups)
+
+
+def channel_forward_kernel(
+    seq_len,
+    whole_ref,
+    delta_ref,
+    key_ref,
+    value_ref,
+    params_ref,
+    mixed_ref,
+    active_ref,
+    squared_ref,
+    part_ref,
+    own_ref,
+):
+    tile = pl.program_id(0)
+    rows_each = mixed_ref.shape[0]
+    width = whole_ref.shape[1]
+    own_width = own_ref.shape[1]
+    start = tile * rows_each
+    at_start = lax.rem(start, seq_len) == 0
+    edge = 16
+    rows = pl.ds(pl.multiple_of(start, rows_each), rows_each)
+    edge_rows = pl.ds(pl.multiple_of(jnp.maximum(start - edge, 0), edge), edge)
+    inverse_width = 1.0 / width
+
+    def residual(place, cols):
+        return whole_ref[place, cols].astype(jnp.float32) + delta_ref[place, cols].astype(jnp.float32)
+
+    def moments(place):
+        values = residual(place, slice(0, width))
+        centre = jnp.sum(values, axis=1, keepdims=True) * inverse_width
+        values = values - centre
+        spread = jnp.sum(values * values, axis=1, keepdims=True) * inverse_width
+        return centre, lax.rsqrt(spread + norm_eps)
+
+    centre, inv = moments(rows)
+    edge_centre, edge_inv = moments(edge_rows)
+    own_start = pl.multiple_of(lax.axis_index(LINE) * own_width, own_width)
+    own_ref[...] = residual(rows, pl.ds(own_start, own_width))
+    block_cols = 256
+    row_index = iota((rows_each, block_cols), 0)
+    for block in range(width // block_cols):
+        cols = slice(block * block_cols, (block + 1) * block_cols)
+        gain, bias, rate = params_ref[0:1, cols], params_ref[1:2, cols], params_ref[2:3, cols]
+        normed = (residual(rows, cols) - centre) * inv * gain + bias
+        edge_unit = (residual(edge_rows, cols) - edge_centre) * edge_inv
+        edge_normed = (edge_unit * gain + bias)[edge - 1 : edge]
+        edge_normed = jnp.where(at_start, 0.0, edge_normed)
+        before = jnp.where(row_index == 0, edge_normed, pltpu.roll(normed, 1, 0))
+        mixed_ref[:, cols] = low(normed + (before - normed) * rate)
+    hidden_cols = 512
+    for block in range(key_ref.shape[1] // hidden_cols):
+        cols = slice(block * hidden_cols, (block + 1) * hidden_cols)
+        active = jnp.maximum(dot_nn(mixed_ref[...], key_ref[:, cols]), 0.0)
+        active_ref[:, cols] = active
+        squared_ref[:, cols] = low(active * active)
+    for block in range(width // hidden_cols):
+        cols = slice(block * hidden_cols, (block + 1) * hidden_cols)
+        part_ref[:, cols] = low(dot_nn(squared_ref[...], value_ref[:, cols]))
+
+
+def channel_forward(whole, delta, key_w, value_w, params, own_width):
+    positions, width = whole.shape
+    units = key_w.shape[1]
+    rows_each = 256
+    tile = lambda cols: pl.BlockSpec((rows_each, cols), lambda i: (i, 0))
+    full = pl.BlockSpec(memory_space=pltpu.VMEM)
+    shape = jax.ShapeDtypeStruct
+    return pl.pallas_call(
+        partial(channel_forward_kernel, SEQ_LEN),
+        grid=(positions // rows_each,),
+        in_specs=[full] * 5,
+        out_specs=[tile(width), tile(units), tile(units), tile(width), tile(own_width)],
+        out_shape=[
+            shape((positions, width), jnp.bfloat16),
+            shape((positions, units), jnp.float32),
+            shape((positions, units), jnp.bfloat16),
+            shape((positions, width), jnp.bfloat16),
+            shape((positions, own_width), jnp.float32),
+        ],
+        compiler_params=pltpu.CompilerParams(
+            dimension_semantics=("arbitrary",), vmem_limit_bytes=56 * 1024 * 1024
+        ),
+        name="channel_forward",
+    )(whole, delta, key_w, value_w, params)
+
+
 def matmul(left_op, right_op):
     return jnp.dot(left_op, right_op, preferred_element_type=jnp.float32)
 
@@ -1410,24 +1671,6 @@
 
 def against(grad_op, weight_op):
     return jnp.einsum("tn,kn->tk", grad_op, weight_op, preferred_element_type=jnp.float32)
-
-
-def layer_norm(values, scale_in, offset):
-    centre = jnp.mean(values, axis=-1, keepdims=True)
-    centred = values - centre
-    spread = jnp.mean(centred * centred, axis=-1, keepdims=True)
-    return centred * lax.rsqrt(spread + norm_eps) * scale_in + offset
-
-
-def shifted(values):
-    grid_view = values.reshape(values.shape[0] // SEQ_LEN, SEQ_LEN, values.shape[1])
-    earlier = jnp.concatenate([jnp.zeros_like(grid_view[:, :1]), grid_view[:, :-1]], axis=1)
-    return earlier.reshape(values.shape)
-
-
-def section_out(residual, scale_in, offset, mix_rate):
-    standardized_source = layer_norm(residual, scale_in, offset)
-    return standardized_source + (shifted(standardized_source) - standardized_source) * mix_rate
 
 
 def body(
@@ -1458,12 +1701,13 @@
     valid = (places[None, :] < own_lengths[:, None]).astype(jnp.float32).reshape(position_count)
     loss_scale = position_count * lax.axis_size("dp") / jnp.sum(lengths).astype(jnp.float32)
     line_size = lax.axis_size("mp")
-    whole_low = line_gather(hidden, line_size, 1)
     low_rank = (decay_down.shape[1], rate_down.shape[1], gate_down.shape[1])
     narrow = jnp.concatenate([decay_down, rate_down, gate_down, feature_params], axis=1)
     narrow = jnp.pad(narrow, ((0, 0), (0, -narrow.shape[1] % 128)))
-    narrow_w = lax.all_gather(narrow, "mp", axis=0, tiled=True)
-    narrow_w = lax.all_gather(narrow_w, "dp", axis=0, tiled=True)
+    ups = jnp.concatenate([decay_up, rate_up, gate_up], axis=0)
+    ups = jnp.pad(ups, ((0, -ups.shape[0] % 16), (0, 0)))
+    whole_low, narrow_w, ups = start_gather(hidden, narrow, ups, line_size, groups, 1)
+    narrow_w = narrow_w.reshape(-1, narrow.shape[1])
     decay_down_w = narrow_w[:, : low_rank[0]]
     rate_down_w = narrow_w[:, low_rank[0] : low_rank[0] + low_rank[1]]
     gate_down_w = narrow_w[:, low_rank[0] + low_rank[1] : sum(low_rank)]
@@ -1472,10 +1716,9 @@
         jnp.concatenate([receptance, key_proj, value_proj], axis=1), "dp", axis=0, tiled=True
     )
     up_rows = (decay_up.shape[0], rate_up.shape[0], gate_up.shape[0])
-    ups = lax.all_gather(jnp.concatenate([decay_up, rate_up, gate_up], axis=0), "dp", axis=0)
     decay_up_w = ups[:, : up_rows[0]].reshape(-1, part_width)
     rate_up_w = ups[:, up_rows[0] : up_rows[0] + up_rows[1]].reshape(-1, part_width)
-    gate_up_w = ups[:, up_rows[0] + up_rows[1] :].reshape(-1, part_width)
+    gate_up_w = ups[:, up_rows[0] + up_rows[1] : sum(up_rows)].reshape(-1, part_width)
     output_w = lax.all_gather(output_proj, "dp", axis=1, tiled=True)
     ffn_key_w = lax.all_gather(ffn_key, "dp", axis=0, tiled=True)
     ffn_value_w = lax.all_gather(ffn_value, "dp", axis=1, tiled=True)
@@ -1517,14 +1760,9 @@
     )
     gated_low, *kept = run_mixer_forward(*mixer_args)
     delta_low = line_sum(matmul(gated_low, output_w).astype(jnp.bfloat16), line_size, 2)
-    residual = whole_low.astype(jnp.float32) + delta_low.astype(jnp.float32)
-    ffn_in = section_out(residual, params[:, 15], params[:, 16], params[:, 17])
-    ffn_low = ffn_in.astype(jnp.bfloat16)
-    pre_act = matmul(ffn_low, ffn_key_w)
-    active = jnp.maximum(pre_act, 0.0)
-    squared = (active * active).astype(jnp.bfloat16)
-    ffn_part = matmul(squared, ffn_value_w).astype(jnp.bfloat16)
-    own_residual = lax.dynamic_slice_in_dim(residual, col_start, part_width, 1)
+    ffn_low, active, squared, ffn_part, own_residual = channel_forward(
+        whole_low, delta_low, ffn_key_w, ffn_value_w, params_rows[15:23], part_width
+    )
     error_scale = jnp.broadcast_to((loss_scale * valid)[:, None], (position_count, 128))
     out_state, grad_low = line_error(ffn_part, own_residual, teacher, error_scale, line_size, 3)
     grad_ffn_value = contract_rows(squared, grad_low).astype(jnp.bfloat16)
@@ -1538,8 +1776,8 @@
     d_resid_part, d_params_out = output_backward(
         whole_low, delta_low, grad_pre, ffn_key_w, params_rows[15:23]
     )
-    d_residual = grad_low.astype(jnp.float32) + line_sum(d_resid_part, line_size, 5).astype(jnp.float32)
-    d_low = d_residual.astype(jnp.bfloat16)
+    d_delta = line_sum(d_resid_part, line_size, 5)
+    d_low = (grad_low.astype(jnp.float32) + d_delta.astype(jnp.float32)).astype(jnp.bfloat16)
     grad_output_proj = contract_rows(gated_low, d_low).astype(jnp.bfloat16)
     d_low, grad_output_proj = lax.optimization_barrier((d_low, grad_output_proj))
     grad_output_proj = lax.psum_scatter(grad_output_proj, "dp", scatter_dimension=1, tiled=True)
@@ -1598,9 +1836,7 @@
         ],
         axis=1,
     ).astype(jnp.bfloat16)
-    d_in_part, grad_three, up_grads = lax.optimization_barrier((d_in_part, grad_three, up_grads))
-    up_grads = lax.psum_scatter(up_grads, "dp", scatter_dimension=0, tiled=True)
-    up_grads = up_grads.reshape(-1, part_width).astype(jnp.float32)
+    d_in_part, grad_three = lax.optimization_barrier((d_in_part, grad_three))
     core_grads = lax.dynamic_update_slice_in_dim(
         jnp.zeros((7, model_width), jnp.float32), d_columns, col_start, 1
     )
@@ -1614,17 +1850,20 @@
     )
     param_count = param_rows.shape[0]
     narrow_grads = jnp.pad(
-        jnp.concatenate([d_down, param_rows], axis=0), ((0, -(own_rank + param_count) % 8), (0, 0))
+        jnp.concatenate([d_down, param_rows], axis=0), ((0, -(own_rank + param_count) % 32), (0, 0))
     )
     d_in_part, narrow_grads = lax.optimization_barrier((d_in_part, narrow_grads))
     narrow_grads = lax.psum_scatter(narrow_grads, "dp", scatter_dimension=1, tiled=True)
-    grad_hidden = lax.dynamic_slice_in_dim(d_residual, col_start, part_width, 1) + line_scatter(
-        d_in_part, line_size, 7
+    up_grads = lax.psum_scatter(up_grads, "dp", scatter_dimension=0, tiled=True)
+    up_grads = up_grads.reshape(-1, part_width).astype(jnp.float32)
+    grad_hidden = line_scatter(d_in_part, line_size, 7) + (
+        lax.dynamic_slice_in_dim(grad_low, col_start, part_width, 1).astype(jnp.float32)
+        + lax.dynamic_slice_in_dim(d_delta, col_start, part_width, 1).astype(jnp.float32)
     )
     row_block = decay_down.shape[0]
     narrow_grads = jnp.pad(narrow_grads, ((0, 0), (0, -narrow_grads.shape[1] % 128)))
     narrow_rows = narrow_grads.shape[0]
-    narrow_grads = line_gather(narrow_grads, line_size, 4, chunk_rows=narrow_rows)
+    narrow_grads = line_gather(narrow_grads, line_size, 4, chunk_rows=narrow_rows // 4)
     narrow_grads = narrow_grads.reshape(narrow_rows, line_size, -1)
     narrow_grads = lax.dynamic_slice_in_dim(narrow_grads, mp_index * row_block, row_block, 2)
 

time: 934 us -> 915 us (0.980)
  Pallas kernels: 675 us -> 728 us
  matrix products: 94.8 us -> 65.9 us
  blocking collectives: 26.7 us -> 0 us
  other arithmetic: 47 us -> 27.4 us
    pallas_call x0 -> x2, Pallas kernels: none -> 121 us  [the longest x1 88.2 us: start_gather(): pl.pallas_call(partial(start_gather_kernel, size, groups, chunk_rows), ou...]
    pallas_call x2 -> x1, Pallas kernels: 86.4 us -> 14.6 us  [line_gather(): pl.pallas_call(partial(line_gather_kernel, size, chunk_rows), out_shape=j...]
    dot_general x3 -> x1, matrix products: 36.2 us -> 5.92 us  [matmul(): return jnp.dot(left_op, right_op, preferred_element_type=jnp.float32)]
    all_gather x2 -> x0, blocking collectives: 26.7 us -> none  [the longest x1 15.6 us: body(): narrow_w = lax.all_gather(narrow, 'mp', axis=0, tiled=True)]
    add x3 -> x1, other arithmetic: 14.8 us -> 3.38 us  [body(): line_scatter(d_in_part, line_size, 7)]
    unnamed x144 -> x142, local copies, waits for them, and re-layouts: 38.6 us -> 43 us
  transfers between devices with their start and end apart: 11 -> 10, of which waited for: 0 -> 1; matrix products, arithmetic and copies ran while one was open for 14% -> 10% of each run, Pallas kernels for 59% -> 62%
where the time goes in v4:
time: 915 us; the launch traced here: 905 us
  Pallas kernels  728 us (80%)
  matrix products  65.9 us (7%)
  local copies, waits for them, and re-layouts  60 us (7%)
  other arithmetic  27.4 us (3%)
  between operations  16.1 us (2%)
    pallas_call x2, Pallas kernels, line_sum(): pl.pallas_call(partial(line_sum_kernel, size, chunk_rows), out_shape=jax....  214 us
    pallas_call x1, Pallas kernels, line_error(): pl.pallas_call(partial(line_error_kernel, size, chunk_rows), out_shape=[j...  118 us
    pallas_call x2, Pallas kernels, line_scatter(): pl.pallas_call(partial(line_scatter_kernel, size, chunk_rows), out_shape=...  93.9 us
    pallas_call x1, Pallas kernels, start_gather(): pl.pallas_call(partial(start_gather_kernel, size, groups, chunk_rows), ou...  88.2 us
    pallas_call x1, Pallas kernels, run_mixer_backward(): pl.pallas_call(partial(mixer_backward, steps_per_seq), grid=(steps,), in_...  43.1 us
    unnamed x142, local copies, waits for them, and re-layouts  43 us
    dot_general x6, matrix products, contract_rows(): jnp.einsum('tk,tn->kn', left_op, right_op, preferred_element_type=jnp.flo...  34 us
    pallas_call x1, Pallas kernels, run_mixer_forward(): pl.pallas_call(partial(mixer_forward, steps_per_seq), grid=(steps,), in_s...  32.6 us
  transfers between devices with their start and end apart: 10, of which 1 were waited for; matrix products, arithmetic and copies ran while one was open for 10% of the time, Pallas kernels for 62%

profile of v4, /device:TPU:0, one launch (start us, length us, event | category | flops | bytes accessed | tf_op | source)
XLA Modules:
  0.0 905.4 jit_solution(9694327839082336302)
XLA Ops:
  7.3 2.1 pad_maximum_fusion
  13.8 88.2 %start_gather.1 = (bf16[1024,2048]{1,0:T(8,128)(2,1)}, bf16[8,4,64,512]{3,2,1,0:T(8,128)(2,1)S(1)}, bf16[8,64,512]{2,1,0:T(8,128)(2,1)S(1)}) custom-call(bf16[1024,512]{1,0:T(8,128)(2,1)S(1)} %copy-done.31, bf16[64,512]{1,0:T(8,128)(2,1)S(1)} %get-tuple-element.157.narrow_ref, bf16[64,512]{1,0:T(8,128)(2,1)S(1)} %get-tuple-element.158.ups_ref), custom_call_target="tpu_custom_call" | custom-call | bytes 251658240 | tf_op jit(solution)/shard_map/start_gather/pallas_call | solution.py:1553
  104.9 26.6 %input_forward.1 = (f32[1024,512]{1,0:T(8,128)}, f32[1024,512]{1,0:T(8,128)}, f32[1024,512]{1,0:T(8,128)}, f32[1024,512]{1,0:T(8,128)}, f32[1024,512]{1,0:T(8,12...) custom-call(bf16[1024,2048]{1,0:T(8,128)(2,1)} %get-tuple-element.73, ...), custom_call_target="tpu_custom_call" | custom-call | tf_op jit(solution)/shard_map/input_forward/pallas_call | solution.py:1389
  131.5 1.6 copy-done.4
  133.1 2.2 copy-done.6
  135.3 32.6 %mixer_forward.1 = (bf16[1024,512]{1,0:T(8,128)(2,1)S(1)}, f32[1024,512]{1,0:T(8,128)S(1)}, bf16[1024,512]{1,0:T(8,128)(2,1)S(1)}, bf16[1024,512]{1,0:T(8,128)(2...) custom-call(s32[1]{0:T(128)} %dynamic_slice.33.length_ref, ...), custom_call_target="tpu_custom_call" | custom-call | tf_op jit(solution)/shard_map/mixer_forward/pallas_call | solution.py:477
  173.6 5.9 convolution_convert_fusion.2.x_ref
  179.5 108.3 %line_sum.2.delta_ref = bf16[1024,2048]{1,0:T(8,128)(2,1)S(1)} custom-call(bf16[1024,2048]{1,0:T(8,128)(2,1)} %convolution_convert_fusion.2.x_ref), custom_call_target="tpu_custom_call" | custom-call | bytes 335544320 | tf_op jit(solution)/shard_map/line_sum/pallas_call | solution.py:665
  287.8 2.0 copy-done
  289.8 32.3 %channel_forward.1 = (bf16[1024,2048]{1,0:T(8,128)(2,1)}, f32[1024,2048]{1,0:T(8,128)}, bf16[1024,2048]{1,0:T(8,128)(2,1)}, bf16[1024,2048]{1,0:T(8,128)(2,1)}, f32[1024,512]{1,0:T(8,128)}) custom-call(bf16[1024,2048]{1,0:T(8,128)(2,1)} %get-tuple-element.73.whole_ref, bf16[1024,2048]{1,0:T(8,128)(2,1)} %copy-done, ...), custom_call_target="tpu_custom_call" | custom-call | tf_op jit(solution)/shard_map/channel_forward/pallas_call | solution.py:1645
  322.3 1.6 copy-done.23
  323.9 117.8 %line_error.1 = (bf16[1024,512]{1,0:T(8,128)(2,1)S(1)}, bf16[1024,2048]{1,0:T(8,128)(2,1)}) custom-call(bf16[1024,2048]{1,0:T(8,128)(2,1)} %get-tuple-element.83.x_ref, f32[1024,512]{1,0:T(8,128)S(1)} %copy-done.23, bf16[1024,512]{1,0:T(8,128)(2,1)S(1)} %copy-done.24, f32[1024,128]{1,0:T(8,128)S(1)} %broadcast_in_dim.4.weight_ref), custom_call_target="tpu_custom_call" | custom-call | bytes 335544320 | tf_op jit(solution)/shard_map/line_error/pallas_call | solution.py:1177
  442.6 13.4 %convolution_convert_fusion.1 = bf16[2048,2048]{1,0:T(8,128)(2,1)} fusion(bf16[1024,2048]{1,0:T(8,128)(2,1)S(1)} %copy-done.65, bf16[1024,2048]{1,0:T(8,128)(2,1)} %get-tuple-element.94), kind=kOutput, calls=%fused_computation.3 | convolution fusion | flops 8594128896 | bytes 16777216 | tf_op jit(solution)/shard_map/tk,tn->kn/dot_general | solution.py:1669
  456.1 14.8 %multiply_convert_fusion.dpre_ref = bf16[1024,2048]{1,0:T(8,128)(2,1)S(1)} fusion(f32[1024,2048]{1,0:T(8,128)} %get-tuple-element.95, bf16[1024,2048]{1,0:T(8,128)(2,1)} %get-tuple-element.94, bf16[2048,2048]{1,0:T(8,128)(2,1)} %all-gather.11.cloned.1.call-done.value_ref), kind=kOutput, calls=%fused_computation.1 | convolution fusion | flops 8596226048 | bytes 25165824 | tf_op jit(solution)/shard_map/tn,kn->tk/dot_general | solution.py:1673
  470.9 2.1 copy-done.44
  473.0 11.4 %convolution_convert_fusion = bf16[2048,2048]{1,0:T(8,128)(2,1)} fusion(bf16[1024,2048]{1,0:T(8,128)(2,1)S(1)} %copy-done.64, bf16[1024,2048]{1,0:T(8,128)(2,1)S(1)} %multiply_convert_fusion.dpre_ref), kind=kOutput, calls=%fused_computation.2 | convolution fusion | flops 8594128896 | bytes 16777216 | tf_op jit(solution)/shard_map/tk,tn->kn/dot_general | solution.py:1669
  485.3 26.0 %output_backward.1 = (bf16[1024,2048]{1,0:T(8,128)(2,1)S(1)}, f32[8,8,2048]{2,1,0:T(8,128)S(1)}) custom-call(bf16[1024,2048]{1,0:T(8,128)(2,1)} %get-tuple-element.73.whole_ref, bf16[1024,2048]{1,0:T(8,128)(2,1)} %copy-done, bf16[1024,2048]{1,0:T(8,128)(2,1)} %copy-done.44, bf16[2048,2048]{1,0:T(8,128)(2,1)} %all-gather.9.cloned.1.call-done.key_ref.weight_ref, ...), custom_call_target="tpu_custom_call" | custom-call | tf_op jit(solution)/shard_map/output_backward/pallas_call | solution.py:1283
  511.2 2.0 copy-done.10
  513.2 106.1 %line_sum.3 = bf16[1024,2048]{1,0:T(8,128)(2,1)S(1)} custom-call(bf16[1024,2048]{1,0:T(8,128)(2,1)} %copy-done.10), custom_call_target="tpu_custom_call" | custom-call | bytes 335544320 | tf_op jit(solution)/shard_map/line_sum/pallas_call | solution.py:665
  619.4 2.3 add_convert_fusion
  622.5 1.9 copy-done.45
  624.4 3.8 convolution_convert_fusion.3
  628.3 6.7 fusion.29.dz_ref
  635.0 1.7 copy-done.7
  640.5 43.1 %mixer_backward.1 = (bf16[1024,512]{1,0:T(8,128)(2,1)S(1)}, bf16[1024,512]{1,0:T(8,128)(2,1)S(1)}, bf16[1024,512]{1,0:T(8,128)(2,1)S(1)}, bf16[1024,512]{1,0:T(8...) custom-call(s32[1]{0:T(128)} %dynamic_slice.33.length_ref, ...), custom_call_target="tpu_custom_call" | custom-call | tf_op jit(solution)/shard_map/mixer_backward/pallas_call | solution.py:514
  685.6 2.2 copy-done.12
  687.8 10.2 %weight_grads.1 = bf16[2048,1536]{1,0:T(8,128)(2,1)} custom-call(bf16[1024,2048]{1,0:T(8,128)(2,1)S(1)} %copy-done.11, bf16[1024,2048]{1,0:T(8,128)(2,1)S(1)} %copy-done.12, bf16[1024,2048]{1,0:T(8,128)(2,1)} %get-tuple-element.111.refs_2_, bf16[1024,512]{1,0:T(8,128)(2,1)S(1)} %get-tuple-element.103.refs_3_.dr_ref, ...), custom_call_target="tpu_custom_call" | custom-call | tf_op jit(solution)/shard_map/weight_grads/pallas_call | solution.py:1027
  701.0 1.7 reshape_reshape.9
  702.7 1.6 reshape_reshape.10
  704.3 1.4 slice.117
  705.7 1.8 pad.48
  707.4 1.7 pad.47
  709.2 1.8 pad.49
  712.6 1.4 fusion.9.down_ref
  719.7 1.6 convolution_convert_fusion.5
  721.9 1.8 fusion.31
  723.8 1.9 fusion.30
  726.5 22.8 %line_scatter.2 = f32[1024,128]{1,0:T(8,128)S(1)} custom-call(bf16[1024,512]{1,0:T(8,128)(2,1)S(1)} %add_convert_fusion.1.x_ref), custom_call_target="tpu_custom_call" | custom-call | bytes 62914560 | tf_op jit(solution)/shard_map/line_scatter/pallas_call | solution.py:856
  750.0 2.6 convolution_convert_fusion.4
  752.7 1.8 pad_maximum_fusion.2
  756.9 28.8 %input_backward.1 = (bf16[1024,2048]{1,0:T(8,128)(2,1)}, f32[8,8,2048]{2,1,0:T(8,128)S(1)}, f32[128,2048]{1,0:T(8,128)S(1)}) custom-call(bf16[1024,2048]{1,0:T(8,128)(2,1)} %get-tuple-element.73.whole_ref, bf16[1024,512]{1,0:T(8,128)(2,1)S(1)} %copy-done.14, bf16[1024,512]{1,0:T(8,128)(2,1)S(1)} %copy-done.16, bf16[1024,512]{1,0:T(8,128)(2,1)S(1)} %copy-done.18, ...), custom_call_target="tpu_custom_call" | custom-call | tf_op jit(solution)/shard_map/input_backward/pallas_call | solution.py:990
  788.8 2.4 select_maximum_fusion
  792.1 1.6 convert_element_type.110
  793.7 1.5 convert_element_type.111
  795.2 5.2 reduce-scatter.17.cloned.1.call-done
  802.5 71.1 %line_scatter.3 = f32[1024,512]{1,0:T(8,128)S(1)} custom-call(bf16[1024,2048]{1,0:T(8,128)(2,1)} %get-tuple-element.125.x_ref), custom_call_target="tpu_custom_call" | custom-call | bytes 251658240 | tf_op jit(solution)/shard_map/line_scatter/pallas_call | solution.py:856
  874.8 3.4 add_add_fusion
  879.1 14.6 %line_gather.1 = f32[160,1024]{1,0:T(8,128)S(1)} custom-call(f32[160,256]{1,0:T(8,128)S(1)} %copy-done.41), custom_call_target="tpu_custom_call" | custom-call | bytes 19660800 | tf_op jit(solution)/shard_map/line_gather/pallas_call | solution.py:749
  (210 shorter events, 48.0 us)
Async XLA Ops:
  7.2 4.4 copy-start.66
  7.2 6.3 copy-start.63
  7.2 6.4 copy-start.58
  7.2 6.4 copy-start.61
  7.2 6.4 copy-start.62
  7.2 6.4 copy-start.57
  7.2 6.4 copy-start.59
  7.3 6.4 copy-start.60
  7.3 6.5 copy-start.31
  7.3 97.6 %all-gather.5.cloned.1.call-start = ((), (), s32[]{:S(2)}) async-start(), calls=%async_computation.6 | async-start | bytes 7077888 | tf_op jit(solution)/shard_map/all_gather | solution.py:1715
  9.5 164.1 %all-gather.7.cloned.1.call-start = ((), (), s32[]{:S(2)}) async-start(), calls=%async_computation.7 | async-start | bytes 2359296 | tf_op jit(solution)/shard_map/all_gather | solution.py:1722
  10.2 279.6 %all-gather.9.cloned.1.call-start = ((), (), s32[]{:S(2)}) async-start(), calls=%async_computation.8 | async-start | bytes 9437184 | tf_op jit(solution)/shard_map/all_gather | solution.py:1723
  11.0 278.9 %all-gather.11.cloned.1.call-start = ((), (), s32[]{:S(2)}) async-start(), calls=%async_computation.9 | async-start | bytes 9437184 | tf_op jit(solution)/shard_map/all_gather | solution.py:1724
  11.5 623.4 %reduce-scatter.7.cloned.1.call-start = ((), (), s32[]{:S(2)}) async-start(), calls=%async_computation.10 | async-start | bytes 9437184 | tf_op jit(solution)/shard_map/reduce_scatter | solution.py:1770
  102.0 2.8 copy-start.2
  102.0 29.5 %copy-start.47 = (bf16[8,32,512]{2,1,0:T(8,128)(2,1)}, bf16[8,32,512]{2,1,0:T(8,128)(2,1)S(1)}, u32[]{:S(2)}) copy-start(bf16[8,32,512]{2,1,0:T(8,128)(2,1)S(1)} %slice.87) | copy-start | bytes 786436
  133.1 2.2 copy-start.6
  289.8 32.5 %copy-start.24 = (bf16[1024,512]{1,0:T(8,128)(2,1)S(1)}, bf16[1024,512]{1,0:T(8,128)(2,1)}, u32[]{:S(2)}) copy-start(bf16[1024,512]{1,0:T(8,128)(2,1)} %teacher_ref.1) | copy-start | bytes 3145732
  323.9 118.7 %copy-start.65 = (bf16[1024,2048]{1,0:T(8,128)(2,1)S(1)}, bf16[1024,2048]{1,0:T(8,128)(2,1)}, u32[]{:S(2)}) copy-start(bf16[1024,2048]{1,0:T(8,128)(2,1)} %get-tuple-element.93) | copy-start | bytes 12582916
  456.0 178.9 %reduce-scatter.9.cloned.1.call-start = ((), (), s32[]{:S(2)}) async-start(), calls=%async_computation.11 | async-start | bytes 9437184 | tf_op jit(solution)/shard_map/reduce_scatter | solution.py:1775
  456.1 16.9 %copy-start.64 = (bf16[1024,2048]{1,0:T(8,128)(2,1)S(1)}, bf16[1024,2048]{1,0:T(8,128)(2,1)}, u32[]{:S(2)}) copy-start(bf16[1024,2048]{1,0:T(8,128)(2,1)} %get-tuple-element.96) | copy-start | bytes 12582916
  484.4 265.6 %reduce-scatter.11.cloned.1.call-start = ((), (), s32[]{:S(2)}) async-start(), calls=%async_computation.12 | async-start | bytes 2359296 | tf_op jit(solution)/shard_map/reduce_scatter | solution.py:1783
  513.2 106.1 %copy-start.38 = (f32[8,8,2048]{2,1,0:T(8,128)}, f32[8,8,2048]{2,1,0:T(8,128)S(1)}, u32[]{:S(2)}) copy-start(f32[8,8,2048]{2,1,0:T(8,128)S(1)} %get-tuple-element.124) | copy-start | bytes 1572868
  513.2 106.1 %copy-start.42 = (bf16[1024,2048]{1,0:T(8,128)(2,1)S(1)}, bf16[1024,2048]{1,0:T(8,128)(2,1)}, u32[]{:S(2)}) copy-start(bf16[1024,2048]{1,0:T(8,128)(2,1)} %get-tuple-element.94) | copy-start | bytes 12582916
  619.4 3.1 copy-start.1
  628.2 6.7 copy-start.5
  628.2 163.0 %reduce-scatter.13.cloned.1.call-start = ((), (), s32[]{:S(2)}) async-start(), calls=%async_computation.13 | async-start | bytes 7077888 | tf_op jit(solution)/shard_map/reduce_scatter | solution.py:1794
  640.5 45.1 %copy-start.11 = (bf16[1024,2048]{1,0:T(8,128)(2,1)S(1)}, bf16[1024,2048]{1,0:T(8,128)(2,1)}, u32[]{:S(2)}) copy-start(bf16[1024,2048]{1,0:T(8,128)(2,1)} %get-tuple-element.109.refs_0_) | copy-start | bytes 12582916
  685.6 2.2 copy-start.12
  700.9 3.4 copy-start.3
  700.9 99.4 %reduce-scatter.17.cloned.1.call-start = ((), (), s32[]{:S(2)}) async-start(), calls=%async_computation.15 | async-start | bytes 516096 | tf_op jit(solution)/shard_map/reduce_scatter | solution.py:1857
  711.0 3.0 copy-start.43
  714.0 2.9 copy-start.39
  715.1 4.5 copy-start.9
  717.0 8.6 copy-start.55
  719.7 6.0 copy-start.36
  721.9 3.8 copy-start.48
  726.4 29.4 %copy-start.14 = (bf16[1024,512]{1,0:T(8,128)(2,1)S(1)}, bf16[1024,512]{1,0:T(8,128)(2,1)}, u32[]{:S(2)}) copy-start(bf16[1024,512]{1,0:T(8,128)(2,1)} %copy-done.13) | copy-start | bytes 3145732
  726.5 29.4 %copy-start.16 = (bf16[1024,512]{1,0:T(8,128)(2,1)S(1)}, bf16[1024,512]{1,0:T(8,128)(2,1)}, u32[]{:S(2)}) copy-start(bf16[1024,512]{1,0:T(8,128)(2,1)} %copy-done.15) | copy-start | bytes 3145732
  726.5 29.4 %copy-start.18 = (bf16[1024,512]{1,0:T(8,128)(2,1)S(1)}, bf16[1024,512]{1,0:T(8,128)(2,1)}, u32[]{:S(2)}) copy-start(bf16[1024,512]{1,0:T(8,128)(2,1)} %copy-done.17) | copy-start | bytes 3145732
  754.5 123.7 %reduce-scatter.15.cloned.1.call-start = ((), (), s32[]{:S(2)}) async-start(), calls=%async_computation.14 | async-start | bytes 1474560 | tf_op jit(solution)/shard_map/reduce_scatter | solution.py:1856
  756.9 31.9 %copy-start.56 = (f32[8,512]{1,0:T(8,128)S(1)}, f32[8,512]{1,0:T(8,128)}, u32[]{:S(2)}) copy-start(f32[8,512]{1,0:T(8,128)} %reduce_sum.47) | copy-start | bytes 49156
  756.9 31.9 %slice-start = ((f32[8,2048]{1,0:T(8,128)}), f32[3,2048]{1,0:T(4,128)S(1)}, s32[]{:S(2)}) async-start(f32[8,2048]{1,0:T(8,128)} %copy-done.55), calls=%async_computation.16 | async-start | bytes 65536 | tf_op jit(solution)/shard_map/slice | solution.py:1847
  787.5 3.8 copy-start.54
  787.5 4.7 copy-start.52
  787.5 6.2 copy-start.51
  793.7 79.9 %copy-start.53 = (bf16[256,1536]{1,0:T(8,128)(2,1)S(1)}, bf16[256,1536]{1,0:T(8,128)(2,1)}, u32[]{:S(2)}) copy-start(bf16[256,1536]{1,0:T(8,128)(2,1)} %reduce-scatter.13.cloned.1.call-done) | copy-start | bytes 2359300
  874.8 22.4 %copy-start.33 = (bf16[1024,512]{1,0:T(8,128)(2,1)S(1)}, bf16[1024,512]{1,0:T(8,128)(2,1)}, u32[]{:S(2)}) copy-start(bf16[1024,512]{1,0:T(8,128)(2,1)} %copy-done.32) | copy-start | bytes 3145732
  (30 other events, 36.7 us)
Sparse Core Ops, SparseCore 0:
  10.6 50.5 all-gather.4
  63.0 40.1 all-gather.6
  105.1 54.6 all-gather.8
  161.5 55.9 all-gather.10
  456.2 70.6 reduce-scatter.6
  530.6 71.2 reduce-scatter.8
  628.3 40.9 reduce-scatter.10
  701.1 61.5 reduce-scatter.12
  766.3 33.9 reduce-scatter.16
  803.8 37.2 reduce-scatter.14

commit v5 on v4

--- a/solution.py
+++ b/solution.py
@@ -497,7 +497,7 @@
         ],
         scratch_shapes=[pltpu.VMEM((pairs, PAIR, PAIR), jnp.float32)],
         compiler_params=pltpu.CompilerParams(
-            dimension_semantics=("arbitrary",), vmem_limit_bytes=40 * 1024 * 1024
+            dimension_semantics=("arbitrary",), vmem_limit_bytes=60 * 1024 * 1024
         ),
         name="mixer_forward",
     )(lengths, r, k, v, dw, da, gate, cols)
@@ -529,7 +529,7 @@
         + [shape((8, 8, part_width), jnp.float32)],
         scratch_shapes=[pltpu.VMEM((pairs, PAIR, PAIR), jnp.float32)],
         compiler_params=pltpu.CompilerParams(
-            dimension_semantics=("arbitrary",), vmem_limit_bytes=40 * 1024 * 1024
+            dimension_semantics=("arbitrary",), vmem_limit_bytes=60 * 1024 * 1024
         ),
         name="mixer_backward",
     )(lengths, r, k, v, dw, da, gate, cols, y, t, u, s, lk, reads, dz)
@@ -1032,7 +1032,7 @@
         out_specs=pl.BlockSpec((block, count * part), lambda i: (i, 0)),
         out_shape=jax.ShapeDtypeStruct((width, count * part), jnp.bfloat16),
         compiler_params=pltpu.CompilerParams(
-            dimension_semantics=("arbitrary",), vmem_limit_bytes=40 * 1024 * 1024
+            dimension_semantics=("arbitrary",), vmem_limit_bytes=60 * 1024 * 1024
         ),
         name="weight_grads",
     )(*lefts, *rights)
@@ -1852,7 +1852,7 @@
     narrow_grads = jnp.pad(
         jnp.concatenate([d_down, param_rows], axis=0), ((0, -(own_rank + param_count) % 32), (0, 0))
     )
-    d_in_part, narrow_grads = lax.optimization_barrier((d_in_part, narrow_grads))
+    d_in_part, narrow_grads, up_grads = lax.optimization_barrier((d_in_part, narrow_grads, up_grads))
     narrow_grads = lax.psum_scatter(narrow_grads, "dp", scatter_dimension=1, tiled=True)
     up_grads = lax.psum_scatter(up_grads, "dp", scatter_dimension=0, tiled=True)
     up_grads = up_grads.reshape(-1, part_width).astype(jnp.float32)

time: 915 us -> 882 us (0.964)
  local copies, waits for them, and re-layouts: 60 us -> 33.1 us
    unnamed x142 -> x104, local copies, waits for them, and re-layouts: 43 us -> 22.2 us
  transfers between devices with their start and end apart: 10 -> 10, of which waited for: 1 -> 0; matrix products, arithmetic and copies ran while one was open for 10% -> 10% of each run, Pallas kernels for 62% -> 64%
where the time goes in v5:
time: 882 us; the launch traced here: 873 us
  Pallas kernels  728 us (83%)
  matrix products  66 us (7%)
  local copies, waits for them, and re-layouts  33.1 us (4%)
  other arithmetic  26.4 us (3%)
  between operations  16.1 us (2%)
    pallas_call x2, Pallas kernels, line_sum(): pl.pallas_call(partial(line_sum_kernel, size, chunk_rows), out_shape=jax....  214 us
    pallas_call x1, Pallas kernels, line_error(): pl.pallas_call(partial(line_error_kernel, size, chunk_rows), out_shape=[j...  119 us
    pallas_call x1, Pallas kernels, start_gather(): pl.pallas_call(partial(start_gather_kernel, size, groups, chunk_rows), ou...  88.2 us
    pallas_call x2, Pallas kernels, line_scatter(): pl.pallas_call(partial(line_scatter_kernel, size, chunk_rows), out_shape=...  87.5 us
    pallas_call x1, Pallas kernels, run_mixer_backward(): pl.pallas_call(partial(mixer_backward, steps_per_seq), grid=(steps,), in_...  44.1 us
    pallas_call x1, Pallas kernels, run_mixer_forward(): pl.pallas_call(partial(mixer_forward, steps_per_seq), grid=(steps,), in_s...  35.1 us
    dot_general x6, matrix products, contract_rows(): jnp.einsum('tk,tn->kn', left_op, right_op, preferred_element_type=jnp.flo...  33.8 us
    pallas_call x1, Pallas kernels, channel_forward(): pl.pallas_call(partial(channel_forward_kernel, SEQ_LEN), grid=(positions...  32.3 us
  transfers between devices with their start and end apart: 10, of which 0 were waited for; matrix products, arithmetic and copies ran while one was open for 10% of the time, Pallas kernels for 64%

profile of v5, /device:TPU:0, one launch (start us, length us, event | category | flops | bytes accessed | tf_op | source)
XLA Modules:
  0.0 872.8 jit_solution(16413792560674211001)
XLA Ops:
  7.3 2.1 pad_maximum_fusion
  13.8 88.2 %start_gather.1 = (bf16[1024,2048]{1,0:T(8,128)(2,1)}, bf16[8,4,64,512]{3,2,1,0:T(8,128)(2,1)S(1)}, bf16[8,64,512]{2,1,0:T(8,128)(2,1)S(1)}) custom-call(bf16[1024,512]{1,0:T(8,128)(2,1)S(1)} %copy-done.12, bf16[64,512]{1,0:T(8,128)(2,1)S(1)} %get-tuple-element.159.narrow_ref, bf16[64,512]{1,0:T(8,128)(2,1)S(1)} %get-tuple-element.160.ups_ref), custom_call_target="tpu_custom_call" | custom-call | bytes 251658240 | tf_op jit(solution)/shard_map/start_gather/pallas_call | solution.py:1553
  105.4 26.6 %input_forward.1 = (f32[1024,512]{1,0:T(8,128)}, f32[1024,512]{1,0:T(8,128)}, f32[1024,512]{1,0:T(8,128)}, f32[1024,512]{1,0:T(8,128)}, f32[1024,512]{1,0:T(8,12...) custom-call(bf16[1024,2048]{1,0:T(8,128)(2,1)} %get-tuple-element.74, ...), custom_call_target="tpu_custom_call" | custom-call | tf_op jit(solution)/shard_map/input_forward/pallas_call | solution.py:1389
  132.0 35.1 %mixer_forward.1 = (bf16[1024,512]{1,0:T(8,128)(2,1)}, f32[1024,512]{1,0:T(8,128)}, bf16[1024,512]{1,0:T(8,128)(2,1)}, bf16[1024,512]{1,0:T(8,128)(2,1)}, f32[16...) custom-call(s32[1]{0:T(128)} %dynamic_slice.33.length_ref, ...), custom_call_target="tpu_custom_call" | custom-call | tf_op jit(solution)/shard_map/mixer_forward/pallas_call | solution.py:477
  167.1 6.6 convolution_convert_fusion.2.x_ref
  173.8 108.3 %line_sum.2.delta_ref = bf16[1024,2048]{1,0:T(8,128)(2,1)S(1)} custom-call(bf16[1024,2048]{1,0:T(8,128)(2,1)} %convolution_convert_fusion.2.x_ref), custom_call_target="tpu_custom_call" | custom-call | bytes 335544320 | tf_op jit(solution)/shard_map/line_sum/pallas_call | solution.py:665
  282.1 2.0 copy-done
  284.0 32.3 %channel_forward.1 = (bf16[1024,2048]{1,0:T(8,128)(2,1)}, f32[1024,2048]{1,0:T(8,128)}, bf16[1024,2048]{1,0:T(8,128)(2,1)}, bf16[1024,2048]{1,0:T(8,128)(2,1)}, f32[1024,512]{1,0:T(8,128)}) custom-call(bf16[1024,2048]{1,0:T(8,128)(2,1)} %get-tuple-element.74.whole_ref, bf16[1024,2048]{1,0:T(8,128)(2,1)} %copy-done, ...), custom_call_target="tpu_custom_call" | custom-call | tf_op jit(solution)/shard_map/channel_forward/pallas_call | solution.py:1645
  316.5 1.6 copy-done.10
  318.1 118.6 %line_error.1 = (bf16[1024,512]{1,0:T(8,128)(2,1)S(1)}, bf16[1024,2048]{1,0:T(8,128)(2,1)}) custom-call(bf16[1024,2048]{1,0:T(8,128)(2,1)} %get-tuple-element.84.x_ref, f32[1024,512]{1,0:T(8,128)S(1)} %copy-done.10, bf16[1024,512]{1,0:T(8,128)(2,1)S(1)} %copy-done.11, f32[1024,128]{1,0:T(8,128)S(1)} %broadcast_in_dim.4.weight_ref), custom_call_target="tpu_custom_call" | custom-call | bytes 335544320 | tf_op jit(solution)/shard_map/line_error/pallas_call | solution.py:1177
  436.8 1.0 copy-done.13
  437.8 13.4 %convolution_convert_fusion.1 = bf16[2048,2048]{1,0:T(8,128)(2,1)} fusion(bf16[1024,2048]{1,0:T(8,128)(2,1)S(1)} %copy-done.44, bf16[1024,2048]{1,0:T(8,128)(2,1)} %get-tuple-element.95), kind=kOutput, calls=%fused_computation.3 | convolution fusion | flops 8594128896 | bytes 16777216 | tf_op jit(solution)/shard_map/tk,tn->kn/dot_general | solution.py:1669
  451.2 15.2 %multiply_convert_fusion.dpre_ref = bf16[1024,2048]{1,0:T(8,128)(2,1)S(1)} fusion(f32[1024,2048]{1,0:T(8,128)} %get-tuple-element.96, bf16[1024,2048]{1,0:T(8,128)(2,1)} %get-tuple-element.95, bf16[2048,2048]{1,0:T(8,128)(2,1)} %all-gather.11.cloned.1.call-done.value_ref), kind=kOutput, calls=%fused_computation.1 | convolution fusion | flops 8596226048 | bytes 25165824 | tf_op jit(solution)/shard_map/tn,kn->tk/dot_general | solution.py:1673
  466.4 2.1 copy-done.22
  468.4 11.4 %convolution_convert_fusion = bf16[2048,2048]{1,0:T(8,128)(2,1)} fusion(bf16[1024,2048]{1,0:T(8,128)(2,1)S(1)} %copy-done.43, bf16[1024,2048]{1,0:T(8,128)(2,1)S(1)} %multiply_convert_fusion.dpre_ref), kind=kOutput, calls=%fused_computation.2 | convolution fusion | flops 8594128896 | bytes 16777216 | tf_op jit(solution)/shard_map/tk,tn->kn/dot_general | solution.py:1669
  480.7 26.0 %output_backward.1 = (bf16[1024,2048]{1,0:T(8,128)(2,1)S(1)}, f32[8,8,2048]{2,1,0:T(8,128)S(1)}) custom-call(bf16[1024,2048]{1,0:T(8,128)(2,1)} %get-tuple-element.74.whole_ref, bf16[1024,2048]{1,0:T(8,128)(2,1)} %copy-done, bf16[1024,2048]{1,0:T(8,128)(2,1)} %copy-done.22, bf16[2048,2048]{1,0:T(8,128)(2,1)} %all-gather.9.cloned.1.call-done.key_ref.weight_ref, ...), custom_call_target="tpu_custom_call" | custom-call | tf_op jit(solution)/shard_map/output_backward/pallas_call | solution.py:1283
  506.7 2.0 copy-done.4
  508.6 105.6 %line_sum.3 = bf16[1024,2048]{1,0:T(8,128)(2,1)S(1)} custom-call(bf16[1024,2048]{1,0:T(8,128)(2,1)} %copy-done.4), custom_call_target="tpu_custom_call" | custom-call | bytes 335544320 | tf_op jit(solution)/shard_map/line_sum/pallas_call | solution.py:665
  614.3 2.3 add_convert_fusion
  617.4 1.9 copy-done.23
  619.4 3.8 convolution_convert_fusion.3
  623.3 5.9 fusion.29.dz_ref
  629.2 44.1 %mixer_backward.1 = (bf16[1024,512]{1,0:T(8,128)(2,1)}, bf16[1024,512]{1,0:T(8,128)(2,1)}, bf16[1024,512]{1,0:T(8,128)(2,1)}, bf16[1024,512]{1,0:T(8,128)(2,1)},...) custom-call(s32[1]{0:T(128)} %dynamic_slice.33.length_ref, ...), custom_call_target="tpu_custom_call" | custom-call | tf_op jit(solution)/shard_map/mixer_backward/pallas_call | solution.py:514
  673.3 12.4 %weight_grads.1 = bf16[2048,1536]{1,0:T(8,128)(2,1)} custom-call(bf16[1024,2048]{1,0:T(8,128)(2,1)} %get-tuple-element.110.refs_0_, bf16[1024,2048]{1,0:T(8,128)(2,1)} %get-tuple-element.111.refs_1_, bf16[1024,2048]{1,0:T(8,128)(2,1)} %get-tuple-element.112.refs_2_, bf16[1024,512]{1,0:T(8,128)(2,1)} %get-tuple-element.104.refs_3_.dr_ref, ...), custom_call_target="tpu_custom_call" | custom-call | tf_op jit(solution)/shard_map/weight_grads/pallas_call | solution.py:1027
  687.4 1.4 slice.117
  692.8 1.4 fusion.9.down_ref
  694.2 1.1 convert_element_type.102
  696.1 1.0 pad_maximum_fusion.1
  697.3 1.3 convolution_convert_fusion.6
  698.7 1.6 convolution_convert_fusion.5
  701.0 1.9 fusion.31
  703.7 1.9 add_convert_fusion.1.x_ref
  705.6 22.4 %line_scatter.2 = f32[1024,128]{1,0:T(8,128)S(1)} custom-call(bf16[1024,512]{1,0:T(8,128)(2,1)S(1)} %add_convert_fusion.1.x_ref), custom_call_target="tpu_custom_call" | custom-call | bytes 62914560 | tf_op jit(solution)/shard_map/line_scatter/pallas_call | solution.py:856
  728.8 1.3 multiply_convert_fusion.1.dl_ref
  730.1 1.1 copy-done.9
  731.2 28.7 %input_backward.1 = (bf16[1024,2048]{1,0:T(8,128)(2,1)}, f32[8,8,2048]{2,1,0:T(8,128)S(1)}, f32[128,2048]{1,0:T(8,128)S(1)}) custom-call(bf16[1024,2048]{1,0:T(8,128)(2,1)} %get-tuple-element.74.whole_ref, bf16[1024,512]{1,0:T(8,128)(2,1)S(1)} %copy-done.5, bf16[1024,512]{1,0:T(8,128)(2,1)S(1)} %copy-done.6, bf16[1024,512]{1,0:T(8,128)(2,1)S(1)} %copy-done.7, ...), custom_call_target="tpu_custom_call" | custom-call | tf_op jit(solution)/shard_map/input_backward/pallas_call | solution.py:990
  761.6 1.3 reduce_sum.46
  762.9 2.3 convolution_convert_fusion.4
  765.2 1.7 pad_maximum_fusion.2
  767.0 1.2 select_maximum_fusion
  768.8 1.8 convert_element_type.109
  770.6 1.6 convert_element_type.110
  772.2 1.5 convert_element_type.111
  773.6 65.1 %line_scatter.3 = f32[1024,512]{1,0:T(8,128)S(1)} custom-call(bf16[1024,2048]{1,0:T(8,128)(2,1)} %get-tuple-element.126.x_ref), custom_call_target="tpu_custom_call" | custom-call | bytes 251658240 | tf_op jit(solution)/shard_map/line_scatter/pallas_call | solution.py:856
  838.7 1.2 slice_convert_fusion
  840.0 3.4 add_add_fusion
  846.4 14.8 %line_gather.1 = f32[160,1024]{1,0:T(8,128)S(1)} custom-call(f32[160,256]{1,0:T(8,128)S(1)} %copy-done.19), custom_call_target="tpu_custom_call" | custom-call | bytes 19660800 | tf_op jit(solution)/shard_map/line_gather/pallas_call | solution.py:749
  864.5 1.0 copy.54
  (172 shorter events, 26.5 us)
Async XLA Ops:
  7.2 4.4 copy-start.47
  7.2 6.3 copy-start.42
  7.2 6.4 copy-start.37
  7.2 6.4 copy-start.40
  7.2 6.4 copy-start.41
  7.2 6.4 copy-start.36
  7.2 6.4 copy-start.38
  7.3 6.4 copy-start.39
  7.3 6.5 copy-start.12
  7.3 98.1 %all-gather.5.cloned.1.call-start = ((), (), s32[]{:S(2)}) async-start(), calls=%async_computation.6 | async-start | bytes 7077888 | tf_op jit(solution)/shard_map/all_gather | solution.py:1715
  9.5 157.6 %all-gather.7.cloned.1.call-start = ((), (), s32[]{:S(2)}) async-start(), calls=%async_computation.7 | async-start | bytes 2359296 | tf_op jit(solution)/shard_map/all_gather | solution.py:1722
  10.2 273.8 %all-gather.9.cloned.1.call-start = ((), (), s32[]{:S(2)}) async-start(), calls=%async_computation.8 | async-start | bytes 9437184 | tf_op jit(solution)/shard_map/all_gather | solution.py:1723
  11.0 273.1 %all-gather.11.cloned.1.call-start = ((), (), s32[]{:S(2)}) async-start(), calls=%async_computation.9 | async-start | bytes 9437184 | tf_op jit(solution)/shard_map/all_gather | solution.py:1724
  11.5 617.6 %reduce-scatter.7.cloned.1.call-start = ((), (), s32[]{:S(2)}) async-start(), calls=%async_computation.10 | async-start | bytes 9437184 | tf_op jit(solution)/shard_map/reduce_scatter | solution.py:1770
  102.0 3.4 copy-start.2
  282.1 2.0 copy-start
  284.0 32.5 %copy-start.11 = (bf16[1024,512]{1,0:T(8,128)(2,1)S(1)}, bf16[1024,512]{1,0:T(8,128)(2,1)}, u32[]{:S(2)}) copy-start(bf16[1024,512]{1,0:T(8,128)(2,1)} %teacher_ref.1) | copy-start | bytes 3145732
  318.1 119.6 %copy-start.44 = (bf16[1024,2048]{1,0:T(8,128)(2,1)S(1)}, bf16[1024,2048]{1,0:T(8,128)(2,1)}, u32[]{:S(2)}) copy-start(bf16[1024,2048]{1,0:T(8,128)(2,1)} %get-tuple-element.94) | copy-start | bytes 12582916
  451.1 178.0 %reduce-scatter.9.cloned.1.call-start = ((), (), s32[]{:S(2)}) async-start(), calls=%async_computation.11 | async-start | bytes 9437184 | tf_op jit(solution)/shard_map/reduce_scatter | solution.py:1775
  451.2 17.2 %copy-start.43 = (bf16[1024,2048]{1,0:T(8,128)(2,1)S(1)}, bf16[1024,2048]{1,0:T(8,128)(2,1)}, u32[]{:S(2)}) copy-start(bf16[1024,2048]{1,0:T(8,128)(2,1)} %get-tuple-element.97) | copy-start | bytes 12582916
  466.4 2.1 copy-start.22
  479.9 248.9 %reduce-scatter.11.cloned.1.call-start = ((), (), s32[]{:S(2)}) async-start(), calls=%async_computation.12 | async-start | bytes 2359296 | tf_op jit(solution)/shard_map/reduce_scatter | solution.py:1783
  506.7 2.0 copy-start.4
  508.6 105.6 %copy-start.20 = (bf16[1024,2048]{1,0:T(8,128)(2,1)S(1)}, bf16[1024,2048]{1,0:T(8,128)(2,1)}, u32[]{:S(2)}) copy-start(bf16[1024,2048]{1,0:T(8,128)(2,1)} %get-tuple-element.95) | copy-start | bytes 12582916
  614.3 3.2 copy-start.1
  614.3 5.1 copy-start.46
  617.4 1.9 copy-start.23
  619.4 3.9 copy-start.45
  623.2 145.0 %reduce-scatter.13.cloned.1.call-start = ((), (), s32[]{:S(2)}) async-start(), calls=%async_computation.13 | async-start | bytes 7077888 | tf_op jit(solution)/shard_map/reduce_scatter | solution.py:1794
  685.8 1.7 copy-start.3
  685.8 157.6 %reduce-scatter.17.cloned.1.call-start = ((), (), s32[]{:S(2)}) async-start(), calls=%async_computation.15 | async-start | bytes 516096 | tf_op jit(solution)/shard_map/reduce_scatter | solution.py:1857
  691.3 2.8 copy-start.21
  694.2 3.0 copy-start.35
  694.2 3.1 copy-start.24
  695.3 3.3 copy-start.25
  697.1 5.8 copy-start.27
  697.2 6.4 copy-start.34
  701.0 2.7 copy-start.32
  703.7 26.4 %copy-start.5 = (bf16[1024,512]{1,0:T(8,128)(2,1)S(1)}, bf16[1024,512]{1,0:T(8,128)(2,1)}, u32[]{:S(2)}) copy-start(bf16[1024,512]{1,0:T(8,128)(2,1)} %get-tuple-element.104.refs_3_.dr_ref) | copy-start | bytes 3145732
  703.7 26.4 %copy-start.6 = (bf16[1024,512]{1,0:T(8,128)(2,1)S(1)}, bf16[1024,512]{1,0:T(8,128)(2,1)}, u32[]{:S(2)}) copy-start(bf16[1024,512]{1,0:T(8,128)(2,1)} %get-tuple-element.105.refs_4_.dk_ref) | copy-start | bytes 3145732
  703.7 26.4 %copy-start.7 = (bf16[1024,512]{1,0:T(8,128)(2,1)S(1)}, bf16[1024,512]{1,0:T(8,128)(2,1)}, u32[]{:S(2)}) copy-start(bf16[1024,512]{1,0:T(8,128)(2,1)} %get-tuple-element.106.refs_5_.dv_ref) | copy-start | bytes 3145732
  731.2 35.8 %slice-start = ((f32[8,2048]{1,0:T(8,128)}), f32[3,2048]{1,0:T(4,128)S(1)}, s32[]{:S(2)}) async-start(f32[8,2048]{1,0:T(8,128)} %copy-done.34), calls=%async_computation.16 | async-start | bytes 65536 | tf_op jit(solution)/shard_map/slice | solution.py:1847
  761.6 5.3 copy-start.16
  762.9 7.7 copy-start.31
  766.9 5.2 copy-start.30
  768.2 77.2 %reduce-scatter.15.cloned.1.call-start = ((), (), s32[]{:S(2)}) async-start(), calls=%async_computation.14 | async-start | bytes 1474560 | tf_op jit(solution)/shard_map/reduce_scatter | solution.py:1856
  772.2 66.6 %copy-start.33 = (bf16[256,1536]{1,0:T(8,128)(2,1)S(1)}, bf16[256,1536]{1,0:T(8,128)(2,1)}, u32[]{:S(2)}) copy-start(bf16[256,1536]{1,0:T(8,128)(2,1)} %reduce-scatter.13.cloned.1.call-done) | copy-start | bytes 2359300
  840.0 24.6 %copy-start.14 = (bf16[1024,512]{1,0:T(8,128)(2,1)S(1)}, bf16[1024,512]{1,0:T(8,128)(2,1)}, u32[]{:S(2)}) copy-start(bf16[1024,512]{1,0:T(8,128)(2,1)} %copy-done.13) | copy-start | bytes 3145732
  (11 other events, 10.9 us)
Sparse Core Ops, SparseCore 0:
  10.6 50.5 all-gather.4
  63.0 40.1 all-gather.6
  105.1 54.6 all-gather.8
  161.5 55.9 all-gather.10
  451.3 69.2 reduce-scatter.6
  524.3 71.2 reduce-scatter.8
  623.3 41.1 reduce-scatter.10
  685.9 61.7 reduce-scatter.12
  768.4 35.7 reduce-scatter.16
  807.6 37.3 reduce-scatter.14

commit v6 on v5

--- a/solution.py
+++ b/solution.py
@@ -1003,7 +1003,7 @@
         ],
         scratch_shapes=[pltpu.VMEM((8, width), jnp.float32), pltpu.VMEM((rows_each, width), jnp.float32)],
         compiler_params=pltpu.CompilerParams(
-            dimension_semantics=("arbitrary",), vmem_limit_bytes=48 * 1024 * 1024
+            dimension_semantics=("arbitrary",), vmem_limit_bytes=60 * 1024 * 1024
         ),
         name="input_backward",
     )(whole, dr, dk, dv, dl, three, down, params)
@@ -1291,7 +1291,7 @@
         ],
         scratch_shapes=[pltpu.VMEM((8, width), jnp.float32), pltpu.VMEM((rows_each, width), jnp.float32)],
         compiler_params=pltpu.CompilerParams(
-            dimension_semantics=("arbitrary",), vmem_limit_bytes=48 * 1024 * 1024
+            dimension_semantics=("arbitrary",), vmem_limit_bytes=60 * 1024 * 1024
         ),
         name="output_backward",
     )(whole, delta, dpre, weight, params)
@@ -1395,7 +1395,7 @@
         + [shape((positions, width), jnp.bfloat16)] * 3
         + [shape((positions, down.shape[1]), jnp.float32)],
         compiler_params=pltpu.CompilerParams(
-            dimension_semantics=("arbitrary",), vmem_limit_bytes=52 * 1024 * 1024
+            dimension_semantics=("arbitrary",), vmem_limit_bytes=60 * 1024 * 1024
         ),
         name="input_forward",
     )(whole, three, down, ups, params)
@@ -1655,7 +1655,7 @@
             shape((positions, own_width), jnp.float32),
         ],
         compiler_params=pltpu.CompilerParams(
-            dimension_semantics=("arbitrary",), vmem_limit_bytes=56 * 1024 * 1024
+            dimension_semantics=("arbitrary",), vmem_limit_bytes=60 * 1024 * 1024
         ),
         name="channel_forward",
     )(whole, delta, key_w, value_w, params)
@@ -1861,17 +1861,14 @@
         + lax.dynamic_slice_in_dim(d_delta, col_start, part_width, 1).astype(jnp.float32)
     )
     row_block = decay_down.shape[0]
-    narrow_grads = jnp.pad(narrow_grads, ((0, 0), (0, -narrow_grads.shape[1] % 128)))
-    narrow_rows = narrow_grads.shape[0]
-    narrow_grads = line_gather(narrow_grads, line_size, 4, chunk_rows=narrow_rows // 4)
-    narrow_grads = narrow_grads.reshape(narrow_rows, line_size, -1)
-    narrow_grads = lax.dynamic_slice_in_dim(narrow_grads, mp_index * row_block, row_block, 2)
+    narrow_grads = narrow_grads.T.reshape(line_size, row_block, -1)
+    narrow_grads = lax.all_to_all(narrow_grads, "mp", 0, 0, tiled=True)
 
     def down_grad(start, share):
-        taken = narrow_grads[start : start + share].transpose(1, 0, 2)
-        return taken.reshape(line_size * share, row_block).T
-
-    grad_params = jnp.sum(narrow_grads[own_rank : own_rank + param_count], axis=1).T
+        taken = narrow_grads[:, :, start : start + share].transpose(1, 0, 2)
+        return taken.reshape(row_block, line_size * share)
+
+    grad_params = jnp.sum(narrow_grads[:, :, own_rank : own_rank + param_count], axis=0)
     return (
         out_state,
         grad_hidden,

time: 882 us -> 880 us (level)
  Pallas kernels: 728 us -> 713 us
  waiting for transfers between devices: 2.59 us -> 13.8 us
    pallas_call x1 -> x0, Pallas kernels: 14.8 us -> none  [line_gather(): pl.pallas_call(partial(line_gather_kernel, size, chunk_rows), out_shape=j...]
    unnamed x104 -> x80, local copies, waits for them, and re-layouts: 22.2 us -> 13.8 us
  transfers between devices with their start and end apart: 10 -> 11, of which waited for: 0 -> 2; matrix products, arithmetic and copies ran while one was open for 10% -> 10% of each run, Pallas kernels for 64% -> 65%
where the time goes in v6:
time: 880 us; the launch traced here: 870 us
  Pallas kernels  713 us (81%)
  matrix products  65.5 us (7%)
  local copies, waits for them, and re-layouts  29.9 us (3%)
  other arithmetic  27.3 us (3%)
  between operations  16 us (2%)
  waiting for transfers between devices  13.8 us (2%)
    pallas_call x2, Pallas kernels, line_sum(): pl.pallas_call(partial(line_sum_kernel, size, chunk_rows), out_shape=jax....  213 us
    pallas_call x1, Pallas kernels, line_error(): pl.pallas_call(partial(line_error_kernel, size, chunk_rows), out_shape=[j...  119 us
    pallas_call x1, Pallas kernels, start_gather(): pl.pallas_call(partial(start_gather_kernel, size, groups, chunk_rows), ou...  88.3 us
    pallas_call x2, Pallas kernels, line_scatter(): pl.pallas_call(partial(line_scatter_kernel, size, chunk_rows), out_shape=...  86.8 us
    pallas_call x1, Pallas kernels, run_mixer_backward(): pl.pallas_call(partial(mixer_backward, steps_per_seq), grid=(steps,), in_...  44.1 us
    pallas_call x1, Pallas kernels, run_mixer_forward(): pl.pallas_call(partial(mixer_forward, steps_per_seq), grid=(steps,), in_s...  34.1 us
    dot_general x6, matrix products, contract_rows(): jnp.einsum('tk,tn->kn', left_op, right_op, preferred_element_type=jnp.flo...  33.4 us
    pallas_call x1, Pallas kernels, channel_forward(): pl.pallas_call(partial(channel_forward_kernel, SEQ_LEN), grid=(positions...  32.3 us
  transfers between devices with their start and end apart: 11, of which 2 were waited for; matrix products, arithmetic and copies ran while one was open for 10% of the time, Pallas kernels for 65%

profile of v6, /device:TPU:0, one launch (start us, length us, event | category | flops | bytes accessed | tf_op | source)
XLA Modules:
  0.0 870.2 jit_solution(7842827463399100936)
XLA Ops:
  7.3 2.1 pad_maximum_fusion
  13.8 88.3 %start_gather.1 = (bf16[1024,2048]{1,0:T(8,128)(2,1)}, bf16[8,4,64,512]{3,2,1,0:T(8,128)(2,1)S(1)}, bf16[8,64,512]{2,1,0:T(8,128)(2,1)S(1)}) custom-call(bf16[1024,512]{1,0:T(8,128)(2,1)S(1)} %copy-done.6, bf16[64,512]{1,0:T(8,128)(2,1)S(1)} %get-tuple-element.189.narrow_ref, bf16[64,512]{1,0:T(8,128)(2,1)S(1)} %get-tuple-element.190.ups_ref), custom_call_target="tpu_custom_call" | custom-call | bytes 251658240 | tf_op jit(solution)/shard_map/start_gather/pallas_call | solution.py:1553
  106.2 26.8 %input_forward.1 = (f32[1024,512]{1,0:T(8,128)}, f32[1024,512]{1,0:T(8,128)}, f32[1024,512]{1,0:T(8,128)}, f32[1024,512]{1,0:T(8,128)}, f32[1024,512]{1,0:T(8,12...) custom-call(bf16[1024,2048]{1,0:T(8,128)(2,1)} %get-tuple-element.74, ...), custom_call_target="tpu_custom_call" | custom-call | tf_op jit(solution)/shard_map/input_forward/pallas_call | solution.py:1389
  133.0 34.1 %mixer_forward.1 = (bf16[1024,512]{1,0:T(8,128)(2,1)}, f32[1024,512]{1,0:T(8,128)}, bf16[1024,512]{1,0:T(8,128)(2,1)}, bf16[1024,512]{1,0:T(8,128)(2,1)}, f32[16...) custom-call(s32[1]{0:T(128)} %dynamic_slice.30.length_ref, ...), custom_call_target="tpu_custom_call" | custom-call | tf_op jit(solution)/shard_map/mixer_forward/pallas_call | solution.py:477
  167.1 6.7 convolution_convert_fusion.2.x_ref
  173.8 108.3 %line_sum.2.delta_ref = bf16[1024,2048]{1,0:T(8,128)(2,1)S(1)} custom-call(bf16[1024,2048]{1,0:T(8,128)(2,1)} %convolution_convert_fusion.2.x_ref), custom_call_target="tpu_custom_call" | custom-call | bytes 335544320 | tf_op jit(solution)/shard_map/line_sum/pallas_call | solution.py:665
  282.1 2.0 copy-done
  284.1 32.3 %channel_forward.1 = (bf16[1024,2048]{1,0:T(8,128)(2,1)}, f32[1024,2048]{1,0:T(8,128)}, bf16[1024,2048]{1,0:T(8,128)(2,1)}, bf16[1024,2048]{1,0:T(8,128)(2,1)}, f32[1024,512]{1,0:T(8,128)}) custom-call(bf16[1024,2048]{1,0:T(8,128)(2,1)} %get-tuple-element.74.whole_ref, bf16[1024,2048]{1,0:T(8,128)(2,1)} %copy-done, ...), custom_call_target="tpu_custom_call" | custom-call | tf_op jit(solution)/shard_map/channel_forward/pallas_call | solution.py:1645
  316.6 1.6 copy-done.4
  318.2 118.5 %line_error.1 = (bf16[1024,512]{1,0:T(8,128)(2,1)S(1)}, bf16[1024,2048]{1,0:T(8,128)(2,1)}) custom-call(bf16[1024,2048]{1,0:T(8,128)(2,1)} %get-tuple-element.84.x_ref, f32[1024,512]{1,0:T(8,128)S(1)} %copy-done.4, bf16[1024,512]{1,0:T(8,128)(2,1)S(1)} %copy-done.5, f32[1024,128]{1,0:T(8,128)S(1)} %broadcast_in_dim.4.weight_ref), custom_call_target="tpu_custom_call" | custom-call | bytes 335544320 | tf_op jit(solution)/shard_map/line_error/pallas_call | solution.py:1177
  436.7 13.4 %convolution_convert_fusion.1 = bf16[2048,2048]{1,0:T(8,128)(2,1)} fusion(bf16[1024,2048]{1,0:T(8,128)(2,1)S(1)} %copy-done.33, bf16[1024,2048]{1,0:T(8,128)(2,1)} %get-tuple-element.95), kind=kOutput, calls=%fused_computation.3 | convolution fusion | flops 8594128896 | bytes 16777216 | tf_op jit(solution)/shard_map/tk,tn->kn/dot_general | solution.py:1669
  450.2 15.1 %multiply_convert_fusion.dpre_ref = bf16[1024,2048]{1,0:T(8,128)(2,1)S(1)} fusion(f32[1024,2048]{1,0:T(8,128)} %get-tuple-element.96, bf16[1024,2048]{1,0:T(8,128)(2,1)} %get-tuple-element.95, bf16[2048,2048]{1,0:T(8,128)(2,1)} %all-gather.11.cloned.1.call-done.value_ref), kind=kOutput, calls=%fused_computation.1 | convolution fusion | flops 8596226048 | bytes 25165824 | tf_op jit(solution)/shard_map/tn,kn->tk/dot_general | solution.py:1673
  465.3 2.0 copy-done.9
  467.3 11.4 %convolution_convert_fusion = bf16[2048,2048]{1,0:T(8,128)(2,1)} fusion(bf16[1024,2048]{1,0:T(8,128)(2,1)S(1)} %copy-done.32, bf16[1024,2048]{1,0:T(8,128)(2,1)S(1)} %multiply_convert_fusion.dpre_ref), kind=kOutput, calls=%fused_computation.2 | convolution fusion | flops 8594128896 | bytes 16777216 | tf_op jit(solution)/shard_map/tk,tn->kn/dot_general | solution.py:1669
  478.8 26.9 %output_backward.1 = (bf16[1024,2048]{1,0:T(8,128)(2,1)}, f32[8,8,2048]{2,1,0:T(8,128)}) custom-call(bf16[1024,2048]{1,0:T(8,128)(2,1)} %get-tuple-element.74.whole_ref, bf16[1024,2048]{1,0:T(8,128)(2,1)} %copy-done, bf16[1024,2048]{1,0:T(8,128)(2,1)} %copy-done.9, bf16[2048,2048]{1,0:T(8,128)(2,1)} %all-gather.9.cloned.1.call-done.key_ref.weight_ref, ...), custom_call_target="tpu_custom_call" | custom-call | tf_op jit(solution)/shard_map/output_backward/pallas_call | solution.py:1283
  505.8 104.9 %line_sum.3 = bf16[1024,2048]{1,0:T(8,128)(2,1)S(1)} custom-call(bf16[1024,2048]{1,0:T(8,128)(2,1)} %get-tuple-element.99.x_ref), custom_call_target="tpu_custom_call" | custom-call | bytes 335544320 | tf_op jit(solution)/shard_map/line_sum/pallas_call | solution.py:665
  610.7 2.3 add_convert_fusion
  613.8 2.0 copy-done.10
  615.8 3.8 convolution_convert_fusion.3
  619.7 5.9 fusion.29.dz_ref
  625.6 44.1 %mixer_backward.1 = (bf16[1024,512]{1,0:T(8,128)(2,1)}, bf16[1024,512]{1,0:T(8,128)(2,1)}, bf16[1024,512]{1,0:T(8,128)(2,1)}, bf16[1024,512]{1,0:T(8,128)(2,1)},...) custom-call(s32[1]{0:T(128)} %dynamic_slice.30.length_ref, ...), custom_call_target="tpu_custom_call" | custom-call | tf_op jit(solution)/shard_map/mixer_backward/pallas_call | solution.py:514
  669.7 12.4 %weight_grads.1 = bf16[2048,1536]{1,0:T(8,128)(2,1)} custom-call(bf16[1024,2048]{1,0:T(8,128)(2,1)} %get-tuple-element.110.refs_0_, bf16[1024,2048]{1,0:T(8,128)(2,1)} %get-tuple-element.111.refs_1_, bf16[1024,2048]{1,0:T(8,128)(2,1)} %get-tuple-element.112.refs_2_, bf16[1024,512]{1,0:T(8,128)(2,1)} %get-tuple-element.104.refs_3_.dr_ref, ...), custom_call_target="tpu_custom_call" | custom-call | tf_op jit(solution)/shard_map/weight_grads/pallas_call | solution.py:1027
  682.2 1.7 reshape_reshape.9
  684.6 1.4 slice.117
  686.0 1.7 pad.48
  687.7 1.7 pad.47
  691.8 1.4 fusion.9.down_ref
  693.3 1.1 convert_element_type.102
  696.2 1.2 reduce_sum.48
  698.0 1.3 convolution_convert_fusion.6
  699.4 1.5 convolution_convert_fusion.5
  700.9 1.9 fusion.31
  702.8 1.8 fusion.30
  705.4 22.4 %line_scatter.2 = f32[1024,128]{1,0:T(8,128)S(1)} custom-call(bf16[1024,512]{1,0:T(8,128)(2,1)S(1)} %add_convert_fusion.1.x_ref), custom_call_target="tpu_custom_call" | custom-call | bytes 62914560 | tf_op jit(solution)/shard_map/line_scatter/pallas_call | solution.py:856
  728.6 29.4 %input_backward.1 = (bf16[1024,2048]{1,0:T(8,128)(2,1)}, f32[8,8,2048]{2,1,0:T(8,128)}, f32[128,2048]{1,0:T(8,128)}) custom-call(bf16[1024,2048]{1,0:T(8,128)(2,1)} %get-tuple-element.74.whole_ref, bf16[1024,512]{1,0:T(8,128)(2,1)} %get-tuple-element.104.refs_3_.dr_ref, bf16[1024,512]{1,0:T(8,128)(2,1)} %get-tuple-element.105.refs_4_.dk_ref, ...), custom_call_target="tpu_custom_call" | custom-call | tf_op jit(solution)/shard_map/input_backward/pallas_call | solution.py:990
  757.9 1.2 reduce_sum.46
  759.1 2.0 convolution_convert_fusion.4
  762.0 2.6 select_maximum_fusion
  765.2 1.8 convert_element_type.109
  767.0 1.6 convert_element_type.110
  768.6 1.5 convert_element_type.111
  770.0 64.4 %line_scatter.3 = f32[1024,512]{1,0:T(8,128)S(1)} custom-call(bf16[1024,2048]{1,0:T(8,128)(2,1)} %get-tuple-element.126.x_ref), custom_call_target="tpu_custom_call" | custom-call | bytes 251658240 | tf_op jit(solution)/shard_map/line_scatter/pallas_call | solution.py:856
  834.5 1.2 slice_convert_fusion
  835.7 3.3 add_add_fusion
  839.8 3.6 reduce-scatter.15.cloned.1.call-done
  843.4 1.8 copy.55
  845.2 4.6 all-to-all-start
  851.1 7.6 all-to-all-done
  (152 shorter events, 23.8 us)
Async XLA Ops:
  7.2 4.4 copy-start.36
  7.2 6.3 copy-start.31
  7.2 6.4 copy-start.26
  7.2 6.4 copy-start.29
  7.2 6.4 copy-start.30
  7.2 6.4 copy-start.25
  7.2 6.4 copy-start.27
  7.3 6.4 copy-start.28
  7.3 6.5 copy-start.6
  7.3 98.9 %all-gather.5.cloned.1.call-start = ((), (), s32[]{:S(2)}) async-start(), calls=%async_computation.7 | async-start | bytes 7077888 | tf_op jit(solution)/shard_map/all_gather | solution.py:1715
  9.5 157.6 %all-gather.7.cloned.1.call-start = ((), (), s32[]{:S(2)}) async-start(), calls=%async_computation.8 | async-start | bytes 2359296 | tf_op jit(solution)/shard_map/all_gather | solution.py:1722
  10.2 273.9 %all-gather.9.cloned.1.call-start = ((), (), s32[]{:S(2)}) async-start(), calls=%async_computation.9 | async-start | bytes 9437184 | tf_op jit(solution)/shard_map/all_gather | solution.py:1723
  11.0 273.1 %all-gather.11.cloned.1.call-start = ((), (), s32[]{:S(2)}) async-start(), calls=%async_computation.10 | async-start | bytes 9437184 | tf_op jit(solution)/shard_map/all_gather | solution.py:1724
  11.5 614.0 %reduce-scatter.7.cloned.1.call-start = ((), (), s32[]{:S(2)}) async-start(), calls=%async_computation.11 | async-start | bytes 9437184 | tf_op jit(solution)/shard_map/reduce_scatter | solution.py:1770
  102.0 4.2 copy-start.2
  102.1 0.8 copy-start.18
  103.3 2.9 copy-start.15
  282.1 2.0 copy-start
  284.1 32.5 %copy-start.5 = (bf16[1024,512]{1,0:T(8,128)(2,1)S(1)}, bf16[1024,512]{1,0:T(8,128)(2,1)}, u32[]{:S(2)}) copy-start(bf16[1024,512]{1,0:T(8,128)(2,1)} %teacher_ref.1) | copy-start | bytes 3145732
  316.6 1.6 copy-start.4
  318.2 118.6 %copy-start.33 = (bf16[1024,2048]{1,0:T(8,128)(2,1)S(1)}, bf16[1024,2048]{1,0:T(8,128)(2,1)}, u32[]{:S(2)}) copy-start(bf16[1024,2048]{1,0:T(8,128)(2,1)} %get-tuple-element.94) | copy-start | bytes 12582916
  450.1 175.4 %reduce-scatter.9.cloned.1.call-start = ((), (), s32[]{:S(2)}) async-start(), calls=%async_computation.12 | async-start | bytes 9437184 | tf_op jit(solution)/shard_map/reduce_scatter | solution.py:1775
  450.2 17.2 %copy-start.32 = (bf16[1024,2048]{1,0:T(8,128)(2,1)S(1)}, bf16[1024,2048]{1,0:T(8,128)(2,1)}, u32[]{:S(2)}) copy-start(bf16[1024,2048]{1,0:T(8,128)(2,1)} %get-tuple-element.97) | copy-start | bytes 12582916
  465.3 2.1 copy-start.9
  478.8 249.0 %reduce-scatter.11.cloned.1.call-start = ((), (), s32[]{:S(2)}) async-start(), calls=%async_computation.13 | async-start | bytes 2359296 | tf_op jit(solution)/shard_map/reduce_scatter | solution.py:1783
  505.8 104.9 %copy-start.7 = (bf16[1024,2048]{1,0:T(8,128)(2,1)S(1)}, bf16[1024,2048]{1,0:T(8,128)(2,1)}, u32[]{:S(2)}) copy-start(bf16[1024,2048]{1,0:T(8,128)(2,1)} %get-tuple-element.95) | copy-start | bytes 12582916
  610.6 3.2 copy-start.1
  610.7 5.1 copy-start.35
  613.8 2.0 copy-start.10
  615.8 3.9 copy-start.34
  619.6 145.0 %reduce-scatter.13.cloned.1.call-start = ((), (), s32[]{:S(2)}) async-start(), calls=%async_computation.14 | async-start | bytes 7077888 | tf_op jit(solution)/shard_map/reduce_scatter | solution.py:1794
  682.1 2.5 copy-start.3
  682.2 156.8 %reduce-scatter.17.cloned.1.call-start = ((), (), s32[]{:S(2)}) async-start(), calls=%async_computation.16 | async-start | bytes 516096 | tf_op jit(solution)/shard_map/reduce_scatter | solution.py:1857
  690.3 1.3 copy-start.14
  690.3 2.9 copy-start.8
  693.3 4.2 copy-start.24
  693.3 4.8 copy-start.11
  694.4 5.0 copy-start.12
  700.9 3.7 copy-start.17
  700.9 3.7 copy-start.21
  704.6 23.2 %copy-start.16 = (f32[1024,112]{1,0:T(8,128)S(1)}, f32[1024,112]{1,0:T(8,128)}, u32[]{:S(2)}) copy-start(f32[1024,112]{1,0:T(8,128)} %pad_maximum_fusion.1) | copy-start | bytes 1376260
  728.6 30.6 %copy-start.13 = (bf16[1024,512]{1,0:T(8,128)(2,1)S(1)}, bf16[1024,512]{1,0:T(8,128)(2,1)}, u32[]{:S(2)}) copy-start(bf16[1024,512]{1,0:T(8,128)(2,1)} %convert_element_type.102) | copy-start | bytes 3145732
  728.6 33.5 %slice-start = ((f32[8,2048]{1,0:T(8,128)}), f32[3,2048]{1,0:T(4,128)S(1)}, s32[]{:S(2)}) async-start(f32[8,2048]{1,0:T(8,128)} %copy-done.23), calls=%async_computation.17 | async-start | bytes 65536 | tf_op jit(solution)/shard_map/slice | solution.py:1847
  759.1 7.9 copy-start.20
  762.0 6.5 copy-start.19
  764.6 78.8 %reduce-scatter.15.cloned.1.call-start = ((), (), s32[]{:S(2)}) async-start(), calls=%async_computation.15 | async-start | bytes 1474560 | tf_op jit(solution)/shard_map/reduce_scatter | solution.py:1856
  768.6 65.9 %copy-start.22 = (bf16[256,1536]{1,0:T(8,128)(2,1)S(1)}, bf16[256,1536]{1,0:T(8,128)(2,1)}, u32[]{:S(2)}) copy-start(bf16[256,1536]{1,0:T(8,128)(2,1)} %reduce-scatter.13.cloned.1.call-done) | copy-start | bytes 2359300
  845.2 13.4 %all-to-all-start = ((f32[4,64,160]{2,1,0:T(8,128)}), f32[4,64,160]{2,1,0:T(8,128)S(1)}, u32[]{:S(2)}, u32[]{:S(2)}) async-start(f32[4,64,160]{2,1,0:T(8,128)} %bitcast.10), calls=%async_computation.5 | async-start | bytes 524288 | tf_op jit(solution)/shard_map/all_to_all | solution.py:1865
  (1 other events, 0.6 us)
Sparse Core Ops, SparseCore 0:
  10.6 50.5 all-gather.4
  63.0 40.1 all-gather.6
  105.1 54.6 all-gather.8
  161.5 55.9 all-gather.10
  450.3 69.7 reduce-scatter.6
  523.8 71.2 reduce-scatter.8
  619.7 42.1 reduce-scatter.10
  682.3 62.6 reduce-scatter.12
  764.8 37.9 reduce-scatter.16
  806.1 37.2 reduce-scatter.14
